TPU v7x, 128 devices: a whole 4x4x4 slice. The times are simulated.
128 devices in a mesh: gx: 16 (over z_lo, y, core), gy: 8 (over x, z_hi).
Axes of the slice: x: 4, y: 4, z: 4 (z_hi: 2, z_lo: 2; z = z_hi * 2 + z_lo), core: 2. Of those that a mesh axis runs over, the one named last changes fastest.
Arguments:
- density: float32 [256, 1024, 256], P('gx', 'gy'), may hold values from 0.5 to 5
- cotangent: float32 [3, 256, 1024, 256], P(None, 'gx', 'gy'), may hold values from -60 to 60
- features: bfloat16 [8, 256, 1024, 256], P(None, 'gx', 'gy'), may hold values from -6 to 6
- w_inner: bfloat16 [64, 8], replicated, may hold values from -2 to 2
- w_outer: bfloat16 [3, 64], replicated, may hold values from -0.75 to 0.75
Outputs:
- grad_velocity: float32 [3, 256, 1024, 256], P(None, 'gx', 'gy')
- grad_inner: float32 [64, 8], replicated
- grad_outer: float32 [3, 64], replicated
All inputs are finite; a program needn't handle non-finite values.
Results may differ from a plain program's by a relative error of at most 0.0003.
Values sent between devices are 32-bit elements; how exact they have to be, the bound alone decides.
No kernel may reach another device: no remote copies, remote signals or barrier semaphores. Data moves between devices by JAX's collectives and lax.ppermute only.
A program may use at most 128 MiB of HBM per device.

v0:
```python
import jax
import jax.numpy as jnp
from jax import lax
from jax.sharding import PartitionSpec as P

ITERS = 2


def extended(value, sides, width):
    for axis, dim in sides:
        devices, length = (lax.axis_size(axis), value.shape[dim])
        up = [(i, (i + 1) % devices) for i in range(devices - 1)]
        down = [(j, i) for i, j in up]
        last = lax.slice_in_dim(value, length - width, length, axis=dim)
        first = lax.slice_in_dim(value, 0, width, axis=dim)
        before = lax.ppermute(last, axis, up)
        after = lax.ppermute(first, axis, down)
        value = jnp.concatenate([before, value, after], axis=dim)
    return value


def shifted(value, axis, by):
    devices = lax.axis_size(axis)
    pairs = [(i, i + by) for i in range(devices) if 0 <= i + by < devices]
    return lax.ppermute(value, axis, pairs)


def next_cells(field, axis):
    size = field.shape[axis]
    tail = jnp.zeros_like(lax.slice_in_dim(field, 0, 1, axis=axis))
    return jnp.concatenate([lax.slice_in_dim(field, 1, size, axis=axis), tail], axis)


def prior_cells(field, axis):
    size = field.shape[axis]
    head = jnp.zeros_like(lax.slice_in_dim(field, 0, 1, axis=axis))
    return jnp.concatenate([head, lax.slice_in_dim(field, 0, size - 1, axis=axis)], axis)


def face_weights(density):
    padded = extended(density, (("gx", 0), ("gy", 1)), 1)
    core = padded[1:-1, 1:-1]
    rows_x = padded[:, 1:-1]
    beta_x = 2.0 / (rows_x[:-1] + rows_x[1:])
    lower_x = (lax.axis_index("gx") > 0).astype(jnp.float32)
    beta_x = jnp.concatenate([beta_x[:1] * lower_x, beta_x[1:]], 0)
    rows_y = padded[1:-1]
    beta_y = 2.0 / (rows_y[:, :-1] + rows_y[:, 1:])
    lower_y = (lax.axis_index("gy") > 0).astype(jnp.float32)
    beta_y = jnp.concatenate([beta_y[:, :1] * lower_y, beta_y[:, 1:]], 1)
    beta_z = 2.0 / (core + next_cells(core, 2))
    return (beta_x, beta_y, beta_z)


def operate(padded, betas):
    beta_x, beta_y, beta_z = betas
    core = padded[1:-1, 1:-1]
    flux_x = beta_x * (padded[1:, 1:-1] - padded[:-1, 1:-1])
    flux_y = beta_y * (padded[1:-1, 1:] - padded[1:-1, :-1])
    flux_z = beta_z * (next_cells(core, 2) - core)
    return (
        flux_x[:-1]
        - flux_x[1:]
        + (flux_y[:, :-1] - flux_y[:, 1:])
        + (prior_cells(flux_z, 2) - flux_z)
    )


def faces(field):
    return extended(field, (("gx", 0), ("gy", 1)), 1)


def squares(residual):
    return lax.psum(jnp.sum(residual * residual), ("gx", "gy"))


def closure_grads(features, gout, w_inner, w_outer):
    feats = features.reshape(features.shape[0], -1)
    gflat = gout.astype(jnp.bfloat16).reshape(3, -1)
    cells = feats.shape[1]
    width = min(cells, 65536)

    def step(index, carry):
        acc_inner, acc_outer = carry
        start = index * width
        block = lax.dynamic_slice_in_dim(feats, start, width, 1)
        gblock = lax.dynamic_slice_in_dim(gflat, start, width, 1)
        hidden = jnp.tanh(jnp.dot(w_inner, block, preferred_element_type=jnp.float32))
        hidden_b = hidden.astype(jnp.bfloat16)
        acc_outer = acc_outer + lax.dot_general(
            gblock, hidden_b, (((1,), (1,)), ((), ())), preferred_element_type=jnp.float32
        )
        back = lax.dot_general(
            w_outer, gblock, (((0,), (0,)), ((), ())), preferred_element_type=jnp.float32
        )
        dpre = (back * (1.0 - hidden * hidden)).astype(jnp.bfloat16)
        acc_inner = acc_inner + lax.dot_general(
            dpre, block, (((1,), (1,)), ((), ())), preferred_element_type=jnp.float32
        )
        return (acc_inner, acc_outer)

    init = (
        jnp.zeros((w_inner.shape[0], feats.shape[0]), jnp.float32),
        jnp.zeros((3, w_inner.shape[0]), jnp.float32),
    )
    return lax.fori_loop(0, cells // width, step, init)


def body(density, cotangent, features, w_inner, w_outer):
    betas = face_weights(density)
    beta_x, beta_y, beta_z = betas
    count = float(density.size * lax.axis_size("gx") * lax.axis_size("gy"))
    weighted_x = beta_x[1:] * cotangent[0]
    weighted_y = beta_y[:, 1:] * cotangent[1]
    weighted_z = beta_z * cotangent[2]
    below_x = shifted(weighted_x[-1:], "gx", 1)
    below_y = shifted(weighted_y[:, -1:], "gy", 1)
    source = jnp.concatenate([below_x, weighted_x[:-1]], 0) - weighted_x
    source = source + jnp.concatenate([below_y, weighted_y[:, :-1]], 1) - weighted_y
    source = source + prior_cells(weighted_z, 2) - weighted_z
    shape_pad = (source.shape[0] + 2, source.shape[1] + 2, source.shape[2])
    multiplier_pad = jnp.zeros(shape_pad, jnp.float32)
    residual = source
    direction = source
    norm_now = squares(residual)
    for step in range(ITERS):
        padded = faces(direction)
        image = operate(padded, betas)
        alpha = norm_now / lax.psum(jnp.sum(direction * image), ("gx", "gy"))
        multiplier_pad = multiplier_pad + alpha * padded
        if step + 1 < ITERS:
            residual = residual - alpha * image
            norm_next = squares(residual)
            direction = residual + norm_next / norm_now * direction
            norm_now = norm_next
    multiplier = multiplier_pad[1:-1, 1:-1]
    correction = jnp.stack(
        [
            multiplier_pad[2:, 1:-1] - multiplier,
            multiplier_pad[1:-1, 2:] - multiplier,
            next_cells(multiplier, 2) - multiplier,
        ],
        0,
    )
    grad_velocity = cotangent - correction
    acc_inner, acc_outer = closure_grads(features, grad_velocity, w_inner, w_outer)
    acc_inner, acc_outer = lax.psum((acc_inner, acc_outer), ("gx", "gy"))
    return (grad_velocity, acc_inner / count, acc_outer / count)


def solution(mesh):
    in_specs = (P("gx", "gy", None), P(None, "gx", "gy", None), P(None, "gx", "gy", None), P(), P())
    out_specs = (P(None, "gx", "gy", None), P(), P())
    return jax.shard_map(body, mesh=mesh, in_specs=in_specs, out_specs=out_specs, check_vma=False)
```

profile of v0, /device:TPU:0, one launch (start us, length us, event | category | flops | bytes accessed | tf_op | source)
XLA Modules:
  0.0 606.4 jit_solution(1340045802563874812)
XLA Ops:
  8.2 6.3 %collective-permute-start.3 = (f32[18,1,256]{2,1,0:T(1,128)S(1)}, f32[18,1,256]{2,1,0:T(1,128)S(1)}, u32[]{:S(2)}, u32[]{:S(2)}) collective-permute-start(f32[18,1,256]{2,1,0:T(1,128)S(1)} %get-tuple-element.187), channel_id=1, source_target_pairs={{0,1},{1,2},{2,3},{3,4},{4,5},{5,6},{6,7},{8,9},{9,10},{10,11},{11... | collective-permute-start | bytes 55304 | tf_op jit(solution)/shard_map/ppermute | solution.py:16
  23.4 8.4 %bitcast_multiply_fusion.2 = (f32[16,128,256]{2,1,0:T(8,128)}, f32[16,128,256]{2,1,0:T(8,128)}, f32[16,128,256]{2,1,0:T(8,128)}, f32[16,128,256]{2,1,0:T(8,128)}, f32[16,128,256]{2,1,0:T(8,128)}) fusion(f32[3,16,128,256]{3,2,1,0:T(8,128)} %param.8, f32[17,128,256]{2,1,0:T(8,128)} %copy-done.13, f32[16,129,256]{2,1,0:T(8,128)} %fusion.24, ...), kind=kLoop, calls=%fused_computation.69 | loop fusion | flops 2621440 | bytes 25157632 | tf_op jit(solution)/shard_map/mul | solution.py:113
  72.7 73.3 %all-reduce.8 = (f32[]{:T(128)}, f32[]{:T(128)}) all-reduce(f32[]{:T(128)} %get-tuple-element.155, f32[]{:T(128)} %get-tuple-element.154), channel_id=1, replica_groups=mesh['gx'=16,'gy'=8] {'gx','gy'}, use_global_device_ids=true, to_apply=%region_1.0 | all-reduce | flops 2 | bytes 16 | tf_op jit(solution)/shard_map/psum | solution.py:74
  150.1 63.0 %psum.44 = f32[]{:T(128)} all-reduce(f32[]{:T(128)} %multiply_reduce_fusion), channel_id=1, replica_groups=mesh['gx'=16,'gy'=8] {'gx','gy'}, use_global_device_ids=true, to_apply=%region_5.0 | all-reduce | flops 1 | bytes 8 | tf_op jit(solution)/shard_map/psum | solution.py:74
  237.2 21.0 %copy.9 = bf16[1,8,2048,256]{3,1,2,0:T(8,128)(2,1)} copy(bf16[1,8,2048,256]{3,2,1,0:T(8,128)(2,1)S(1)} %bitcast.39) | data formatting | bytes 16777216
  258.3 69.9 %psum.45 = f32[]{:T(128)} all-reduce(f32[]{:T(128)} %fusion.33), channel_id=1, replica_groups=mesh['gx'=16,'gy'=8] {'gx','gy'}, use_global_device_ids=true, to_apply=%region_7.0 | all-reduce | flops 1 | bytes 8 | tf_op jit(solution)/shard_map/psum | solution.py:129
  338.0 17.1 %copy.8 = bf16[1,3,2048,256]{3,1,2,0:T(4,128)(2,1)} copy(bf16[1,3,2048,256]{3,2,1,0:T(8,128)(2,1)S(1)} %bitcast.36) | data formatting | bytes 6291456
  355.2 186.8 %while.16 = (s32[]{:T(128)}, f32[64,8]{0,1:T(8,128)S(1)}, f32[3,64]{1,0:T(4,128)S(1)}, bf16[3,524288]{1,0:T(4,128)(2,1)}, bf16[3,64]{1,0:T(4,128)(2,1)S(1)}, /*i...) while((s32[]{:T(128)}, f32[64,8]{0,1:T(8,128)S(1)}, ...), condition=%wide.region_9.0_spmd.clone, body=%wide.region_8.0_spmd.clone.sunk | while | flops 205522304 | bytes 120595024 | solution.py:106
  359.0 5.7 copy-done
  368.1 10.7 %fusion.64 = f32[64,8]{0,1:T(8,128)S(1)} fusion(bf16[3,64]{1,0:T(4,128)(2,1)S(1)} %get-tuple-element.266, f32[65536,64]{0,1:T(8,128)} %copy-done, bf16[8,524288]{1,0:T(8,128)(2,1)} %get-tuple-element.267, s32[]{:T(128)S(6)} %select_n.10, bf16[3,524288]{1,0:T(4,128)(2,1)} %get-tuple-element.265, f32[64,8]{0,1:T(8,128)S(1)} %get-tuple-element.252, ...), kind=kOutput, calls=%fused_computation.6.clone.1 | convolution fusion | flops 109052928 | bytes 18356096 | tf_op jit(solution)/shard_map/while/body/eval_jaxpr/dot_general | solution.py:97
  382.3 5.7 copy-done
  391.4 10.7 %fusion.64 = f32[64,8]{0,1:T(8,128)S(1)} fusion(bf16[3,64]{1,0:T(4,128)(2,1)S(1)} %get-tuple-element.266, f32[65536,64]{0,1:T(8,128)} %copy-done, bf16[8,524288]{1,0:T(8,128)(2,1)} %get-tuple-element.267, s32[]{:T(128)S(6)} %select_n.10, bf16[3,524288]{1,0:T(4,128)(2,1)} %get-tuple-element.265, f32[64,8]{0,1:T(8,128)S(1)} %get-tuple-element.252, ...), kind=kOutput, calls=%fused_computation.6.clone.1 | convolution fusion | flops 109052928 | bytes 18356096 | tf_op jit(solution)/shard_map/while/body/eval_jaxpr/dot_general | solution.py:97
  405.7 5.7 copy-done
  414.7 10.7 %fusion.64 = f32[64,8]{0,1:T(8,128)S(1)} fusion(bf16[3,64]{1,0:T(4,128)(2,1)S(1)} %get-tuple-element.266, f32[65536,64]{0,1:T(8,128)} %copy-done, bf16[8,524288]{1,0:T(8,128)(2,1)} %get-tuple-element.267, s32[]{:T(128)S(6)} %select_n.10, bf16[3,524288]{1,0:T(4,128)(2,1)} %get-tuple-element.265, f32[64,8]{0,1:T(8,128)S(1)} %get-tuple-element.252, ...), kind=kOutput, calls=%fused_computation.6.clone.1 | convolution fusion | flops 109052928 | bytes 18356096 | tf_op jit(solution)/shard_map/while/body/eval_jaxpr/dot_general | solution.py:97
  429.0 5.7 copy-done
  438.0 10.7 %fusion.64 = f32[64,8]{0,1:T(8,128)S(1)} fusion(bf16[3,64]{1,0:T(4,128)(2,1)S(1)} %get-tuple-element.266, f32[65536,64]{0,1:T(8,128)} %copy-done, bf16[8,524288]{1,0:T(8,128)(2,1)} %get-tuple-element.267, s32[]{:T(128)S(6)} %select_n.10, bf16[3,524288]{1,0:T(4,128)(2,1)} %get-tuple-element.265, f32[64,8]{0,1:T(8,128)S(1)} %get-tuple-element.252, ...), kind=kOutput, calls=%fused_computation.6.clone.1 | convolution fusion | flops 109052928 | bytes 18356096 | tf_op jit(solution)/shard_map/while/body/eval_jaxpr/dot_general | solution.py:97
  452.3 5.7 copy-done
  461.3 10.7 %fusion.64 = f32[64,8]{0,1:T(8,128)S(1)} fusion(bf16[3,64]{1,0:T(4,128)(2,1)S(1)} %get-tuple-element.266, f32[65536,64]{0,1:T(8,128)} %copy-done, bf16[8,524288]{1,0:T(8,128)(2,1)} %get-tuple-element.267, s32[]{:T(128)S(6)} %select_n.10, bf16[3,524288]{1,0:T(4,128)(2,1)} %get-tuple-element.265, f32[64,8]{0,1:T(8,128)S(1)} %get-tuple-element.252, ...), kind=kOutput, calls=%fused_computation.6.clone.1 | convolution fusion | flops 109052928 | bytes 18356096 | tf_op jit(solution)/shard_map/while/body/eval_jaxpr/dot_general | solution.py:97
  475.6 5.7 copy-done
  484.7 10.7 %fusion.64 = f32[64,8]{0,1:T(8,128)S(1)} fusion(bf16[3,64]{1,0:T(4,128)(2,1)S(1)} %get-tuple-element.266, f32[65536,64]{0,1:T(8,128)} %copy-done, bf16[8,524288]{1,0:T(8,128)(2,1)} %get-tuple-element.267, s32[]{:T(128)S(6)} %select_n.10, bf16[3,524288]{1,0:T(4,128)(2,1)} %get-tuple-element.265, f32[64,8]{0,1:T(8,128)S(1)} %get-tuple-element.252, ...), kind=kOutput, calls=%fused_computation.6.clone.1 | convolution fusion | flops 109052928 | bytes 18356096 | tf_op jit(solution)/shard_map/while/body/eval_jaxpr/dot_general | solution.py:97
  499.0 5.7 copy-done
  508.0 10.7 %fusion.64 = f32[64,8]{0,1:T(8,128)S(1)} fusion(bf16[3,64]{1,0:T(4,128)(2,1)S(1)} %get-tuple-element.266, f32[65536,64]{0,1:T(8,128)} %copy-done, bf16[8,524288]{1,0:T(8,128)(2,1)} %get-tuple-element.267, s32[]{:T(128)S(6)} %select_n.10, bf16[3,524288]{1,0:T(4,128)(2,1)} %get-tuple-element.265, f32[64,8]{0,1:T(8,128)S(1)} %get-tuple-element.252, ...), kind=kOutput, calls=%fused_computation.6.clone.1 | convolution fusion | flops 109052928 | bytes 18356096 | tf_op jit(solution)/shard_map/while/body/eval_jaxpr/dot_general | solution.py:97
  531.3 10.7 %fusion.64 = f32[64,8]{0,1:T(8,128)S(1)} fusion(bf16[3,64]{1,0:T(4,128)(2,1)S(1)} %get-tuple-element.266, f32[65536,64]{0,1:T(8,128)} %copy-done, bf16[8,524288]{1,0:T(8,128)(2,1)} %get-tuple-element.267, s32[]{:T(128)S(6)} %select_n.10, bf16[3,524288]{1,0:T(4,128)(2,1)} %get-tuple-element.265, f32[64,8]{0,1:T(8,128)S(1)} %get-tuple-element.252, ...), kind=kOutput, calls=%fused_computation.6.clone.1 | convolution fusion | flops 109052928 | bytes 18356096 | tf_op jit(solution)/shard_map/while/body/eval_jaxpr/dot_general | solution.py:97
  542.0 62.8 %all-reduce.7 = (f32[64,8]{0,1:T(8,128)S(1)}, f32[3,64]{1,0:T(4,128)S(1)}) all-reduce(f32[64,8]{0,1:T(8,128)S(1)} %get-tuple-element.128, f32[3,64]{1,0:T(4,128)S(1)} %get-tuple-element.129), channel_id=1, replica_groups=mesh['gx'=16,'gy'=8] {'gx','gy'}, use_global_device_ids=true, to_apply=%region_10.0 | all-reduce | flops 704 | bytes 5632 | tf_op jit(solution)/shard_map/psum | solution.py:147
  (130 shorter events, 153.2 us)
Async XLA Ops:
  1.6 6.3 %collective-permute-start = (f32[1,128,256]{2,1,0:T(8,128)S(1)}, f32[1,128,256]{2,1,0:T(8,128)S(1)}, u32[]{:S(2)}, u32[]{:S(2)}) collective-permute-start(f32[1,128,256]{2,1,0:T(8,128)S(1)} %get-tuple-element.196), channel_id=1, source_target_pairs={{0,8},{8,16},{16,24},{24,32},{32,40},{40,48},{48,56},{56,64},{64,7... | collective-permute-start | bytes 393224 | tf_op jit(solution)/shard_map/ppermute | solution.py:16
  2.9 5.2 collective-permute-start.1
  8.2 9.3 %collective-permute-start.3 = (f32[18,1,256]{2,1,0:T(1,128)S(1)}, f32[18,1,256]{2,1,0:T(1,128)S(1)}, u32[]{:S(2)}, u32[]{:S(2)}) collective-permute-start(f32[18,1,256]{2,1,0:T(1,128)S(1)} %get-tuple-element.187), channel_id=1, source_target_pairs={{0,1},{1,2},{2,3},{3,4},{4,5},{5,6},{6,7},{8,9},{9,10},{10,11},{11... | collective-permute-start | bytes 55304 | tf_op jit(solution)/shard_map/ppermute | solution.py:16
  14.5 7.2 %collective-permute-start.4 = (f32[18,1,256]{2,1,0:T(1,128)S(1)}, f32[18,1,256]{2,1,0:T(1,128)S(1)}, u32[]{:S(2)}, u32[]{:S(2)}) collective-permute-start(f32[18,1,256]{2,1,0:T(1,128)S(1)} %get-tuple-element.188), channel_id=1, source_target_pairs={{1,0},{2,1},{3,2},{4,3},{5,4},{6,5},{7,6},{9,8},{10,9},{11,10},{12... | collective-permute-start | bytes 55304 | tf_op jit(solution)/shard_map/ppermute | solution.py:17
  17.5 5.9 copy-start.5
  31.8 11.3 %copy-start.7 = (f32[16,128,256]{2,1,0:T(8,128)S(1)}, f32[16,128,256]{2,1,0:T(8,128)}, u32[]{:S(2)}) copy-start(f32[16,128,256]{2,1,0:T(8,128)} %get-tuple-element.178) | copy-start | bytes 6291460
  31.8 11.3 %copy-start.12 = (f32[16,128,256]{2,1,0:T(8,128)S(1)}, f32[16,128,256]{2,1,0:T(8,128)}, u32[]{:S(2)}) copy-start(f32[16,128,256]{2,1,0:T(8,128)} %get-tuple-element.177) | copy-start | bytes 6291460
  32.9 10.2 %collective-permute-start.5 = (f32[16,1,256]{2,1,0:T(1,128)S(1)}, f32[16,1,256]{2,1,0:T(1,128)S(1)}, u32[]{:S(2)}, u32[]{:S(2)}) collective-permute-start(f32[16,1,256]{2,1,0:T(1,128)S(1)} %slice.216), channel_id=1, source_target_pairs={{0,1},{1,2},{2,3},{3,4},{4,5},{5,6},{6,7},{8,9},{9,10},{10,11},{11... | collective-permute-start | bytes 49160 | tf_op jit(solution)/shard_map/ppermute | solution.py:25
  37.4 5.8 collective-permute-start.2
  46.9 6.9 %copy-start.3 = (f32[16,128,256]{2,1,0:T(8,128)S(1)}, f32[16,128,256]{2,1,0:T(8,128)}, u32[]{:S(2)}) copy-start(f32[16,128,256]{2,1,0:T(8,128)} %param.7) | copy-start | bytes 6291460
  47.5 7.1 %collective-permute-start.7 = (f32[1,128,256]{2,1,0:T(8,128)S(1)}, f32[1,128,256]{2,1,0:T(8,128)S(1)}, u32[]{:S(2)}, u32[]{:S(2)}) collective-permute-start(f32[1,128,256]{2,1,0:T(8,128)S(1)} %get-tuple-element.193), channel_id=1, source_target_pairs={{0,8},{8,16},{16,24},{24,32},{32,40},{40,48},{48,56},{56,64},{64,7... | collective-permute-start | bytes 393224 | tf_op jit(solution)/shard_map/ppermute | solution.py:16
  52.5 4.5 collective-permute-start.6
  54.5 8.7 %copy-start.10 = (f32[16,128,256]{2,1,0:T(8,128)S(1)}, f32[16,128,256]{2,1,0:T(8,128)}, u32[]{:S(2)}) copy-start(f32[16,128,256]{2,1,0:T(8,128)} %get-tuple-element.190) | copy-start | bytes 6291460
  57.0 6.5 %collective-permute-start.9 = (f32[18,1,256]{2,1,0:T(1,128)S(1)}, f32[18,1,256]{2,1,0:T(1,128)S(1)}, u32[]{:S(2)}, u32[]{:S(2)}) collective-permute-start(f32[18,1,256]{2,1,0:T(1,128)S(1)} %get-tuple-element.185), channel_id=1, source_target_pairs={{0,1},{1,2},{2,3},{3,4},{4,5},{5,6},{6,7},{8,9},{9,10},{10,11},{11... | collective-permute-start | bytes 55304 | tf_op jit(solution)/shard_map/ppermute | solution.py:16
  61.9 7.2 %collective-permute-start.8 = (f32[18,1,256]{2,1,0:T(1,128)S(1)}, f32[18,1,256]{2,1,0:T(1,128)S(1)}, u32[]{:S(2)}, u32[]{:S(2)}) collective-permute-start(f32[18,1,256]{2,1,0:T(1,128)S(1)} %get-tuple-element.186), channel_id=1, source_target_pairs={{1,0},{2,1},{3,2},{4,3},{5,4},{6,5},{7,6},{9,8},{10,9},{11,10},{12... | collective-permute-start | bytes 55304 | tf_op jit(solution)/shard_map/ppermute | solution.py:17
  216.3 17.8 %copy-start.1 = (f32[16,128,256]{2,1,0:T(8,128)}, f32[16,128,256]{2,1,0:T(8,128)S(1)}, u32[]{:S(2)}) copy-start(f32[16,128,256]{2,1,0:T(8,128)S(1)} %multiply_add_fusion) | copy-start | bytes 6291460
  217.0 4.1 collective-permute-start.11
  219.0 3.9 collective-permute-start.10
  221.1 6.7 %copy-start.11 = (f32[16,128,256]{2,1,0:T(8,128)S(1)}, f32[16,128,256]{2,1,0:T(8,128)}, u32[]{:S(2)}) copy-start(f32[16,128,256]{2,1,0:T(8,128)} %get-tuple-element.190) | copy-start | bytes 6291460
  222.9 5.2 collective-permute-start.13
  226.3 7.3 %copy-start.9 = (f32[16,128,256]{2,1,0:T(8,128)S(1)}, f32[16,128,256]{2,1,0:T(8,128)}, u32[]{:S(2)}) copy-start(f32[16,128,256]{2,1,0:T(8,128)} %get-tuple-element.189) | copy-start | bytes 6291460
  226.4 7.3 %collective-permute-start.12 = (f32[18,1,256]{2,1,0:T(1,128)S(1)}, f32[18,1,256]{2,1,0:T(1,128)S(1)}, u32[]{:S(2)}, u32[]{:S(2)}) collective-permute-start(f32[18,1,256]{2,1,0:T(1,128)S(1)} %get-tuple-element.184), channel_id=1, source_target_pairs={{1,0},{2,1},{3,2},{4,3},{5,4},{6,5},{7,6},{9,8},{10,9},{11,10},{12... | collective-permute-start | bytes 55304 | tf_op jit(solution)/shard_map/ppermute | solution.py:17
  338.0 17.1 %copy-start.14 = (bf16[64,8]{0,1:T(8,128)(2,1)S(1)}, bf16[64,8]{0,1:T(8,128)(2,1)}, u32[]{:S(2)}) copy-start(bf16[64,8]{0,1:T(8,128)(2,1)} %param.10) | copy-start | bytes 3076
  338.0 17.1 %copy-start.15 = (bf16[3,64]{1,0:T(4,128)(2,1)S(1)}, bf16[3,64]{1,0:T(4,128)(2,1)}, u32[]{:S(2)}) copy-start(bf16[3,64]{1,0:T(4,128)(2,1)} %param.11) | copy-start | bytes 1156
  (17 other events, 74.5 us)
where the time goes:
time: 616 us; the launch traced here: 606 us
  blocking collectives  269 us (44%)
  matrix products  141 us (23%)
  local copies, waits for them, and re-layouts  98.6 us (16%)
  starting transfers between devices  37.5 us (6%)
  other arithmetic  35.1 us (6%)
  waiting for transfers between devices  19.5 us (3%)
    psum x2, blocking collectives, squares(): return lax.psum(jnp.sum(residual * residual), ('gx', 'gy'))  136 us
    dot_general x8, matrix products, step(): lax.dot_general(dpre, block, (((1,), (1,)), ((), ())), preferred_element_...  85.3 us
    psum x1, blocking collectives, body(): alpha = norm_now / lax.psum(jnp.sum(direction * image), ('gx', 'gy'))  69.9 us
    psum x1, blocking collectives, body(): acc_inner, acc_outer = lax.psum((acc_inner, acc_outer), ('gx', 'gy'))  62.8 us
    while x16, local copies, waits for them, and re-layouts  45.7 us
    unnamed x42, local copies, waits for them, and re-layouts  42.6 us
    dot_general x8, matrix products, step(): jnp.dot(w_inner, block, preferred_element_type=jnp.float32)  28.8 us
    dot_general x8, matrix products, step(): lax.dot_general(gblock, hidden_b, (((1,), (1,)), ((), ())), preferred_ele...  26.6 us
  transfers between devices with their start and end apart: 14, of which 5 were waited for; matrix products, arithmetic and copies ran while one was open for 2% of the time, Pallas kernels for 0%

commit v1 on v0

v1 whole, which is shorter than its diff:
```python
import jax
import jax.numpy as jnp
from jax import lax
from jax.experimental import pallas as pl
from jax.experimental.pallas import tpu as pltpu
from jax.sharding import PartitionSpec as P

F32 = jnp.float32
BF16 = jnp.bfloat16
LAST = (((1,), (1,)), ((), ()))
STAGES = ((8, 16), (32, 64), (1, 2), (4,))
VMEM = 56 * 2**20


def shifted(value, axis, by):
    devices = lax.axis_size(axis)
    pairs = [(i, i + by) for i in range(devices) if 0 <= i + by < devices]
    return lax.ppermute(value, axis, pairs)


def total(value):
    devices = lax.axis_size("gx") * lax.axis_size("gy")
    for bits in STAGES:
        level = [value]
        masks = [0]
        for bit in bits:
            masks = masks + [mask ^ bit for mask in masks]
        for mask in masks[1:]:
            pairs = [(i, i ^ mask) for i in range(devices)]
            level.append(lax.ppermute(value, ("gx", "gy"), pairs))
        while len(level) > 1:
            level = [level[k] + level[k + 1] for k in range(0, len(level), 2)]
        value = level[0]
    return value


def next_row(plane, row):
    size = plane.shape[0]
    at = lax.broadcasted_iota(jnp.int32, plane.shape, 0)
    return jnp.where(at == size - 1, row, pltpu.roll(plane, size - 1, 0))


def prior_row(plane, row):
    at = lax.broadcasted_iota(jnp.int32, plane.shape, 0)
    return jnp.where(at == 0, row, pltpu.roll(plane, 1, 0))


def next_lane(plane):
    size = plane.shape[1]
    at = lax.broadcasted_iota(jnp.int32, plane.shape, 1)
    return jnp.where(at == size - 1, 0.0, pltpu.roll(plane, size - 1, 1))


def prior_lane(plane):
    at = lax.broadcasted_iota(jnp.int32, plane.shape, 1)
    return jnp.where(at == 0, 0.0, pltpu.roll(plane, 1, 1))


def fold(plane):
    return jnp.sum(plane.reshape(-1, 8, plane.shape[1]), 0)


def lanes(folded):
    row = jnp.sum(folded, 0, keepdims=True)
    return sum(row[:, k : k + 128] for k in range(0, row.shape[1], 128))


def source_kernel(
    dens, cot, below_x, above_x, below_y, above_y, s_out, x_lo, x_hi, y_lo, y_hi, carry
):
    step, planes = pl.program_id(0), dens.shape[0]
    here = dens[step]
    ahead = jnp.where(step == planes - 1, above_x[...], dens[jnp.minimum(step + 1, planes - 1)])

    @pl.when(step == 0)
    def _():
        carry[...] = 2.0 / (below_x[0] + here) * below_x[1]

    flux = 2.0 / (here + ahead) * cot[0, 0]
    out = carry[...] - flux
    carry[...] = flux
    row = pl.ds(step, 1)
    first = 2.0 / (below_y[0, row] + here[:1]) * below_y[1, row]
    flux = 2.0 / (here + next_row(here, above_y[row])) * cot[1, 0]
    out = out + prior_row(flux, first) - flux
    flux = 2.0 / (here + next_lane(here)) * cot[2, 0]
    out = out + prior_lane(flux) - flux
    s_out[0] = out
    y_lo[row] = out[:1]
    y_hi[row] = out[-1:]

    @pl.when(step == 0)
    def _():
        x_lo[...] = out

    @pl.when(step == planes - 1)
    def _():
        x_hi[...] = out


def image_kernel(
    dens, s, dens_bx, dens_ax, dens_by, dens_ay, s_bx, s_ax, s_by, s_ay,
    q_out, x_lo, x_hi, y_lo, y_hi, beta_x, beta_y, sums, flux_x, acc,
):
    step, planes = pl.program_id(0), dens.shape[0]
    here, field = dens[step], s[step]
    last = step == planes - 1
    ahead = jnp.minimum(step + 1, planes - 1)
    row = pl.ds(step, 1)

    @pl.when(step == 0)
    def _():
        below = dens_bx[...]
        flux_x[...] = jnp.where(below > 0, 2.0 / (below + here) * (field - s_bx[...]), 0.0)
        acc[...] = jnp.zeros_like(acc)

    b_x = 2.0 / (here + jnp.where(last, dens_ax[...], dens[ahead]))
    flux = b_x * (jnp.where(last, s_ax[...], s[ahead]) - field)
    out = flux_x[...] - flux
    flux_x[...] = flux
    below = dens_by[row]
    first = jnp.where(below > 0, 2.0 / (below + here[:1]) * (field[:1] - s_by[row]), 0.0)
    b_y = 2.0 / (here + next_row(here, dens_ay[row]))
    flux = b_y * (next_row(field, s_ay[row]) - field)
    out = out + (prior_row(flux, first) - flux)
    b_z = 2.0 / (here + next_lane(here))
    flux = b_z * (next_lane(field) - field)
    out = out + (prior_lane(flux) - flux)
    q_out[0] = out
    y_lo[row] = out[:1]
    y_hi[row] = out[-1:]
    beta_y[row] = b_y[-1:]
    acc[0] += fold(field * field)
    acc[1] += fold(field * out)
    acc[2] += fold(out * out)
    jump = next_row(out, out[-1:]) - out
    jump_z = next_lane(out) - out
    acc[3] += fold(b_y * jump * jump + b_z * jump_z * jump_z)

    @pl.when(step == 0)
    def _():
        x_lo[...] = out

    @pl.when(step > 0)
    def _():
        jump = out - x_hi[...]
        acc[3] += fold(beta_x[...] * jump * jump)

    x_hi[...] = out
    beta_x[...] = b_x

    @pl.when(last)
    def _():
        rows = [lanes(acc[k]) for k in range(4)]
        sums[...] = jnp.concatenate(rows + [jnp.zeros((4, 128), F32)], 0)


def edge_kernel(sums, x_hi, y_hi, beta_x, beta_y, q_ax, q_ay, out):
    jump_x = q_ax[...] - x_hi[...]
    jump_y = q_ay[...] - y_hi[...]
    edge = lanes(fold(beta_x[...] * jump_x * jump_x)) + lanes(fold(beta_y[...] * jump_y * jump_y))
    at = lax.broadcasted_iota(jnp.int32, (8, 128), 0)
    out[...] = sums[...] + jnp.where(at == 3, edge, 0.0)


def closure_kernel(
    sums, cot, s, q, s_ax, q_ax, s_ay, q_ay, feats, w_in, w_out,
    grad, grads, velocity, hid, slope, vel, prod, acc_o, acc_t,
):
    step, planes = pl.program_id(0), s.shape[0]
    rows, width = s.shape[1], s.shape[2]
    count = feats.shape[0]
    m0, m1, m2, m3 = (jnp.sum(sums[k : k + 1], 1, keepdims=True) for k in range(4))
    alpha0 = m0 / m1
    rr1 = alpha0 * alpha0 * m2 - m0
    beta = rr1 / m0
    more = 1.0 + beta
    alpha1 = rr1 / (more * more * m1 - 2.0 * more * alpha0 * m2 + alpha0 * alpha0 * m3)
    on_s, on_q = alpha0 + alpha1 * more, -alpha1 * alpha0

    @pl.when(step == 0)
    def _():
        acc_o[...] = jnp.zeros_like(acc_o)
        acc_t[...] = jnp.zeros_like(acc_t)

    last = step == planes - 1
    ahead = jnp.minimum(step + 1, planes - 1)
    row = pl.ds(step, 1)
    here = on_s * s[step] + on_q * q[step]
    beyond = on_s * jnp.where(last, s_ax[...], s[ahead]) + on_q * jnp.where(last, q_ax[...], q[ahead])
    edge = on_s * s_ay[row] + on_q * q_ay[row]
    for a, after in enumerate((beyond, next_row(here, edge), next_lane(here))):
        value = cot[a, 0] - (after - here)
        grad[a, 0] = value
        velocity[a] = value.astype(BF16).astype(F32)

    half = w_in.shape[0] // 2
    for block in range(rows // 16):
        at = slice(block * 16, block * 16 + 16)
        inner = feats[:, 0, at, :].reshape(count * 16, width)
        pre = lax.dot_general(
            w_in[...], inner, (((1,), (0,)), ((), ())), preferred_element_type=F32
        )
        hidden = jnp.tanh(pre)
        hidden_b = hidden.astype(BF16)
        slope_b = (1.0 - hidden * hidden).astype(BF16)
        wide = [feats[c, 0, at, :].astype(F32) for c in range(count)]
        for part in range(2):
            to = slice((block * 2 + part) * width, (block * 2 + part + 1) * width)
            hid[:, to] = hidden_b[part * half : (part + 1) * half]
            slope[:, to] = slope_b[part * half : (part + 1) * half]
            low = block * 16 + part * 8
            vs = [velocity[a, low : low + 8, :] for a in range(3)]
            vel[:, to] = jnp.concatenate(vs + [jnp.zeros_like(vs[0])], 0).astype(BF16)
            fs = [f[part * 8 : part * 8 + 8] for f in wide]
            prod[:, to] = jnp.concatenate([v * f for v in vs for f in fs], 0).astype(BF16)
    acc_o[...] += lax.dot_general(vel[...], hid[...], LAST, preferred_element_type=F32)
    acc_t[...] += lax.dot_general(prod[...], slope[...], LAST, preferred_element_type=F32)

    @pl.when(last)
    def _():
        def own(value):
            at_row = lax.broadcasted_iota(jnp.int32, value.shape, 0) % 8
            at_col = lax.broadcasted_iota(jnp.int32, value.shape, 1) % 8
            kept = jnp.where(at_row == at_col, value, 0.0)
            return jnp.sum(kept.reshape(-1, 8, value.shape[1]), 1)

        outer = own(acc_o[...])
        terms = own(acc_t[...])
        inner = sum(
            w_out[a : a + 1] * terms[a * count : (a + 1) * count] for a in range(3)
        )
        both = jnp.concatenate([inner, outer, jnp.zeros_like(outer)], 0)
        hidden_at = lax.broadcasted_iota(jnp.int32, (half, 128), 0) // 8
        column = lax.broadcasted_iota(jnp.int32, (half, 128), 1)
        pick = (hidden_at == column).astype(F32)
        grads[...] = jnp.dot(
            both, pick, precision=lax.Precision.HIGHEST, preferred_element_type=F32
        )


def whole(shape):
    return pl.BlockSpec(shape, lambda i: (0,) * len(shape))


def shape(*dims):
    return jax.ShapeDtypeStruct(dims, F32)


def params():
    return pltpu.CompilerParams(vmem_limit_bytes=VMEM)


def body(density, cotangent, features, w_inner, w_outer):
    nx, ny, nz = density.shape
    count, hidden = features.shape[0], w_inner.shape[0]
    cells = float(density.size * lax.axis_size("gx") * lax.axis_size("gy"))
    field, side_x, side_y = (nx, ny, nz), (ny, nz), (nx, nz)
    plane = pl.BlockSpec((1, ny, nz), lambda i: (i, 0, 0))
    planes = pl.BlockSpec((3, 1, ny, nz), lambda i: (0, i, 0, 0))

    dens_ax = shifted(density[0], "gx", -1)
    below_x = shifted(jnp.stack([density[-1], cotangent[0, -1]]), "gx", 1)
    dens_ay = shifted(density[:, 0], "gy", -1)
    below_y = shifted(jnp.stack([density[:, -1], cotangent[1, :, -1]]), "gy", 1)

    pick = jnp.arange(16)[None, None, :] == jnp.arange(16).reshape(2, 8)[:, :, None]
    w_in = w_inner[None, :, None, :, None] * pick[:, None, :, None, :].astype(BF16)
    w_in = w_in.reshape(2 * hidden * 8, count * 16)
    w_out = jnp.repeat(w_outer.astype(F32), 8, axis=1)

    s, s_x0, s_x1, s_y0, s_y1 = pl.pallas_call(
        source_kernel,
        grid=(nx,),
        in_specs=[whole(field), planes, whole((2,) + side_x), whole(side_x), whole((2,) + side_y), whole(side_y)],
        out_specs=[plane, whole(side_x), whole(side_x), whole(side_y), whole(side_y)],
        out_shape=[shape(*field), shape(*side_x), shape(*side_x), shape(*side_y), shape(*side_y)],
        scratch_shapes=[pltpu.VMEM(side_x, F32)],
        compiler_params=params(),
    )(density, cotangent, below_x, dens_ax, below_y, dens_ay)

    s_ax = shifted(s_x0, "gx", -1)
    s_bx = shifted(s_x1, "gx", 1)
    s_ay = shifted(s_y0, "gy", -1)
    s_by = shifted(s_y1, "gy", 1)

    q, q_x0, q_x1, q_y0, q_y1, beta_x, beta_y, sums = pl.pallas_call(
        image_kernel,
        grid=(nx,),
        in_specs=[whole(field)] * 2 + [whole(side_x)] * 2 + [whole(side_y)] * 2 + [whole(side_x)] * 2 + [whole(side_y)] * 2,
        out_specs=[plane, whole(side_x), whole(side_x), whole(side_y), whole(side_y), whole(side_x), whole(side_y), whole((8, 128))],
        out_shape=[shape(*field), shape(*side_x), shape(*side_x), shape(*side_y), shape(*side_y), shape(*side_x), shape(*side_y), shape(8, 128)],
        scratch_shapes=[pltpu.VMEM(side_x, F32), pltpu.VMEM((4, 8, nz), F32)],
        compiler_params=params(),
    )(density, s, below_x[0], dens_ax, below_y[0], dens_ay, s_bx, s_ax, s_by, s_ay)

    q_ax = shifted(q_x0, "gx", -1)
    q_ay = shifted(q_y0, "gy", -1)
    sums = pl.pallas_call(edge_kernel, out_shape=shape(8, 128), compiler_params=params())(
        sums, q_x1, q_y1, beta_x, beta_y, q_ax, q_ay
    )
    sums = total(sums)

    half = hidden * 8
    long = ny // 8 * nz
    grad, grads = pl.pallas_call(
        closure_kernel,
        grid=(nx,),
        in_specs=[
            whole((8, 128)), planes, whole(field), whole(field), whole(side_x), whole(side_x), whole(side_y), whole(side_y),
            pl.BlockSpec((count, 1, ny, nz), lambda i: (0, i, 0, 0)), whole(w_in.shape), whole(w_out.shape),
        ],
        out_specs=[planes, whole((16, 128))],
        out_shape=[shape(3, *field), shape(16, 128)],
        scratch_shapes=[
            pltpu.VMEM((3, ny, nz), F32),
            pltpu.VMEM((half, long), BF16),
            pltpu.VMEM((half, long), BF16),
            pltpu.VMEM((32, long), BF16),
            pltpu.VMEM((24 * count, long), BF16),
            pltpu.VMEM((32, half), F32),
            pltpu.VMEM((24 * count, half), F32),
        ],
        compiler_params=params(),
    )(sums, cotangent, s, q, s_ax, q_ax, s_ay, q_ay, features, w_in, w_out)
    grads = total(grads) / cells
    return grad, grads[:count, :hidden].T, grads[count : count + 3, :hidden]


def solution(mesh):
    in_specs = (P("gx", "gy", None), P(None, "gx", "gy", None), P(None, "gx", "gy", None), P(), P())
    out_specs = (P(None, "gx", "gy", None), P(), P())
    return jax.shard_map(body, mesh=mesh, in_specs=in_specs, out_specs=out_specs, check_vma=False)
```

time: 616 us -> 208 us (0.34); the launches traced: 606 us -> 207 us
  blocking collectives: 269 us -> 0 us
  matrix products: 141 us -> 0 us
  Pallas kernels: 0 us -> 93.6 us
  local copies, waits for them, and re-layouts: 98.6 us -> 12.9 us
  other arithmetic: 35.1 us -> 2.32 us
  starting transfers between devices: 37.5 us -> 64 us
  waiting for transfers between devices: 19.5 us -> 33.3 us
    psum x4 -> x0, blocking collectives: 269 us -> none  [the longest x2 136 us: squares(): return lax.psum(jnp.sum(residual * residual), ('gx', 'gy'))]
    dot_general x24 -> x0, matrix products: 141 us -> none  [the longest x8 85.3 us: step(): lax.dot_general(dpre, block, (((1,), (1,)), ((), ())), preferred_element_...]
    pallas_call x0 -> x4, Pallas kernels: none -> 93.6 us  [the longest x1 67.7 us: body(): pl.pallas_call(closure_kernel, grid=(nx,), in_specs=[whole((8, 128)), pla...]
    while x16 -> x0, local copies, waits for them, and re-layouts: 45.7 us -> none
    unnamed x42 -> x28, local copies, waits for them, and re-layouts: 42.6 us -> 2.83 us
    ppermute x2 -> x10, starting transfers between devices: 6.67 us -> 24.8 us  [shifted(): return lax.ppermute(value, axis, pairs)]
    mul x9 -> x1, other arithmetic: 12.3 us -> 0.2 us  [body(): w_inner[None, :, None, :, None] * pick[:, None, :, None, :].astype(BF16)]
    ppermute x2 -> x10, waiting for transfers between devices: 0.01 us -> 10.8 us  [shifted(): return lax.ppermute(value, axis, pairs)]
  transfers between devices with their start and end apart: 14 -> 30, of which waited for: 5 -> 17; matrix products, arithmetic and copies ran while one was open for 2% -> 4% of each run, Pallas kernels for 0% -> 0%
where the time goes in v1:
time: 208 us; the launch traced here: 207 us
  Pallas kernels  93.6 us (45%)
  starting transfers between devices  64 us (31%)
  waiting for transfers between devices  33.3 us (16%)
  local copies, waits for them, and re-layouts  12.9 us (6%)
  other arithmetic  2.32 us (1%)
    pallas_call x1, Pallas kernels, body(): pl.pallas_call(closure_kernel, grid=(nx,), in_specs=[whole((8, 128)), pla...  67.7 us
    ppermute x20, starting transfers between devices, total(): level.append(lax.ppermute(value, ('gx', 'gy'), pairs))  39.3 us
    ppermute x10, starting transfers between devices, shifted(): return lax.ppermute(value, axis, pairs)  24.8 us
    ppermute x20, waiting for transfers between devices, total(): level.append(lax.ppermute(value, ('gx', 'gy'), pairs))  22.4 us
    pallas_call x1, Pallas kernels, body(): pl.pallas_call(source_kernel, grid=(nx,), in_specs=[whole(field), planes,...  12.8 us
    pallas_call x1, Pallas kernels, body(): pl.pallas_call(image_kernel, grid=(nx,), in_specs=[whole(field)] * 2 + [w...  11.5 us
    ppermute x10, waiting for transfers between devices, shifted(): return lax.ppermute(value, axis, pairs)  10.8 us
  transfers between devices with their start and end apart: 30, of which 17 were waited for; matrix products, arithmetic and copies ran while one was open for 4% of the time, Pallas kernels for 0%

profile of v1, /device:TPU:0, one launch (start us, length us, event | category | flops | bytes accessed | tf_op | source)
XLA Modules:
  0.0 207.1 jit_solution(14021038392493880090)
XLA Ops:
  5.8 6.3 %collective-permute-start.2 = (f32[2,16,256]{2,1,0:T(8,128)S(1)}, f32[2,16,256]{2,1,0:T(8,128)S(1)}, u32[]{:S(2)}, u32[]{:S(2)}) collective-permute-start(f32[2,16,256]{2,1,0:T(8,128)S(1)} %pad_maximum_fusion.1), channel_id=1, source_target_pairs={{0,1},{1,2},{2,3},{3,4},{4,5},{5,6},{6,7},{8,9},{9,10},{10,11},{11... | collective-permute-start | bytes 98312 | tf_op jit(solution)/shard_map/ppermute | solution.py:18
  15.4 3.9 %collective-permute-done.3.above_y.dens_ay = f32[16,256]{1,0:T(8,128)S(1)} collective-permute-done((f32[16,256]{1,0:T(8,128)S(1)}, f32[16,256]{1,0:T(8,128)S(1)}, u32[]{:S(2)}, u32[]{:S(2)}) %collective-permute-start.3) | collective-permute-done | bytes 16416 | tf_op jit(solution)/shard_map/ppermute | solution.py:18
  20.7 12.8 %shard_map.76 = (f32[16,128,256]{2,1,0:T(8,128)}, f32[128,256]{1,0:T(8,128)}, f32[128,256]{1,0:T(8,128)}, f32[16,256]{1,0:T(8,128)}, f32[16,256]{1,0:T(8,128)}) custom-call(f32[16,128,256]{2,1,0:T(8,128)} %dens.3, f32[3,16,128,256]{3,2,1,0:T(8,128)} %cot.3, f32[2,128,256]{2,1,0:T(8,128)} %copy-done, f32[128,256]{1,0:T(8,128)} %copy-done.3, ...), custom_call_target="tpu_custom_call" | custom-call | tf_op jit(solution)/shard_map/pallas_call | solution.py:272
  33.5 4.2 %collective-permute-start.6 = (f32[16,256]{1,0:T(8,128)}, f32[16,256]{1,0:T(8,128)S(1)}, u32[]{:S(2)}, u32[]{:S(2)}) collective-permute-start(f32[16,256]{1,0:T(8,128)} %get-tuple-element.21), channel_id=1, source_target_pairs={{0,1},{1,2},{2,3},{3,4},{4,5},{5,6},{6,7},{8,9},{9,10},{10,11},{11... | collective-permute-start | bytes 49160 | tf_op jit(solution)/shard_map/ppermute | solution.py:18
  39.0 5.2 %collective-permute-start.4 = (f32[128,256]{1,0:T(8,128)}, f32[128,256]{1,0:T(8,128)S(1)}, u32[]{:S(2)}, u32[]{:S(2)}) collective-permute-start(f32[128,256]{1,0:T(8,128)} %get-tuple-element.19), channel_id=1, source_target_pairs={{0,8},{8,16},{16,24},{24,32},{32,40},{40,48},{48,56},{56,64},{64,7... | collective-permute-start | bytes 393224 | tf_op jit(solution)/shard_map/ppermute | solution.py:18
  48.3 11.5 %shard_map.77 = (f32[16,128,256]{2,1,0:T(8,128)}, f32[128,256]{1,0:T(8,128)}, f32[128,256]{1,0:T(8,128)}, f32[16,256]{1,0:T(8,128)}, f32[16,256]{1,0:T(8,128)}, ...) custom-call(f32[16,128,256]{2,1,0:T(8,128)} %dens.3, f32[16,128,256]{2,1,0:T(8,128)} %get-tuple-element.18.s, ...), custom_call_target="tpu_custom_call" | custom-call | tf_op jit(solution)/shard_map/pallas_call | solution.py:287
  62.4 6.4 %collective-permute-done.9.q_ay = f32[16,256]{1,0:T(8,128)S(1)} collective-permute-done((f32[16,256]{1,0:T(8,128)}, f32[16,256]{1,0:T(8,128)S(1)}, u32[]{:S(2)}, u32[]{:S(2)}) %collective-permute-start.9) | collective-permute-done | bytes 16416 | tf_op jit(solution)/shard_map/ppermute | solution.py:18
  71.2 4.4 %collective-permute-start.12 = (f32[8,128]{1,0:T(8,128)}, f32[8,128]{1,0:T(8,128)S(1)}, u32[]{:S(2)}, u32[]{:S(2)}) collective-permute-start(f32[8,128]{1,0:T(8,128)} %shard_map.78), channel_id=1, source_target_pairs={{0,24},{1,25},{2,26},{3,27},{4,28},{5,29},{6,30},{7,31},{8,16},{9,... | collective-permute-start | bytes 12296 | tf_op jit(solution)/shard_map/ppermute | solution.py:30
  77.1 2.3 %collective-permute-done.11 = f32[8,128]{1,0:T(8,128)S(1)} collective-permute-done((f32[8,128]{1,0:T(8,128)}, f32[8,128]{1,0:T(8,128)S(1)}, u32[]{:S(2)}, u32[]{:S(2)}) %collective-permute-start.11) | collective-permute-done | bytes 4128 | tf_op jit(solution)/shard_map/ppermute | solution.py:30
  80.1 3.4 %collective-permute-start.15 = (f32[8,128]{1,0:T(8,128)S(1)}, f32[8,128]{1,0:T(8,128)S(1)}, u32[]{:S(2)}, u32[]{:S(2)}) collective-permute-start(f32[8,128]{1,0:T(8,128)S(1)} %add_add_fusion.5), channel_id=1, source_target_pairs={{0,96},{1,97},{2,98},{3,99},{4,100},{5,101},{6,102},{7,103},{8,104... | collective-permute-start | bytes 12296 | tf_op jit(solution)/shard_map/ppermute | solution.py:30
  83.5 4.9 %collective-permute-start.14 = (f32[8,128]{1,0:T(8,128)S(1)}, f32[8,128]{1,0:T(8,128)S(1)}, u32[]{:S(2)}, u32[]{:S(2)}) collective-permute-start(f32[8,128]{1,0:T(8,128)S(1)} %add_add_fusion.5), channel_id=1, source_target_pairs={{0,64},{1,65},{2,66},{3,67},{4,68},{5,69},{6,70},{7,71},{8,72},{9,... | collective-permute-start | bytes 12296 | tf_op jit(solution)/shard_map/ppermute | solution.py:30
  90.2 3.3 %collective-permute-done.13 = f32[8,128]{1,0:T(8,128)S(1)} collective-permute-done((f32[8,128]{1,0:T(8,128)S(1)}, f32[8,128]{1,0:T(8,128)S(1)}, u32[]{:S(2)}, u32[]{:S(2)}) %collective-permute-start.13) | collective-permute-done | bytes 4128 | tf_op jit(solution)/shard_map/ppermute | solution.py:30
  93.5 5.1 %collective-permute-start.18 = (f32[8,128]{1,0:T(8,128)S(1)}, f32[8,128]{1,0:T(8,128)S(1)}, u32[]{:S(2)}, u32[]{:S(2)}) collective-permute-start(f32[8,128]{1,0:T(8,128)S(1)} %add_add_fusion.4), channel_id=1, source_target_pairs={{0,3},{1,2},{2,1},{3,0},{4,7},{5,6},{6,5},{7,4},{8,11},{9,10},{10,... | collective-permute-start | bytes 12296 | tf_op jit(solution)/shard_map/ppermute | solution.py:30
  100.2 2.0 collective-permute-done.17
  102.2 2.0 collective-permute-done.16
  104.2 3.0 %collective-permute-start.19 = (f32[8,128]{1,0:T(8,128)S(1)}, f32[8,128]{1,0:T(8,128)S(1)}, u32[]{:S(2)}, u32[]{:S(2)}) collective-permute-start(f32[8,128]{1,0:T(8,128)S(1)} %add_add_fusion.3), channel_id=1, source_target_pairs={{0,4},{1,5},{2,6},{3,7},{4,0},{5,1},{6,2},{7,3},{8,12},{9,13},{10,... | collective-permute-start | bytes 12296 | tf_op jit(solution)/shard_map/ppermute | solution.py:30
  108.3 2.0 mul.20.w_in
  110.9 67.7 %shard_map.79 = (f32[3,16,128,256]{3,2,1,0:T(8,128)}, f32[16,128]{1,0:T(8,128)}) custom-call(f32[8,128]{1,0:T(8,128)} %add.75.sums, f32[3,16,128,256]{3,2,1,0:T(8,128)} %cot.3, f32[16,128,256]{2,1,0:T(8,128)} %get-tuple-element.18.s, f32[16,128,256]{2,1,0:T(8,128)} %get-tuple-element.30.q, f32[128,256]{1,0:T(8,128)} %copy-done.1, f32[128,256]{1,0:T(8,128)} %copy-done.2, ...), custom_call_target="tpu_custom_call" | custom-call | tf_op jit(solution)/shard_map/pallas_call | solution.py:306
  183.3 3.5 %collective-permute-start.25 = (f32[16,128]{1,0:T(8,128)S(1)}, f32[16,128]{1,0:T(8,128)S(1)}, u32[]{:S(2)}, u32[]{:S(2)}) collective-permute-start(f32[16,128]{1,0:T(8,128)S(1)} %add_add_fusion.2), channel_id=1, source_target_pairs={{0,96},{1,97},{2,98},{3,99},{4,100},{5,101},{6,102},{7,103},{8,104... | collective-permute-start | bytes 24584 | tf_op jit(solution)/shard_map/ppermute | solution.py:30
  190.5 2.1 %collective-permute-done.23 = f32[16,128]{1,0:T(8,128)S(1)} collective-permute-done((f32[16,128]{1,0:T(8,128)S(1)}, f32[16,128]{1,0:T(8,128)S(1)}, u32[]{:S(2)}, u32[]{:S(2)}) %collective-permute-start.23) | collective-permute-done | bytes 8224 | tf_op jit(solution)/shard_map/ppermute | solution.py:30
  195.6 2.1 %collective-permute-start.26 = (f32[16,128]{1,0:T(8,128)S(1)}, f32[16,128]{1,0:T(8,128)S(1)}, u32[]{:S(2)}, u32[]{:S(2)}) collective-permute-start(f32[16,128]{1,0:T(8,128)S(1)} %add_add_fusion.1), channel_id=1, source_target_pairs={{0,1},{1,0},{2,3},{3,2},{4,5},{5,4},{6,7},{7,6},{8,9},{9,8},{10,11... | collective-permute-start | bytes 24584 | tf_op jit(solution)/shard_map/ppermute | solution.py:30
  198.7 2.0 collective-permute-done.26
  200.7 2.0 collective-permute-start.29
  202.8 3.1 %collective-permute-done.29 = f32[16,128]{1,0:T(8,128)S(1)} collective-permute-done((f32[16,128]{1,0:T(8,128)S(1)}, f32[16,128]{1,0:T(8,128)S(1)}, u32[]{:S(2)}, u32[]{:S(2)}) %collective-permute-start.29) | collective-permute-done | bytes 8224 | tf_op jit(solution)/shard_map/ppermute | solution.py:30
  (92 shorter events, 40.8 us)
Async XLA Ops:
  2.6 16.8 %collective-permute-start = (f32[2,128,256]{2,1,0:T(8,128)S(1)}, f32[2,128,256]{2,1,0:T(8,128)S(1)}, u32[]{:S(2)}, u32[]{:S(2)}) collective-permute-start(f32[2,128,256]{2,1,0:T(8,128)S(1)} %pad_maximum_fusion), channel_id=1, source_target_pairs={{0,8},{8,16},{16,24},{24,32},{32,40},{40,48},{48,56},{56,64},{64,7... | collective-permute-start | bytes 786440 | tf_op jit(solution)/shard_map/ppermute | solution.py:18
  5.8 8.9 %collective-permute-start.2 = (f32[2,16,256]{2,1,0:T(8,128)S(1)}, f32[2,16,256]{2,1,0:T(8,128)S(1)}, u32[]{:S(2)}, u32[]{:S(2)}) collective-permute-start(f32[2,16,256]{2,1,0:T(8,128)S(1)} %pad_maximum_fusion.1), channel_id=1, source_target_pairs={{0,1},{1,2},{2,3},{3,4},{4,5},{5,6},{6,7},{8,9},{9,10},{10,11},{11... | collective-permute-start | bytes 98312 | tf_op jit(solution)/shard_map/ppermute | solution.py:18
  12.2 7.1 %collective-permute-start.3 = (f32[16,256]{1,0:T(8,128)S(1)}, f32[16,256]{1,0:T(8,128)S(1)}, u32[]{:S(2)}, u32[]{:S(2)}) collective-permute-start(f32[16,256]{1,0:T(8,128)S(1)} %bitcast.23), channel_id=1, source_target_pairs={{1,0},{2,1},{3,2},{4,3},{5,4},{6,5},{7,6},{9,8},{10,9},{11,10},{12... | collective-permute-start | bytes 49160 | tf_op jit(solution)/shard_map/ppermute | solution.py:18
  13.5 5.8 %collective-permute-start.1 = (f32[128,256]{1,0:T(8,128)S(1)}, f32[128,256]{1,0:T(8,128)S(1)}, u32[]{:S(2)}, u32[]{:S(2)}) collective-permute-start(f32[128,256]{1,0:T(8,128)S(1)} %get-tuple-element.35), channel_id=1, source_target_pairs={{8,0},{16,8},{24,16},{32,24},{40,32},{48,40},{56,48},{64,56},{72,6... | collective-permute-start | bytes 393224 | tf_op jit(solution)/shard_map/ppermute | solution.py:18
  33.5 13.6 %collective-permute-start.6 = (f32[16,256]{1,0:T(8,128)}, f32[16,256]{1,0:T(8,128)S(1)}, u32[]{:S(2)}, u32[]{:S(2)}) collective-permute-start(f32[16,256]{1,0:T(8,128)} %get-tuple-element.21), channel_id=1, source_target_pairs={{0,1},{1,2},{2,3},{3,4},{4,5},{5,6},{6,7},{8,9},{9,10},{10,11},{11... | collective-permute-start | bytes 49160 | tf_op jit(solution)/shard_map/ppermute | solution.py:18
  37.7 9.4 %collective-permute-start.7 = (f32[16,256]{1,0:T(8,128)}, f32[16,256]{1,0:T(8,128)S(1)}, u32[]{:S(2)}, u32[]{:S(2)}) collective-permute-start(f32[16,256]{1,0:T(8,128)} %get-tuple-element.22), channel_id=1, source_target_pairs={{1,0},{2,1},{3,2},{4,3},{5,4},{6,5},{7,6},{9,8},{10,9},{11,10},{12... | collective-permute-start | bytes 49160 | tf_op jit(solution)/shard_map/ppermute | solution.py:18
  39.0 8.1 %collective-permute-start.4 = (f32[128,256]{1,0:T(8,128)}, f32[128,256]{1,0:T(8,128)S(1)}, u32[]{:S(2)}, u32[]{:S(2)}) collective-permute-start(f32[128,256]{1,0:T(8,128)} %get-tuple-element.19), channel_id=1, source_target_pairs={{0,8},{8,16},{16,24},{24,32},{32,40},{40,48},{48,56},{56,64},{64,7... | collective-permute-start | bytes 393224 | tf_op jit(solution)/shard_map/ppermute | solution.py:18
  59.8 9.0 %collective-permute-start.8 = (f32[128,256]{1,0:T(8,128)}, f32[128,256]{1,0:T(8,128)S(1)}, u32[]{:S(2)}, u32[]{:S(2)}) collective-permute-start(f32[128,256]{1,0:T(8,128)} %get-tuple-element.28), channel_id=1, source_target_pairs={{8,0},{16,8},{24,16},{32,24},{40,32},{48,40},{56,48},{64,56},{72,6... | collective-permute-start | bytes 393224 | tf_op jit(solution)/shard_map/ppermute | solution.py:18
  61.1 7.7 %collective-permute-start.9 = (f32[16,256]{1,0:T(8,128)}, f32[16,256]{1,0:T(8,128)S(1)}, u32[]{:S(2)}, u32[]{:S(2)}) collective-permute-start(f32[16,256]{1,0:T(8,128)} %get-tuple-element.29), channel_id=1, source_target_pairs={{1,0},{2,1},{3,2},{4,3},{5,4},{6,5},{7,6},{9,8},{10,9},{11,10},{12... | collective-permute-start | bytes 49160 | tf_op jit(solution)/shard_map/ppermute | solution.py:18
  71.2 6.0 %collective-permute-start.12 = (f32[8,128]{1,0:T(8,128)}, f32[8,128]{1,0:T(8,128)S(1)}, u32[]{:S(2)}, u32[]{:S(2)}) collective-permute-start(f32[8,128]{1,0:T(8,128)} %shard_map.78), channel_id=1, source_target_pairs={{0,24},{1,25},{2,26},{3,27},{4,28},{5,29},{6,30},{7,31},{8,16},{9,... | collective-permute-start | bytes 12296 | tf_op jit(solution)/shard_map/ppermute | solution.py:30
  80.1 10.1 %collective-permute-start.15 = (f32[8,128]{1,0:T(8,128)S(1)}, f32[8,128]{1,0:T(8,128)S(1)}, u32[]{:S(2)}, u32[]{:S(2)}) collective-permute-start(f32[8,128]{1,0:T(8,128)S(1)} %add_add_fusion.5), channel_id=1, source_target_pairs={{0,96},{1,97},{2,98},{3,99},{4,100},{5,101},{6,102},{7,103},{8,104... | collective-permute-start | bytes 12296 | tf_op jit(solution)/shard_map/ppermute | solution.py:30
  83.5 6.7 %collective-permute-start.14 = (f32[8,128]{1,0:T(8,128)S(1)}, f32[8,128]{1,0:T(8,128)S(1)}, u32[]{:S(2)}, u32[]{:S(2)}) collective-permute-start(f32[8,128]{1,0:T(8,128)S(1)} %add_add_fusion.5), channel_id=1, source_target_pairs={{0,64},{1,65},{2,66},{3,67},{4,68},{5,69},{6,70},{7,71},{8,72},{9,... | collective-permute-start | bytes 12296 | tf_op jit(solution)/shard_map/ppermute | solution.py:30
  88.4 5.1 %collective-permute-start.13 = (f32[8,128]{1,0:T(8,128)S(1)}, f32[8,128]{1,0:T(8,128)S(1)}, u32[]{:S(2)}, u32[]{:S(2)}) collective-permute-start(f32[8,128]{1,0:T(8,128)S(1)} %add_add_fusion.5), channel_id=1, source_target_pairs={{0,32},{1,33},{2,34},{3,35},{4,36},{5,37},{6,38},{7,39},{8,40},{9,... | collective-permute-start | bytes 12296 | tf_op jit(solution)/shard_map/ppermute | solution.py:30
  93.5 6.7 %collective-permute-start.18 = (f32[8,128]{1,0:T(8,128)S(1)}, f32[8,128]{1,0:T(8,128)S(1)}, u32[]{:S(2)}, u32[]{:S(2)}) collective-permute-start(f32[8,128]{1,0:T(8,128)S(1)} %add_add_fusion.4), channel_id=1, source_target_pairs={{0,3},{1,2},{2,1},{3,0},{4,7},{5,6},{6,5},{7,4},{8,11},{9,10},{10,... | collective-permute-start | bytes 12296 | tf_op jit(solution)/shard_map/ppermute | solution.py:30
  99.1 5.1 %collective-permute-start.16 = (f32[8,128]{1,0:T(8,128)S(1)}, f32[8,128]{1,0:T(8,128)S(1)}, u32[]{:S(2)}, u32[]{:S(2)}) collective-permute-start(f32[8,128]{1,0:T(8,128)S(1)} %add_add_fusion.4), channel_id=1, source_target_pairs={{0,1},{1,0},{2,3},{3,2},{4,5},{5,4},{6,7},{7,6},{8,9},{9,8},{10,11... | collective-permute-start | bytes 12296 | tf_op jit(solution)/shard_map/ppermute | solution.py:30
  104.2 6.1 %collective-permute-start.19 = (f32[8,128]{1,0:T(8,128)S(1)}, f32[8,128]{1,0:T(8,128)S(1)}, u32[]{:S(2)}, u32[]{:S(2)}) collective-permute-start(f32[8,128]{1,0:T(8,128)S(1)} %add_add_fusion.3), channel_id=1, source_target_pairs={{0,4},{1,5},{2,6},{3,7},{4,0},{5,1},{6,2},{7,3},{8,12},{9,13},{10,... | collective-permute-start | bytes 12296 | tf_op jit(solution)/shard_map/ppermute | solution.py:30
  178.7 3.9 %collective-permute-start.21 = (f32[16,128]{1,0:T(8,128)}, f32[16,128]{1,0:T(8,128)S(1)}, u32[]{:S(2)}, u32[]{:S(2)}) collective-permute-start(f32[16,128]{1,0:T(8,128)} %get-tuple-element.32), channel_id=1, source_target_pairs={{0,16},{1,17},{2,18},{3,19},{4,20},{5,21},{6,22},{7,23},{8,24},{9,... | collective-permute-start | bytes 24584 | tf_op jit(solution)/shard_map/ppermute | solution.py:30
  178.8 3.9 %collective-permute-start.20 = (f32[16,128]{1,0:T(8,128)}, f32[16,128]{1,0:T(8,128)S(1)}, u32[]{:S(2)}, u32[]{:S(2)}) collective-permute-start(f32[16,128]{1,0:T(8,128)} %get-tuple-element.32), channel_id=1, source_target_pairs={{0,8},{1,9},{2,10},{3,11},{4,12},{5,13},{6,14},{7,15},{8,0},{9,1},... | collective-permute-start | bytes 24584 | tf_op jit(solution)/shard_map/ppermute | solution.py:30
  183.3 6.1 %collective-permute-start.25 = (f32[16,128]{1,0:T(8,128)S(1)}, f32[16,128]{1,0:T(8,128)S(1)}, u32[]{:S(2)}, u32[]{:S(2)}) collective-permute-start(f32[16,128]{1,0:T(8,128)S(1)} %add_add_fusion.2), channel_id=1, source_target_pairs={{0,96},{1,97},{2,98},{3,99},{4,100},{5,101},{6,102},{7,103},{8,104... | collective-permute-start | bytes 24584 | tf_op jit(solution)/shard_map/ppermute | solution.py:30
  187.5 5.2 %collective-permute-start.23 = (f32[16,128]{1,0:T(8,128)S(1)}, f32[16,128]{1,0:T(8,128)S(1)}, u32[]{:S(2)}, u32[]{:S(2)}) collective-permute-start(f32[16,128]{1,0:T(8,128)S(1)} %add_add_fusion.2), channel_id=1, source_target_pairs={{0,32},{1,33},{2,34},{3,35},{4,36},{5,37},{6,38},{7,39},{8,40},{9,... | collective-permute-start | bytes 24584 | tf_op jit(solution)/shard_map/ppermute | solution.py:30
  192.6 6.1 %collective-permute-start.28 = (f32[16,128]{1,0:T(8,128)S(1)}, f32[16,128]{1,0:T(8,128)S(1)}, u32[]{:S(2)}, u32[]{:S(2)}) collective-permute-start(f32[16,128]{1,0:T(8,128)S(1)} %add_add_fusion.1), channel_id=1, source_target_pairs={{0,3},{1,2},{2,1},{3,0},{4,7},{5,6},{6,5},{7,4},{8,11},{9,10},{10,... | collective-permute-start | bytes 24584 | tf_op jit(solution)/shard_map/ppermute | solution.py:30
  194.1 4.6 %collective-permute-start.27 = (f32[16,128]{1,0:T(8,128)S(1)}, f32[16,128]{1,0:T(8,128)S(1)}, u32[]{:S(2)}, u32[]{:S(2)}) collective-permute-start(f32[16,128]{1,0:T(8,128)S(1)} %add_add_fusion.1), channel_id=1, source_target_pairs={{0,2},{1,3},{2,0},{3,1},{4,6},{5,7},{6,4},{7,5},{8,10},{9,11},{10,... | collective-permute-start | bytes 24584 | tf_op jit(solution)/shard_map/ppermute | solution.py:30
  195.6 5.2 %collective-permute-start.26 = (f32[16,128]{1,0:T(8,128)S(1)}, f32[16,128]{1,0:T(8,128)S(1)}, u32[]{:S(2)}, u32[]{:S(2)}) collective-permute-start(f32[16,128]{1,0:T(8,128)S(1)} %add_add_fusion.1), channel_id=1, source_target_pairs={{0,1},{1,0},{2,3},{3,2},{4,5},{5,4},{6,7},{7,6},{8,9},{9,8},{10,11... | collective-permute-start | bytes 24584 | tf_op jit(solution)/shard_map/ppermute | solution.py:30
  200.7 5.2 %collective-permute-start.29 = (f32[16,128]{1,0:T(8,128)S(1)}, f32[16,128]{1,0:T(8,128)S(1)}, u32[]{:S(2)}, u32[]{:S(2)}) collective-permute-start(f32[16,128]{1,0:T(8,128)S(1)} %add_add_fusion), channel_id=1, source_target_pairs={{0,4},{1,5},{2,6},{3,7},{4,0},{5,1},{6,2},{7,3},{8,12},{9,13},{10,... | collective-permute-start | bytes 24584 | tf_op jit(solution)/shard_map/ppermute | solution.py:30
  (18 other events, 130.0 us)

commit v2 on v1

--- a/solution.py
+++ b/solution.py
@@ -7,8 +7,8 @@
 
 F32 = jnp.float32
 BF16 = jnp.bfloat16
-LAST = (((1,), (1,)), ((), ()))
-STAGES = ((8, 16), (32, 64), (1, 2), (4,))
+PLAIN = (((1,), (0,)), ((), ()))
+FIRST = (((0,), (0,)), ((), ()))
 VMEM = 56 * 2**20
 
 
@@ -18,20 +18,8 @@
     return lax.ppermute(value, axis, pairs)
 
 
-def total(value):
-    devices = lax.axis_size("gx") * lax.axis_size("gy")
-    for bits in STAGES:
-        level = [value]
-        masks = [0]
-        for bit in bits:
-            masks = masks + [mask ^ bit for mask in masks]
-        for mask in masks[1:]:
-            pairs = [(i, i ^ mask) for i in range(devices)]
-            level.append(lax.ppermute(value, ("gx", "gy"), pairs))
-        while len(level) > 1:
-            level = [level[k] + level[k + 1] for k in range(0, len(level), 2)]
-        value = level[0]
-    return value
+def collect(copies):
+    return lax.all_to_all(copies, ("gx", "gy"), 0, 0)
 
 
 def next_row(plane, row):
@@ -160,29 +148,38 @@
     jump_y = q_ay[...] - y_hi[...]
     edge = lanes(fold(beta_x[...] * jump_x * jump_x)) + lanes(fold(beta_y[...] * jump_y * jump_y))
     at = lax.broadcasted_iota(jnp.int32, (8, 128), 0)
-    out[...] = sums[...] + jnp.where(at == 3, edge, 0.0)
+    each = jnp.sum(sums[...] + jnp.where(at == 3, edge, 0.0), 1, keepdims=True)
+    at_lane = lax.broadcasted_iota(jnp.int32, (8, 128), 1)
+    row = jnp.sum(jnp.where(at == at_lane, each, 0.0), 0, keepdims=True)
+    out[...] = jnp.broadcast_to(row, out.shape)
 
 
 def closure_kernel(
     sums, cot, s, q, s_ax, q_ax, s_ay, q_ay, feats, w_in, w_out,
-    grad, grads, velocity, hid, slope, vel, prod, acc_o, acc_t,
+    grad, grads, scale, velocity, hid, slope, vel, prod, acc_o, acc_t,
 ):
     step, planes = pl.program_id(0), s.shape[0]
     rows, width = s.shape[1], s.shape[2]
     count = feats.shape[0]
-    m0, m1, m2, m3 = (jnp.sum(sums[k : k + 1], 1, keepdims=True) for k in range(4))
-    alpha0 = m0 / m1
-    rr1 = alpha0 * alpha0 * m2 - m0
-    beta = rr1 / m0
-    more = 1.0 + beta
-    alpha1 = rr1 / (more * more * m1 - 2.0 * more * alpha0 * m2 + alpha0 * alpha0 * m3)
-    on_s, on_q = alpha0 + alpha1 * more, -alpha1 * alpha0
-
-    @pl.when(step == 0)
-    def _():
+
+    @pl.when(step == 0)
+    def _():
+        all_sums = jnp.sum(sums[...], 0, keepdims=True)
+        at_lane = lax.broadcasted_iota(jnp.int32, (1, 128), 1)
+        m0, m1, m2, m3 = (
+            jnp.sum(jnp.where(at_lane == k, all_sums, 0.0), 1, keepdims=True) for k in range(4)
+        )
+        alpha0 = m0 / m1
+        rr1 = alpha0 * alpha0 * m2 - m0
+        beta = rr1 / m0
+        more = 1.0 + beta
+        alpha1 = rr1 / (more * more * m1 - 2.0 * more * alpha0 * m2 + alpha0 * alpha0 * m3)
+        scale[0] = jnp.broadcast_to(alpha0 + alpha1 * more, scale.shape[1:])
+        scale[1] = jnp.broadcast_to(-alpha1 * alpha0, scale.shape[1:])
         acc_o[...] = jnp.zeros_like(acc_o)
         acc_t[...] = jnp.zeros_like(acc_t)
 
+    on_s, on_q = scale[0][:1], scale[1][:1]
     last = step == planes - 1
     ahead = jnp.minimum(step + 1, planes - 1)
     row = pl.ds(step, 1)
@@ -194,28 +191,26 @@
         grad[a, 0] = value
         velocity[a] = value.astype(BF16).astype(F32)
 
-    half = w_in.shape[0] // 2
+    half = w_in.shape[1] // 2
     for block in range(rows // 16):
         at = slice(block * 16, block * 16 + 16)
         inner = feats[:, 0, at, :].reshape(count * 16, width)
-        pre = lax.dot_general(
-            w_in[...], inner, (((1,), (0,)), ((), ())), preferred_element_type=F32
-        )
+        pre = lax.dot_general(inner, w_in[...], FIRST, preferred_element_type=F32)
         hidden = jnp.tanh(pre)
         hidden_b = hidden.astype(BF16)
         slope_b = (1.0 - hidden * hidden).astype(BF16)
         wide = [feats[c, 0, at, :].astype(F32) for c in range(count)]
         for part in range(2):
             to = slice((block * 2 + part) * width, (block * 2 + part + 1) * width)
-            hid[:, to] = hidden_b[part * half : (part + 1) * half]
-            slope[:, to] = slope_b[part * half : (part + 1) * half]
+            hid[to, :] = hidden_b[:, part * half : (part + 1) * half]
+            slope[to, :] = slope_b[:, part * half : (part + 1) * half]
             low = block * 16 + part * 8
             vs = [velocity[a, low : low + 8, :] for a in range(3)]
             vel[:, to] = jnp.concatenate(vs + [jnp.zeros_like(vs[0])], 0).astype(BF16)
             fs = [f[part * 8 : part * 8 + 8] for f in wide]
             prod[:, to] = jnp.concatenate([v * f for v in vs for f in fs], 0).astype(BF16)
-    acc_o[...] += lax.dot_general(vel[...], hid[...], LAST, preferred_element_type=F32)
-    acc_t[...] += lax.dot_general(prod[...], slope[...], LAST, preferred_element_type=F32)
+    acc_o[...] += lax.dot_general(vel[...], hid[...], PLAIN, preferred_element_type=F32)
+    acc_t[...] += lax.dot_general(prod[...], slope[...], PLAIN, preferred_element_type=F32)
 
     @pl.when(last)
     def _():
@@ -230,13 +225,13 @@
         inner = sum(
             w_out[a : a + 1] * terms[a * count : (a + 1) * count] for a in range(3)
         )
-        both = jnp.concatenate([inner, outer, jnp.zeros_like(outer)], 0)
-        hidden_at = lax.broadcasted_iota(jnp.int32, (half, 128), 0) // 8
-        column = lax.broadcasted_iota(jnp.int32, (half, 128), 1)
+        both = jnp.concatenate([inner, outer[:3], jnp.zeros((5, half), F32)], 0)
+        hidden_at = lax.broadcasted_iota(jnp.int32, (half, 64), 0) // 8
+        column = lax.broadcasted_iota(jnp.int32, (half, 64), 1)
         pick = (hidden_at == column).astype(F32)
-        grads[...] = jnp.dot(
-            both, pick, precision=lax.Precision.HIGHEST, preferred_element_type=F32
-        )
+        sums16 = jnp.dot(both, pick, precision=lax.Precision.HIGHEST, preferred_element_type=F32)
+        value = jnp.concatenate([sums16[:8], sums16[8:]], 1)
+        grads[...] = jnp.broadcast_to(value[None], grads.shape)
 
 
 def whole(shape):
@@ -254,7 +249,8 @@
 def body(density, cotangent, features, w_inner, w_outer):
     nx, ny, nz = density.shape
     count, hidden = features.shape[0], w_inner.shape[0]
-    cells = float(density.size * lax.axis_size("gx") * lax.axis_size("gy"))
+    devices = lax.axis_size("gx") * lax.axis_size("gy")
+    cells = float(density.size * devices)
     field, side_x, side_y = (nx, ny, nz), (ny, nz), (nx, nz)
     plane = pl.BlockSpec((1, ny, nz), lambda i: (i, 0, 0))
     planes = pl.BlockSpec((3, 1, ny, nz), lambda i: (0, i, 0, 0))
@@ -264,9 +260,9 @@
     dens_ay = shifted(density[:, 0], "gy", -1)
     below_y = shifted(jnp.stack([density[:, -1], cotangent[1, :, -1]]), "gy", 1)
 
-    pick = jnp.arange(16)[None, None, :] == jnp.arange(16).reshape(2, 8)[:, :, None]
-    w_in = w_inner[None, :, None, :, None] * pick[:, None, :, None, :].astype(BF16)
-    w_in = w_in.reshape(2 * hidden * 8, count * 16)
+    pick = jnp.arange(16)[:, None, None] == jnp.arange(16).reshape(1, 2, 8)
+    w_in = w_inner.T[:, None, None, :, None] * pick[None, :, :, None, :].astype(BF16)
+    w_in = w_in.reshape(count * 16, 2 * hidden * 8)
     w_out = jnp.repeat(w_outer.astype(F32), 8, axis=1)
 
     s, s_x0, s_x1, s_y0, s_y1 = pl.pallas_call(
@@ -296,10 +292,10 @@
 
     q_ax = shifted(q_x0, "gx", -1)
     q_ay = shifted(q_y0, "gy", -1)
-    sums = pl.pallas_call(edge_kernel, out_shape=shape(8, 128), compiler_params=params())(
+    sums = pl.pallas_call(edge_kernel, out_shape=shape(devices, 128), compiler_params=params())(
         sums, q_x1, q_y1, beta_x, beta_y, q_ax, q_ay
     )
-    sums = total(sums)
+    sums = collect(sums)
 
     half = hidden * 8
     long = ny // 8 * nz
@@ -307,15 +303,16 @@
         closure_kernel,
         grid=(nx,),
         in_specs=[
-            whole((8, 128)), planes, whole(field), whole(field), whole(side_x), whole(side_x), whole(side_y), whole(side_y),
+            whole((devices, 128)), planes, whole(field), whole(field), whole(side_x), whole(side_x), whole(side_y), whole(side_y),
             pl.BlockSpec((count, 1, ny, nz), lambda i: (0, i, 0, 0)), whole(w_in.shape), whole(w_out.shape),
         ],
-        out_specs=[planes, whole((16, 128))],
-        out_shape=[shape(3, *field), shape(16, 128)],
+        out_specs=[planes, whole((devices, 8, 128))],
+        out_shape=[shape(3, *field), shape(devices, 8, 128)],
         scratch_shapes=[
+            pltpu.VMEM((2, 8, nz), F32),
             pltpu.VMEM((3, ny, nz), F32),
-            pltpu.VMEM((half, long), BF16),
-            pltpu.VMEM((half, long), BF16),
+            pltpu.VMEM((long, half), BF16),
+            pltpu.VMEM((long, half), BF16),
             pltpu.VMEM((32, long), BF16),
             pltpu.VMEM((24 * count, long), BF16),
             pltpu.VMEM((32, half), F32),
@@ -323,8 +320,8 @@
         ],
         compiler_params=params(),
     )(sums, cotangent, s, q, s_ax, q_ax, s_ay, q_ay, features, w_in, w_out)
-    grads = total(grads) / cells
-    return grad, grads[:count, :hidden].T, grads[count : count + 3, :hidden]
+    grads = jnp.sum(collect(grads), 0) / cells
+    return grad, grads[:, :hidden].T, grads[:3, hidden:]
 
 
 def solution(mesh):

time: 208 us -> 179 us (0.86)
  waiting for transfers between devices: 33.3 us -> 14.6 us
  blocking collectives: 0 us -> 18.2 us
  Pallas kernels: 93.6 us -> 79.6 us
  starting transfers between devices: 64 us -> 51 us
    ppermute x20 -> x0, starting transfers between devices: 39.3 us -> none  [total(): level.append(lax.ppermute(value, ('gx', 'gy'), pairs))]
    all_to_all x0 -> x1, starting transfers between devices: none -> 22.6 us  [collect(): return lax.all_to_all(copies, ('gx', 'gy'), 0, 0)]
    ppermute x20 -> x0, waiting for transfers between devices: 22.4 us -> none  [total(): level.append(lax.ppermute(value, ('gx', 'gy'), pairs))]
    all_to_all x0 -> x1, blocking collectives: none -> 18.2 us  [collect(): return lax.all_to_all(copies, ('gx', 'gy'), 0, 0)]
    pallas_call x2, Pallas kernels: 69.4 us -> 55.4 us  [the longest x1 53.6 us: body(): pl.pallas_call(closure_kernel, grid=(nx,), in_specs=[whole((devices, 128)...]
    all_to_all x0 -> x1, waiting for transfers between devices: none -> 6.05 us  [collect(): return lax.all_to_all(copies, ('gx', 'gy'), 0, 0)]
    ppermute x10, starting transfers between devices: 24.8 us -> 28.4 us  [shifted(): return lax.ppermute(value, axis, pairs)]
    ppermute x10, waiting for transfers between devices: 10.8 us -> 8.5 us  [shifted(): return lax.ppermute(value, axis, pairs)]
  transfers between devices with their start and end apart: 30 -> 11, of which waited for: 17 -> 4; matrix products, arithmetic and copies ran while one was open for 4% -> 5% of each run, Pallas kernels for 0% -> 0%
where the time goes in v2:
time: 179 us; the launch traced here: 178 us
  Pallas kernels  79.6 us (44%)
  starting transfers between devices  51 us (28%)
  blocking collectives  18.2 us (10%)
  waiting for transfers between devices  14.6 us (8%)
  local copies, waits for them, and re-layouts  13.2 us (7%)
    pallas_call x1, Pallas kernels, body(): pl.pallas_call(closure_kernel, grid=(nx,), in_specs=[whole((devices, 128)...  53.6 us
    ppermute x10, starting transfers between devices, shifted(): return lax.ppermute(value, axis, pairs)  28.4 us
    all_to_all x1, starting transfers between devices, collect(): return lax.all_to_all(copies, ('gx', 'gy'), 0, 0)  22.6 us
    all_to_all x1, blocking collectives, collect(): return lax.all_to_all(copies, ('gx', 'gy'), 0, 0)  18.2 us
    pallas_call x1, Pallas kernels, body(): pl.pallas_call(source_kernel, grid=(nx,), in_specs=[whole(field), planes,...  12.7 us
    pallas_call x1, Pallas kernels, body(): pl.pallas_call(image_kernel, grid=(nx,), in_specs=[whole(field)] * 2 + [w...  11.4 us
    ppermute x10, waiting for transfers between devices, shifted(): return lax.ppermute(value, axis, pairs)  8.5 us
    all_to_all x1, waiting for transfers between devices, collect(): return lax.all_to_all(copies, ('gx', 'gy'), 0, 0)  6.05 us
  transfers between devices with their start and end apart: 11, of which 4 were waited for; matrix products, arithmetic and copies ran while one was open for 5% of the time, Pallas kernels for 0%

profile of v2, /device:TPU:0, one launch (start us, length us, event | category | flops | bytes accessed | tf_op | source)
XLA Modules:
  0.0 178.0 jit_solution(1228200092396265349)
XLA Ops:
  0.6 1.0 fusion.1
  1.6 1.3 collective-permute-start.3
  2.9 0.9 slice.34
  3.9 6.5 %collective-permute-start.2 = (f32[2,16,256]{2,1,0:T(8,128)S(1)}, f32[2,16,256]{2,1,0:T(8,128)S(1)}, u32[]{:S(2)}, u32[]{:S(2)}) collective-permute-start(f32[2,16,256]{2,1,0:T(8,128)S(1)} %pad_maximum_fusion.1), channel_id=1, source_target_pairs={{0,1},{1,2},{2,3},{3,4},{4,5},{5,6},{6,7},{8,9},{9,10},{10,11},{11... | collective-permute-start | bytes 98312 | tf_op jit(solution)/shard_map/ppermute | solution.py:18
  10.4 1.0 slice_bitcast_fusion.1
  11.4 1.3 collective-permute-start.1
  13.6 3.0 %collective-permute-start = (f32[2,128,256]{2,1,0:T(8,128)S(1)}, f32[2,128,256]{2,1,0:T(8,128)S(1)}, u32[]{:S(2)}, u32[]{:S(2)}) collective-permute-start(f32[2,128,256]{2,1,0:T(8,128)S(1)} %pad_maximum_fusion), channel_id=1, source_target_pairs={{0,8},{8,16},{16,24},{24,32},{32,40},{40,48},{48,56},{56,64},{64,7... | collective-permute-start | bytes 786440 | tf_op jit(solution)/shard_map/ppermute | solution.py:18
  18.7 12.7 %shard_map.76 = (f32[16,128,256]{2,1,0:T(8,128)}, f32[128,256]{1,0:T(8,128)}, f32[128,256]{1,0:T(8,128)}, f32[16,256]{1,0:T(8,128)}, f32[16,256]{1,0:T(8,128)}) custom-call(f32[16,128,256]{2,1,0:T(8,128)} %dens.3, f32[3,16,128,256]{3,2,1,0:T(8,128)} %cot.3, f32[2,128,256]{2,1,0:T(8,128)} %copy-done, f32[128,256]{1,0:T(8,128)} %copy-done.2, ...), custom_call_target="tpu_custom_call" | custom-call | tf_op jit(solution)/shard_map/pallas_call | solution.py:268
  31.4 6.3 %collective-permute-start.6 = (f32[16,256]{1,0:T(8,128)}, f32[16,256]{1,0:T(8,128)S(1)}, u32[]{:S(2)}, u32[]{:S(2)}) collective-permute-start(f32[16,256]{1,0:T(8,128)} %get-tuple-element.21), channel_id=1, source_target_pairs={{0,1},{1,2},{2,3},{3,4},{4,5},{5,6},{6,7},{8,9},{9,10},{10,11},{11... | collective-permute-start | bytes 49160 | tf_op jit(solution)/shard_map/ppermute | solution.py:18
  37.8 1.3 collective-permute-start.7
  39.1 4.8 %collective-permute-start.4 = (f32[128,256]{1,0:T(8,128)}, f32[128,256]{1,0:T(8,128)S(1)}, u32[]{:S(2)}, u32[]{:S(2)}) collective-permute-start(f32[128,256]{1,0:T(8,128)} %get-tuple-element.19), channel_id=1, source_target_pairs={{0,8},{8,16},{16,24},{24,32},{32,40},{40,48},{48,56},{56,64},{64,7... | collective-permute-start | bytes 393224 | tf_op jit(solution)/shard_map/ppermute | solution.py:18
  43.9 1.3 collective-permute-start.5
  45.2 1.6 slice_bitcast_fusion.dens_bx
  46.8 2.8 %collective-permute-done.5.s_ax = f32[128,256]{1,0:T(8,128)S(1)} collective-permute-done((f32[128,256]{1,0:T(8,128)}, f32[128,256]{1,0:T(8,128)S(1)}, u32[]{:S(2)}, u32[]{:S(2)}) %collective-permute-start.5) | collective-permute-done | bytes 131104 | tf_op jit(solution)/shard_map/ppermute | solution.py:18
  50.2 11.4 %shard_map.77 = (f32[16,128,256]{2,1,0:T(8,128)}, f32[128,256]{1,0:T(8,128)}, f32[128,256]{1,0:T(8,128)}, f32[16,256]{1,0:T(8,128)}, f32[16,256]{1,0:T(8,128)}, ...) custom-call(f32[16,128,256]{2,1,0:T(8,128)} %dens.3, f32[16,128,256]{2,1,0:T(8,128)} %get-tuple-element.18.s, ...), custom_call_target="tpu_custom_call" | custom-call | tf_op jit(solution)/shard_map/pallas_call | solution.py:283
  61.7 1.3 collective-permute-start.9
  63.0 1.3 collective-permute-start.8
  64.5 5.2 %collective-permute-done.9.q_ay = f32[16,256]{1,0:T(8,128)S(1)} collective-permute-done((f32[16,256]{1,0:T(8,128)}, f32[16,256]{1,0:T(8,128)S(1)}, u32[]{:S(2)}, u32[]{:S(2)}) %collective-permute-start.9) | collective-permute-done | bytes 16416 | tf_op jit(solution)/shard_map/ppermute | solution.py:18
  70.4 1.8 %shard_map.78 = f32[128,128]{1,0:T(8,128)} custom-call(f32[8,128]{1,0:T(8,128)} %get-tuple-element.23.sums, f32[128,256]{1,0:T(8,128)} %get-tuple-element.24.x_hi, f32[16,256]{1,0:T(8,128)} %get-tuple-element.25.y_hi, f32[128,256]{1,0:T(8,128)} %get-tuple-element.26.beta_x, f32[16,256]{1,0:T(8,128)} %get-tuple-element.27.beta_y, f32[128,256]{1,0:T(8,128)} %copy-done.3, ...), custom_call_target="tpu_custom_call" | custom-call | tf_op jit(solution)/shard_map/pallas_call | solution.py:295
  72.1 22.6 %all-to-all-start = ((f32[128,1,128]{2,1,0:T(1,128)}), f32[128,1,128]{2,1,0:T(1,128)S(1)}, u32[]{:S(2)}, u32[]{:S(2)}) async-start(f32[128,1,128]{2,1,0:T(1,128)} %bitcast.29), calls=%async_computation | async-start | bytes 131072 | tf_op jit(solution)/shard_map/all_to_all | solution.py:22
  95.8 1.4 mul.20
  98.0 6.1 %all-to-all-done = f32[128,1,128]{2,1,0:T(1,128)S(1)} async-done(((f32[128,1,128]{2,1,0:T(1,128)}), f32[128,1,128]{2,1,0:T(1,128)S(1)}, u32[]{:S(2)}, u32[]{:S(2)}) %all-to-all-start) | async-done | bytes 65568 | tf_op jit(solution)/shard_map/all_to_all | solution.py:22
  104.7 53.6 %shard_map.79 = (f32[3,16,128,256]{3,2,1,0:T(8,128)}, f32[128,8,128]{2,1,0:T(8,128)}) custom-call(f32[128,128]{1,0:T(8,128)} %bitcast.28, f32[3,16,128,256]{3,2,1,0:T(8,128)} %cot.3, f32[16,128,256]{2,1,0:T(8,128)} %get-tuple-element.18.s, f32[16,128,256]{2,1,0:T(8,128)} %get-tuple-element.30.q, f32[128,256]{1,0:T(8,128)} %copy-done.1, ...), custom_call_target="tpu_custom_call" | custom-call | tf_op jit(solution)/shard_map/pallas_call | solution.py:302
  158.3 18.2 %all_to_all.16 = f32[128,8,128]{2,1,0:T(8,128)S(1)} all-to-all(f32[128,8,128]{2,1,0:T(8,128)} %get-tuple-element.32), channel_id=1, replica_groups=mesh['gx'=16,'gy'=8] {'gx','gy'}, dimensions={0} | all-to-all | bytes 1048576 | tf_op jit(solution)/shard_map/all_to_all | solution.py:22
  (52 shorter events, 8.3 us)
Async XLA Ops:
  1.6 15.7 %collective-permute-start.3 = (f32[16,256]{1,0:T(8,128)S(1)}, f32[16,256]{1,0:T(8,128)S(1)}, u32[]{:S(2)}, u32[]{:S(2)}) collective-permute-start(f32[16,256]{1,0:T(8,128)S(1)} %bitcast.32), channel_id=1, source_target_pairs={{1,0},{2,1},{3,2},{4,3},{5,4},{6,5},{7,6},{9,8},{10,9},{11,10},{12... | collective-permute-start | bytes 49160 | tf_op jit(solution)/shard_map/ppermute | solution.py:18
  3.9 12.8 %collective-permute-start.2 = (f32[2,16,256]{2,1,0:T(8,128)S(1)}, f32[2,16,256]{2,1,0:T(8,128)S(1)}, u32[]{:S(2)}, u32[]{:S(2)}) collective-permute-start(f32[2,16,256]{2,1,0:T(8,128)S(1)} %pad_maximum_fusion.1), channel_id=1, source_target_pairs={{0,1},{1,2},{2,3},{3,4},{4,5},{5,6},{6,7},{8,9},{9,10},{10,11},{11... | collective-permute-start | bytes 98312 | tf_op jit(solution)/shard_map/ppermute | solution.py:18
  11.4 6.0 %collective-permute-start.1 = (f32[128,256]{1,0:T(8,128)S(1)}, f32[128,256]{1,0:T(8,128)S(1)}, u32[]{:S(2)}, u32[]{:S(2)}) collective-permute-start(f32[128,256]{1,0:T(8,128)S(1)} %get-tuple-element.35), channel_id=1, source_target_pairs={{8,0},{16,8},{24,16},{32,24},{40,32},{48,40},{56,48},{64,56},{72,6... | collective-permute-start | bytes 393224 | tf_op jit(solution)/shard_map/ppermute | solution.py:18
  13.6 4.2 %collective-permute-start = (f32[2,128,256]{2,1,0:T(8,128)S(1)}, f32[2,128,256]{2,1,0:T(8,128)S(1)}, u32[]{:S(2)}, u32[]{:S(2)}) collective-permute-start(f32[2,128,256]{2,1,0:T(8,128)S(1)} %pad_maximum_fusion), channel_id=1, source_target_pairs={{0,8},{8,16},{16,24},{24,32},{32,40},{40,48},{48,56},{56,64},{64,7... | collective-permute-start | bytes 786440 | tf_op jit(solution)/shard_map/ppermute | solution.py:18
  16.7 1.1 copy-start.6
  17.3 0.6 copy-start.7
  17.3 0.7 copy-start.2
  18.0 0.7 copy-start
  31.4 15.3 %collective-permute-start.6 = (f32[16,256]{1,0:T(8,128)}, f32[16,256]{1,0:T(8,128)S(1)}, u32[]{:S(2)}, u32[]{:S(2)}) collective-permute-start(f32[16,256]{1,0:T(8,128)} %get-tuple-element.21), channel_id=1, source_target_pairs={{0,1},{1,2},{2,3},{3,4},{4,5},{5,6},{6,7},{8,9},{9,10},{10,11},{11... | collective-permute-start | bytes 49160 | tf_op jit(solution)/shard_map/ppermute | solution.py:18
  37.8 9.0 %collective-permute-start.7 = (f32[16,256]{1,0:T(8,128)}, f32[16,256]{1,0:T(8,128)S(1)}, u32[]{:S(2)}, u32[]{:S(2)}) collective-permute-start(f32[16,256]{1,0:T(8,128)} %get-tuple-element.22), channel_id=1, source_target_pairs={{1,0},{2,1},{3,2},{4,3},{5,4},{6,5},{7,6},{9,8},{10,9},{11,10},{12... | collective-permute-start | bytes 49160 | tf_op jit(solution)/shard_map/ppermute | solution.py:18
  39.1 7.7 %collective-permute-start.4 = (f32[128,256]{1,0:T(8,128)}, f32[128,256]{1,0:T(8,128)S(1)}, u32[]{:S(2)}, u32[]{:S(2)}) collective-permute-start(f32[128,256]{1,0:T(8,128)} %get-tuple-element.19), channel_id=1, source_target_pairs={{0,8},{8,16},{16,24},{24,32},{32,40},{40,48},{48,56},{56,64},{64,7... | collective-permute-start | bytes 393224 | tf_op jit(solution)/shard_map/ppermute | solution.py:18
  43.9 5.7 %collective-permute-start.5 = (f32[128,256]{1,0:T(8,128)}, f32[128,256]{1,0:T(8,128)S(1)}, u32[]{:S(2)}, u32[]{:S(2)}) collective-permute-start(f32[128,256]{1,0:T(8,128)} %get-tuple-element.20), channel_id=1, source_target_pairs={{8,0},{16,8},{24,16},{32,24},{40,32},{48,40},{56,48},{64,56},{72,6... | collective-permute-start | bytes 393224 | tf_op jit(solution)/shard_map/ppermute | solution.py:18
  46.7 2.9 %copy-start.10 = (f32[16,256]{1,0:T(8,128)}, f32[16,256]{1,0:T(8,128)S(1)}, u32[]{:S(2)}) copy-start(f32[16,256]{1,0:T(8,128)S(1)} %collective-permute-done.6.s_by) | copy-start | bytes 49156
  46.7 2.9 %copy-start.8 = (f32[16,256]{1,0:T(8,128)}, f32[16,256]{1,0:T(8,128)S(1)}, u32[]{:S(2)}) copy-start(f32[16,256]{1,0:T(8,128)S(1)} %collective-permute-done.7.s_ay) | copy-start | bytes 49156
  46.8 2.8 %copy-start.5 = (f32[128,256]{1,0:T(8,128)}, f32[128,256]{1,0:T(8,128)S(1)}, u32[]{:S(2)}) copy-start(f32[128,256]{1,0:T(8,128)S(1)} %collective-permute-done.4.s_bx) | copy-start | bytes 393220
  49.6 0.6 copy-start.1
  50.2 14.1 %copy-start.11 = (bf16[64,8]{0,1:T(8,128)(2,1)S(1)}, bf16[64,8]{0,1:T(8,128)(2,1)}, u32[]{:S(2)}) copy-start(bf16[64,8]{0,1:T(8,128)(2,1)} %param.8) | copy-start | bytes 3076
  61.7 33.3 %copy-start.12 = (bf16[3,64]{1,0:T(4,128)(2,1)S(1)}, bf16[3,64]{1,0:T(4,128)(2,1)}, u32[]{:S(2)}) copy-start(bf16[3,64]{1,0:T(4,128)(2,1)} %param.9) | copy-start | bytes 1156
  61.7 8.0 %collective-permute-start.9 = (f32[16,256]{1,0:T(8,128)}, f32[16,256]{1,0:T(8,128)S(1)}, u32[]{:S(2)}, u32[]{:S(2)}) collective-permute-start(f32[16,256]{1,0:T(8,128)} %get-tuple-element.29), channel_id=1, source_target_pairs={{1,0},{2,1},{3,2},{4,3},{5,4},{6,5},{7,6},{9,8},{10,9},{11,10},{12... | collective-permute-start | bytes 49160 | tf_op jit(solution)/shard_map/ppermute | solution.py:18
  63.0 6.7 %collective-permute-start.8 = (f32[128,256]{1,0:T(8,128)}, f32[128,256]{1,0:T(8,128)S(1)}, u32[]{:S(2)}, u32[]{:S(2)}) collective-permute-start(f32[128,256]{1,0:T(8,128)} %get-tuple-element.28), channel_id=1, source_target_pairs={{8,0},{16,8},{24,16},{32,24},{40,32},{48,40},{56,48},{64,56},{72,6... | collective-permute-start | bytes 393224 | tf_op jit(solution)/shard_map/ppermute | solution.py:18
  69.7 0.6 copy-start.9
  69.7 0.7 copy-start.3
  72.1 31.9 %all-to-all-start = ((f32[128,1,128]{2,1,0:T(1,128)}), f32[128,1,128]{2,1,0:T(1,128)S(1)}, u32[]{:S(2)}, u32[]{:S(2)}) async-start(f32[128,1,128]{2,1,0:T(1,128)} %bitcast.29), calls=%async_computation | async-start | bytes 131072 | tf_op jit(solution)/shard_map/all_to_all | solution.py:22
  104.1 0.6 copy-start.4

commit v3 on v2

v3 whole, which is shorter than its diff:
```python
import jax
import jax.numpy as jnp
from jax import lax
from jax.experimental import pallas as pl
from jax.experimental.pallas import tpu as pltpu
from jax.sharding import PartitionSpec as P

F32 = jnp.float32
BF16 = jnp.bfloat16
PLAIN = (((1,), (0,)), ((), ()))
FIRST = (((0,), (0,)), ((), ()))
VMEM = 56 * 2**20


def collect(copies):
    return lax.all_to_all(copies, ("gx", "gy"), 0, 0)


def neighbours(value, by_x, by_y):
    nx, ny = lax.axis_size("gx"), lax.axis_size("gy")
    pairs = [
        (i * ny + j, (i + by_x) * ny + j + by_y)
        for i in range(nx)
        for j in range(ny)
        if 0 <= i + by_x < nx and 0 <= j + by_y < ny
    ]
    return lax.ppermute(value, ("gx", "gy"), pairs)


def next_lane(plane):
    size = plane.shape[1]
    at = lax.broadcasted_iota(jnp.int32, plane.shape, 1)
    return jnp.where(at == size - 1, 0.0, pltpu.roll(plane, size - 1, 1))


def prior_lane(plane):
    at = lax.broadcasted_iota(jnp.int32, plane.shape, 1)
    return jnp.where(at == 0, 0.0, pltpu.roll(plane, 1, 1))


def next_row(plane):
    return pltpu.roll(plane, plane.shape[0] - 1, 0)


def prior_row(plane):
    return pltpu.roll(plane, 1, 0)


def fold(plane):
    return jnp.sum(plane.reshape(-1, 8, plane.shape[1]), 0)


def twice_over(value):
    return 2.0 / value


LOWER_X = ((0, 2), (1, 2), (2, 1), (3, 1))
UPPER_X = ((0, 3), (1, 2), (2, 2), (3, 2))
LOWER_Y = ((0, 2), (1, 1), (2, 2), (3, 1))
UPPER_Y = ((0, 3), (1, 2), (2, 2), (3, 2))


def starts(plan):
    places, at = [], 0
    for _, width in plan:
        places.append(at)
        at += width
    return places, at


def pack_kernel(
    d_first, d_last, c_first, c_last, d_low, d_high, c_low, c_high,
    up_x, down_x, up_y, down_y, up_up, up_down, down_up, down_down,
):
    planes = d_first.shape[0]
    for plan, to, d, c, low in ((LOWER_X, up_x, d_high, c_high, False), (UPPER_X, down_x, d_low, c_low, True)):
        at = 0
        for field, width in plan:
            block = d if field == 0 else c.at[field - 1]
            first = 0 if low else block.shape[0] - width
            for x in range(first, first + width):
                to[at] = block[x]
                at += 1

    def line(field, x, y):
        if field == 0:
            block = d_first if y >= 0 else d_last
            return block[x, y % 8 : y % 8 + 1, :]
        block = c_first if y >= 0 else c_last
        return block[field - 1, x, y % 8 : y % 8 + 1, :]

    for plan, to, low in ((LOWER_Y, up_y, False), (UPPER_Y, down_y, True)):
        at = 0
        for field, width in plan:
            for y in range(width):
                for x in range(planes):
                    to[at : at + 1, :] = line(field, x, y if low else y - width)
                    at += 1
    for to, first_x, first_y in (
        (up_up, planes - 2, -2), (up_down, planes - 2, 0), (down_up, 0, -2), (down_down, 0, 0),
    ):
        at = 0
        for field in range(4):
            for x in (first_x, first_x + 1):
                for y in (first_y, first_y + 1):
                    to[at : at + 1, :] = line(field, x, y)
                    at += 1


def moments_kernel(
    dens, cot, below_x, above_x, below_y, above_y, low_low, low_high, high_low, high_high,
    s_out, q_out, sums, d_all, b_x, b_y, b_z, s_all, before, acc,
):
    planes, rows, width = dens.shape
    own = slice(8, rows + 8)
    lower_x, upper_x = starts(LOWER_X)[0], starts(UPPER_X)[0]
    lower_y, upper_y = starts(LOWER_Y)[0], starts(UPPER_Y)[0]

    def tiles(below, above):
        low, high = (8 - sum(part.shape[0] for part in parts) for parts in (below, above))
        low = jnp.concatenate([jnp.zeros((low, width), F32)] + below, 0)
        return low, jnp.concatenate(above + [jnp.zeros((high, width), F32)], 0)

    def sides(field, x):
        low, high = LOWER_Y[field][1], UPPER_Y[field][1]
        below = [below_y[pl.ds((lower_y[field] + k) * planes + x, 1), :] for k in range(low)]
        above = [above_y[pl.ds((upper_y[field] + k) * planes + x, 1), :] for k in range(high)]
        return tiles(below, above)

    def corners(field, x):
        low, high = (low_low, low_high) if x < 0 else (high_low, high_high)
        at = field * 4 + (x % 2) * 2
        return tiles([low[at : at + 2, :]], [high[at : at + 2, :]])

    def plane_of(field, x):
        if x < 0:
            return below_x[lower_x[field] + x + LOWER_X[field][1]]
        return above_x[upper_x[field] + x - planes]

    def put(x, low, middle, high):
        d_all[x + 2, 0:8, :] = low
        d_all[x + 2, own, :] = middle
        d_all[x + 2, rows + 8 : rows + 16, :] = high

    def fill(x, carry):
        low, high = sides(0, x)
        put(x, low, dens[x], high)
        return carry

    for x in (-2, -1, planes, planes + 1):
        low, high = corners(0, x)
        put(x, low, plane_of(0, x), high)
    none = jnp.zeros((8, width), F32)
    put(planes + 2, none, plane_of(0, planes + 2), none)
    lax.fori_loop(0, planes, fill, 0)

    def weight(value, inside, after):
        return jnp.where(inside, twice_over(value + after), 0.0)

    def outer_field(field, x):
        low, high = corners(field, x)
        return jnp.concatenate([low, plane_of(field, x), high], 0)

    def own_field(field, x):
        low, high = sides(field, x)
        return jnp.concatenate([low, cot[field - 1, x], high], 0)

    def source(x, field_of):
        at = x + 2
        here = d_all[at]
        inside = here > 0
        beta = weight(here, inside, d_all[at + 1])
        b_x[at] = beta
        flux = beta * field_of(1, x)
        out = before[...] - flux
        before[...] = flux
        beta = weight(here, inside, next_row(here))
        b_y[at] = beta
        flux = beta * field_of(2, x)
        out = out + prior_row(flux) - flux
        beta = weight(here, inside, next_lane(here))
        b_z[at] = beta
        flux = beta * field_of(3, x)
        out = out + prior_lane(flux) - flux
        s_all[at] = jnp.where(inside, out, 0.0)

    here = d_all[0]
    before[...] = weight(here, here > 0, d_all[1]) * outer_field(1, -2)
    source(-1, outer_field)

    def own_source(x, carry):
        source(x, own_field)
        return carry

    lax.fori_loop(0, planes, own_source, 0)
    source(planes, outer_field)
    source(planes + 1, outer_field)

    def image(x):
        at = x + 2
        here = s_all[at]
        flux = b_x[at] * (s_all[at + 1] - here)
        out = before[...] - flux
        before[...] = flux
        flux = b_y[at] * (next_row(here) - here)
        out = out + (prior_row(flux) - flux)
        flux = b_z[at] * (next_lane(here) - here)
        out = out + (prior_lane(flux) - flux)
        out = jnp.where(d_all[at] > 0, out, 0.0)
        s_out[x] = here[8:]
        q_out[x] = out[8:]
        return here, out

    def squares(x, out):
        at = x + 2
        jump = (next_row(out) - out)[own]
        jump_z = next_lane(out[own]) - out[own]
        acc[3] += fold(b_y[at, own, :] * jump * jump + b_z[at, own, :] * jump_z * jump_z)

    def jumps(x, out):
        jump = out[own] - q_out[x - 1, 0:rows, :]
        acc[3] += fold(b_x[x + 1, own, :] * jump * jump)

    def products(here, out):
        here, out = here[own], out[own]
        acc[0] += fold(here * here)
        acc[1] += fold(here * out)
        acc[2] += fold(out * out)

    before[...] = b_x[1] * (s_all[2] - s_all[1])
    acc[...] = jnp.zeros_like(acc)
    here, out = image(0)
    products(here, out)
    squares(0, out)

    def own_image(x, carry):
        here, out = image(x)
        products(here, out)
        squares(x, out)
        jumps(x, out)
        return carry

    lax.fori_loop(1, planes, own_image, 0)
    here, out = image(planes)
    jumps(planes, out)
    at = lax.broadcasted_iota(jnp.int32, (1, 128), 1)
    row = jnp.zeros((1, 128), F32)
    for k in range(4):
        value = jnp.sum(jnp.sum(acc[k], 0, keepdims=True), 1, keepdims=True)
        row = row + jnp.where(at == k, value, 0.0)
    sums[...] = jnp.broadcast_to(row, sums.shape)


def closure_kernel(
    sums, cot, s, q, feats, w_in, w_out,
    grad, grads, scale, velocity, hid, slope, vel, prod, acc_o, acc_t,
):
    step, planes = pl.program_id(0), s.shape[0] - 1
    rows, width = cot.shape[2], s.shape[2]
    count = feats.shape[0]

    @pl.when(step == 0)
    def _():
        all_sums = jnp.sum(sums[...], 0, keepdims=True)
        at_lane = lax.broadcasted_iota(jnp.int32, (1, 128), 1)
        m0, m1, m2, m3 = (
            jnp.sum(jnp.where(at_lane == k, all_sums, 0.0), 1, keepdims=True) for k in range(4)
        )
        alpha0 = m0 / m1
        rr1 = alpha0 * alpha0 * m2 - m0
        beta = rr1 / m0
        more = 1.0 + beta
        alpha1 = rr1 / (more * more * m1 - 2.0 * more * alpha0 * m2 + alpha0 * alpha0 * m3)
        scale[0] = jnp.broadcast_to(alpha0 + alpha1 * more, scale.shape[1:])
        scale[1] = jnp.broadcast_to(-alpha1 * alpha0, scale.shape[1:])
        acc_o[...] = jnp.zeros_like(acc_o)
        acc_t[...] = jnp.zeros_like(acc_t)

    on_s, on_q = scale[0][:1], scale[1][:1]
    last = step == planes - 1
    wide = on_s * s[step] + on_q * q[step]
    here = wide[:rows]
    beyond = on_s * s[step + 1, :rows, :] + on_q * q[step + 1, :rows, :]
    for a, after in enumerate((beyond, next_row(wide)[:rows], next_lane(here))):
        value = cot[a, 0] - (after - here)
        grad[a, 0] = value
        velocity[a] = value.astype(BF16).astype(F32)

    half = w_in.shape[1] // 2
    for block in range(rows // 16):
        at = slice(block * 16, block * 16 + 16)
        inner = feats[:, 0, at, :].reshape(count * 16, width)
        pre = lax.dot_general(inner, w_in[...], FIRST, preferred_element_type=F32)
        hidden = jnp.tanh(pre)
        hidden_b = hidden.astype(BF16)
        slope_b = (1.0 - hidden * hidden).astype(BF16)
        wide = [feats[c, 0, at, :].astype(F32) for c in range(count)]
        for part in range(2):
            to = slice((block * 2 + part) * width, (block * 2 + part + 1) * width)
            hid[to, :] = hidden_b[:, part * half : (part + 1) * half]
            slope[to, :] = slope_b[:, part * half : (part + 1) * half]
            low = block * 16 + part * 8
            vs = [velocity[a, low : low + 8, :] for a in range(3)]
            vel[:, to] = jnp.concatenate(vs + [jnp.zeros_like(vs[0])], 0).astype(BF16)
            fs = [f[part * 8 : part * 8 + 8] for f in wide]
            prod[:, to] = jnp.concatenate([v * f for v in vs for f in fs], 0).astype(BF16)
    acc_o[...] += lax.dot_general(vel[...], hid[...], PLAIN, preferred_element_type=F32)
    acc_t[...] += lax.dot_general(prod[...], slope[...], PLAIN, preferred_element_type=F32)

    @pl.when(last)
    def _():
        def own(value):
            at_row = lax.broadcasted_iota(jnp.int32, value.shape, 0) % 8
            at_col = lax.broadcasted_iota(jnp.int32, value.shape, 1) % 8
            kept = jnp.where(at_row == at_col, value, 0.0)
            return jnp.sum(kept.reshape(-1, 8, value.shape[1]), 1)

        outer = own(acc_o[...])
        terms = own(acc_t[...])
        inner = sum(
            w_out[a : a + 1] * terms[a * count : (a + 1) * count] for a in range(3)
        )
        both = jnp.concatenate([inner, outer[:3], jnp.zeros((5, half), F32)], 0)
        hidden_at = lax.broadcasted_iota(jnp.int32, (half, 64), 0) // 8
        column = lax.broadcasted_iota(jnp.int32, (half, 64), 1)
        pick = (hidden_at == column).astype(F32)
        sums16 = jnp.dot(both, pick, precision=lax.Precision.HIGHEST, preferred_element_type=F32)
        value = jnp.concatenate([sums16[:8], sums16[8:]], 1)
        grads[...] = jnp.broadcast_to(value[None], grads.shape)


def whole(shape):
    return pl.BlockSpec(shape, lambda i: (0,) * len(shape))


def shape(*dims):
    return jax.ShapeDtypeStruct(dims, F32)


def params():
    return pltpu.CompilerParams(vmem_limit_bytes=VMEM)


def body(density, cotangent, features, w_inner, w_outer):
    nx, ny, nz = density.shape
    count, hidden = features.shape[0], w_inner.shape[0]
    devices = lax.axis_size("gx") * lax.axis_size("gy")
    cells = float(density.size * devices)
    planes = pl.BlockSpec((3, 1, ny, nz), lambda i: (0, i, 0, 0))
    sides = [(starts(LOWER_X)[1], ny, nz), (starts(UPPER_X)[1], ny, nz), (starts(LOWER_Y)[1] * nx, nz), (starts(UPPER_Y)[1] * nx, nz)]
    corner = (16, nz)
    lines, ends = ny // 8 - 1, nx // 2 - 1
    sent = pl.pallas_call(
        pack_kernel,
        grid=(1,),
        in_specs=[
            pl.BlockSpec((nx, 8, nz), lambda i: (0, 0, 0)),
            pl.BlockSpec((nx, 8, nz), lambda i: (0, lines, 0)),
            pl.BlockSpec((3, nx, 8, nz), lambda i: (0, 0, 0, 0)),
            pl.BlockSpec((3, nx, 8, nz), lambda i: (0, 0, lines, 0)),
            pl.BlockSpec((4, ny, nz), lambda i: (0, 0, 0)),
            pl.BlockSpec((2, ny, nz), lambda i: (ends, 0, 0)),
            pl.BlockSpec((3, 2, ny, nz), lambda i: (0, 0, 0, 0)),
            pl.BlockSpec((3, 2, ny, nz), lambda i: (0, ends, 0, 0)),
        ],
        out_specs=[whole(side) for side in sides] + [whole(corner)] * 4,
        out_shape=[shape(*side) for side in sides] + [shape(*corner)] * 4,
        compiler_params=params(),
    )(density, density, cotangent, cotangent, density, density, cotangent, cotangent)
    steps = ((1, 0), (-1, 0), (0, 1), (0, -1), (1, 1), (1, -1), (-1, 1), (-1, -1))
    halo = [neighbours(value, *step) for value, step in zip(sent, steps)]

    pick = jnp.arange(16)[:, None, None] == jnp.arange(16).reshape(1, 2, 8)
    w_in = w_inner.T[:, None, None, :, None] * pick[None, :, :, None, :].astype(BF16)
    w_in = w_in.reshape(count * 16, 2 * hidden * 8)
    w_out = jnp.repeat(w_outer.astype(F32), 8, axis=1)

    extended = (nx + 1, ny + 8, nz)
    around = (ny + 16, nz)
    s, q, sums = pl.pallas_call(
        moments_kernel,
        out_shape=[shape(*extended), shape(*extended), shape(devices, 128)],
        scratch_shapes=[pltpu.VMEM((nx + 5,) + around, F32)]
        + [pltpu.VMEM((nx + 4,) + around, F32)] * 4
        + [pltpu.VMEM(around, F32), pltpu.VMEM((4, 8, nz), F32)],
        compiler_params=params(),
    )(density, cotangent, *halo)
    sums = collect(sums)

    half = hidden * 8
    long = ny // 8 * nz
    grad, grads = pl.pallas_call(
        closure_kernel,
        grid=(nx,),
        in_specs=[
            whole((devices, 128)), planes, whole(extended), whole(extended),
            pl.BlockSpec((count, 1, ny, nz), lambda i: (0, i, 0, 0)), whole(w_in.shape), whole(w_out.shape),
        ],
        out_specs=[planes, whole((devices, 8, 128))],
        out_shape=[shape(3, nx, ny, nz), shape(devices, 8, 128)],
        scratch_shapes=[
            pltpu.VMEM((2, 8, nz), F32),
            pltpu.VMEM((3, ny, nz), F32),
            pltpu.VMEM((long, half), BF16),
            pltpu.VMEM((long, half), BF16),
            pltpu.VMEM((32, long), BF16),
            pltpu.VMEM((24 * count, long), BF16),
            pltpu.VMEM((32, half), F32),
            pltpu.VMEM((24 * count, half), F32),
        ],
        compiler_params=params(),
    )(sums, cotangent, s, q, features, w_in, w_out)
    grads = jnp.sum(collect(grads), 0) / cells
    return grad, grads[:, :hidden].T, grads[:3, hidden:]


def solution(mesh):
    in_specs = (P("gx", "gy", None), P(None, "gx", "gy", None), P(None, "gx", "gy", None), P(), P())
    out_specs = (P(None, "gx", "gy", None), P(), P())
    return jax.shard_map(body, mesh=mesh, in_specs=in_specs, out_specs=out_specs, check_vma=False)
```

time: 179 us -> 153 us (0.85)
  starting transfers between devices: 51 us -> 39.5 us
  Pallas kernels: 79.6 us -> 73.3 us
  local copies, waits for them, and re-layouts: 13.2 us -> 6.92 us
    ppermute x10 -> x8, starting transfers between devices: 28.4 us -> 21.9 us  [neighbours(): return lax.ppermute(value, ('gx', 'gy'), pairs)]
    pallas_call x3 -> x2, Pallas kernels: 26 us -> 19.4 us  [the longest x1 15.9 us: body(): pl.pallas_call(moments_kernel, out_shape=[shape(*extended), shape(*extend...]
    all_to_all x1, starting transfers between devices: 22.6 us -> 17.6 us  [collect(): return lax.all_to_all(copies, ('gx', 'gy'), 0, 0)]
    squeeze x3 -> x0, local copies, waits for them, and re-layouts: 3.15 us -> none  [the longest x1 1.56 us: body(): below_x[0]]
    slice x2 -> x0, local copies, waits for them, and re-layouts: 1.92 us -> none  [the longest x1 1 us: body(): dens_ay = shifted(density[:, 0], 'gy', -1)]
    ppermute x10 -> x8, waiting for transfers between devices: 8.5 us -> 7.56 us  [neighbours(): return lax.ppermute(value, ('gx', 'gy'), pairs)]
  transfers between devices with their start and end apart: 11 -> 9, of which waited for: 4 -> 4; matrix products, arithmetic and copies ran while one was open for 5% -> 2% of each run, Pallas kernels for 0% -> 0%
where the time goes in v3:
time: 153 us
  Pallas kernels  73.3 us (48%)
  starting transfers between devices  39.5 us (26%)
  blocking collectives  18.2 us (12%)
  waiting for transfers between devices  13.7 us (9%)
  local copies, waits for them, and re-layouts  6.92 us (5%)
    pallas_call x1, Pallas kernels, body(): pl.pallas_call(closure_kernel, grid=(nx,), in_specs=[whole((devices, 128)...  53.8 us
    ppermute x8, starting transfers between devices, neighbours(): return lax.ppermute(value, ('gx', 'gy'), pairs)  21.9 us
    all_to_all x1, blocking collectives, collect(): return lax.all_to_all(copies, ('gx', 'gy'), 0, 0)  18.2 us
    all_to_all x1, starting transfers between devices, collect(): return lax.all_to_all(copies, ('gx', 'gy'), 0, 0)  17.6 us
    pallas_call x1, Pallas kernels, body(): pl.pallas_call(moments_kernel, out_shape=[shape(*extended), shape(*extend...  15.9 us
    ppermute x8, waiting for transfers between devices, neighbours(): return lax.ppermute(value, ('gx', 'gy'), pairs)  7.56 us
    all_to_all x1, waiting for transfers between devices, collect(): return lax.all_to_all(copies, ('gx', 'gy'), 0, 0)  6.13 us
    pallas_call x1, Pallas kernels, body(): pl.pallas_call(pack_kernel, grid=(1,), in_specs=[pl.BlockSpec((nx, 8, nz)...  3.48 us
  transfers between devices with their start and end apart: 9, of which 4 were waited for; matrix products, arithmetic and copies ran while one was open for 2% of the time, Pallas kernels for 0%

profile of v3, /device:TPU:0, one launch (start us, length us, event | category | flops | bytes accessed | tf_op | source)
XLA Modules:
  0.0 152.9 jit_solution(13401310962971674346)
XLA Ops:
  0.6 3.5 %shard_map.76 = (f32[6,128,256]{2,1,0:T(8,128)}, f32[9,128,256]{2,1,0:T(8,128)}, f32[96,256]{1,0:T(8,128)}, f32[144,256]{1,0:T(8,128)}, f32[16,256]{1,0:T(8,128)...) custom-call(f32[16,128,256]{2,1,0:T(8,128)} %dens.1, f32[16,128,256]{2,1,0:T(8,128)} %dens.1, ...), custom_call_target="tpu_custom_call" | custom-call | tf_op jit(solution)/shard_map/pallas_call | solution.py:353
  4.1 1.3 collective-permute-start.1
  5.4 3.1 %collective-permute-start = (f32[6,128,256]{2,1,0:T(8,128)}, f32[6,128,256]{2,1,0:T(8,128)S(1)}, u32[]{:S(2)}, u32[]{:S(2)}) collective-permute-start(f32[6,128,256]{2,1,0:T(8,128)} %get-tuple-element.16), channel_id=1, source_target_pairs={{0,8},{1,9},{2,10},{3,11},{4,12},{5,13},{6,14},{7,15},{8,16},{9,17... | collective-permute-start | bytes 2359304 | tf_op jit(solution)/shard_map/ppermute | solution.py:27
  8.5 6.6 %collective-permute-start.4 = (f32[16,256]{1,0:T(8,128)}, f32[16,256]{1,0:T(8,128)S(1)}, u32[]{:S(2)}, u32[]{:S(2)}) collective-permute-start(f32[16,256]{1,0:T(8,128)} %get-tuple-element.20), channel_id=1, source_target_pairs={{0,9},{1,10},{2,11},{3,12},{4,13},{5,14},{6,15},{8,17},{9,18},{10,... | collective-permute-start | bytes 49160 | tf_op jit(solution)/shard_map/ppermute | solution.py:27
  15.1 0.7 collective-permute-start.5
  15.8 0.7 collective-permute-start.6
  16.8 1.3 collective-permute-start.7
  18.1 7.0 %collective-permute-start.2 = (f32[96,256]{1,0:T(8,128)}, f32[96,256]{1,0:T(8,128)S(1)}, u32[]{:S(2)}, u32[]{:S(2)}) collective-permute-start(f32[96,256]{1,0:T(8,128)} %get-tuple-element.18), channel_id=1, source_target_pairs={{0,1},{1,2},{2,3},{3,4},{4,5},{5,6},{6,7},{8,9},{9,10},{10,11},{11... | collective-permute-start | bytes 294920 | tf_op jit(solution)/shard_map/ppermute | solution.py:27
  25.1 1.3 collective-permute-start.3
  26.6 3.0 %collective-permute-done.7.high_high = f32[16,256]{1,0:T(8,128)S(1)} collective-permute-done((f32[16,256]{1,0:T(8,128)}, f32[16,256]{1,0:T(8,128)S(1)}, u32[]{:S(2)}, u32[]{:S(2)}) %collective-permute-start.7) | collective-permute-done | bytes 16416 | tf_op jit(solution)/shard_map/ppermute | solution.py:27
  29.6 4.3 %collective-permute-done.3.above_y = f32[144,256]{1,0:T(8,128)S(1)} collective-permute-done((f32[144,256]{1,0:T(8,128)}, f32[144,256]{1,0:T(8,128)S(1)}, u32[]{:S(2)}, u32[]{:S(2)}) %collective-permute-start.3) | collective-permute-done | bytes 147488 | tf_op jit(solution)/shard_map/ppermute | solution.py:27
  33.9 0.6 copy-done.3
  34.8 1.0 copy-done
  35.8 15.9 %shard_map.77 = (f32[17,136,256]{2,1,0:T(8,128)}, f32[17,136,256]{2,1,0:T(8,128)}, f32[128,128]{1,0:T(8,128)}) custom-call(f32[16,128,256]{2,1,0:T(8,128)} %dens.1, f32[3,16,128,256]{3,2,1,0:T(8,128)} %cot.3, f32[6,128,256]{2,1,0:T(8,128)} %copy-done.1, f32[9,128,256]{2,1,0:T(8,128)} %copy-done, f32[96,256]{1,0:T(8,128)} %copy-done.4, f32[144,256]{1,0:T(8,128)} %copy-done.3, ...), custom_call_target="tpu_custom_call" | custom-call | tf_op jit(solution)/shard_map/pallas_call | solution.py:380
  51.8 17.6 %all-to-all-start = ((f32[128,1,128]{2,1,0:T(1,128)}), f32[128,1,128]{2,1,0:T(1,128)S(1)}, u32[]{:S(2)}, u32[]{:S(2)}) async-start(f32[128,1,128]{2,1,0:T(1,128)} %bitcast.12), calls=%async_computation | async-start | bytes 131072 | tf_op jit(solution)/shard_map/all_to_all | solution.py:16
  69.7 0.7 reshape.41.w_out
  70.4 1.4 mul.20
  71.8 0.8 copy.12.w_in
  72.7 6.1 %all-to-all-done = f32[128,1,128]{2,1,0:T(1,128)S(1)} async-done(((f32[128,1,128]{2,1,0:T(1,128)}), f32[128,1,128]{2,1,0:T(1,128)S(1)}, u32[]{:S(2)}, u32[]{:S(2)}) %all-to-all-start) | async-done | bytes 65568 | tf_op jit(solution)/shard_map/all_to_all | solution.py:16
  78.8 0.6 copy-done.2
  79.4 53.8 %shard_map.78 = (f32[3,16,128,256]{3,2,1,0:T(8,128)}, f32[128,8,128]{2,1,0:T(8,128)}) custom-call(f32[128,128]{1,0:T(8,128)} %bitcast.11, f32[3,16,128,256]{3,2,1,0:T(8,128)} %cot.3, f32[17,136,256]{2,1,0:T(8,128)} %get-tuple-element.25.s, f32[17,136,256]{2,1,0:T(8,128)} %get-tuple-element.26.q, bf16[8,16,128,256]{3,2,1,0:T(8,128)(2,1)} %feats.1, ...), custom_call_target="tpu_custom_call" | custom-call | tf_op jit(solution)/shard_map/pallas_call | solution.py:392
  133.2 18.2 %all_to_all.16 = f32[128,8,128]{2,1,0:T(8,128)S(1)} all-to-all(f32[128,8,128]{2,1,0:T(8,128)} %get-tuple-element.28), channel_id=1, replica_groups=mesh['gx'=16,'gy'=8] {'gx','gy'}, dimensions={0} | all-to-all | bytes 1048576 | tf_op jit(solution)/shard_map/all_to_all | solution.py:16
  151.6 0.7 slice.7
  152.3 0.6 slice_bitcast_fusion
  (32 shorter events, 1.2 us)
Async XLA Ops:
  0.6 25.8 %copy-start.9 = (bf16[64,8]{0,1:T(8,128)(2,1)S(1)}, bf16[64,8]{0,1:T(8,128)(2,1)}, u32[]{:S(2)}) copy-start(bf16[64,8]{0,1:T(8,128)(2,1)} %param.8) | copy-start | bytes 3076
  4.1 29.7 %collective-permute-start.1 = (f32[9,128,256]{2,1,0:T(8,128)}, f32[9,128,256]{2,1,0:T(8,128)S(1)}, u32[]{:S(2)}, u32[]{:S(2)}) collective-permute-start(f32[9,128,256]{2,1,0:T(8,128)} %get-tuple-element.17), channel_id=1, source_target_pairs={{8,0},{9,1},{10,2},{11,3},{12,4},{13,5},{14,6},{15,7},{16,8},{17,9... | collective-permute-start | bytes 3538952 | tf_op jit(solution)/shard_map/ppermute | solution.py:27
  5.4 28.4 %collective-permute-start = (f32[6,128,256]{2,1,0:T(8,128)}, f32[6,128,256]{2,1,0:T(8,128)S(1)}, u32[]{:S(2)}, u32[]{:S(2)}) collective-permute-start(f32[6,128,256]{2,1,0:T(8,128)} %get-tuple-element.16), channel_id=1, source_target_pairs={{0,8},{1,9},{2,10},{3,11},{4,12},{5,13},{6,14},{7,15},{8,16},{9,17... | collective-permute-start | bytes 2359304 | tf_op jit(solution)/shard_map/ppermute | solution.py:27
  8.5 8.3 %collective-permute-start.4 = (f32[16,256]{1,0:T(8,128)}, f32[16,256]{1,0:T(8,128)S(1)}, u32[]{:S(2)}, u32[]{:S(2)}) collective-permute-start(f32[16,256]{1,0:T(8,128)} %get-tuple-element.20), channel_id=1, source_target_pairs={{0,9},{1,10},{2,11},{3,12},{4,13},{5,14},{6,15},{8,17},{9,18},{10,... | collective-permute-start | bytes 49160 | tf_op jit(solution)/shard_map/ppermute | solution.py:27
  15.1 2.9 %collective-permute-start.5 = (f32[16,256]{1,0:T(8,128)}, f32[16,256]{1,0:T(8,128)S(1)}, u32[]{:S(2)}, u32[]{:S(2)}) collective-permute-start(f32[16,256]{1,0:T(8,128)} %get-tuple-element.21), channel_id=1, source_target_pairs={{1,8},{2,9},{3,10},{4,11},{5,12},{6,13},{7,14},{9,16},{10,17},{11,... | collective-permute-start | bytes 49160 | tf_op jit(solution)/shard_map/ppermute | solution.py:27
  15.8 9.3 %collective-permute-start.6 = (f32[16,256]{1,0:T(8,128)}, f32[16,256]{1,0:T(8,128)S(1)}, u32[]{:S(2)}, u32[]{:S(2)}) collective-permute-start(f32[16,256]{1,0:T(8,128)} %get-tuple-element.22), channel_id=1, source_target_pairs={{8,1},{9,2},{10,3},{11,4},{12,5},{13,6},{14,7},{16,9},{17,10},{18,... | collective-permute-start | bytes 49160 | tf_op jit(solution)/shard_map/ppermute | solution.py:27
  16.8 17.1 %copy-start.5 = (f32[16,256]{1,0:T(8,128)}, f32[16,256]{1,0:T(8,128)S(1)}, u32[]{:S(2)}) copy-start(f32[16,256]{1,0:T(8,128)S(1)} %collective-permute-done.4.low_low) | copy-start | bytes 49156
  16.8 12.8 %collective-permute-start.7 = (f32[16,256]{1,0:T(8,128)}, f32[16,256]{1,0:T(8,128)S(1)}, u32[]{:S(2)}, u32[]{:S(2)}) collective-permute-start(f32[16,256]{1,0:T(8,128)} %get-tuple-element.23), channel_id=1, source_target_pairs={{9,0},{10,1},{11,2},{12,3},{13,4},{14,5},{15,6},{17,8},{18,9},{19,... | collective-permute-start | bytes 49160 | tf_op jit(solution)/shard_map/ppermute | solution.py:27
  18.1 15.8 %copy-start.6 = (f32[16,256]{1,0:T(8,128)}, f32[16,256]{1,0:T(8,128)S(1)}, u32[]{:S(2)}) copy-start(f32[16,256]{1,0:T(8,128)S(1)} %collective-permute-done.5.low_high) | copy-start | bytes 49156
  18.1 11.5 %collective-permute-start.2 = (f32[96,256]{1,0:T(8,128)}, f32[96,256]{1,0:T(8,128)S(1)}, u32[]{:S(2)}, u32[]{:S(2)}) collective-permute-start(f32[96,256]{1,0:T(8,128)} %get-tuple-element.18), channel_id=1, source_target_pairs={{0,1},{1,2},{2,3},{3,4},{4,5},{5,6},{6,7},{8,9},{9,10},{10,11},{11... | collective-permute-start | bytes 294920 | tf_op jit(solution)/shard_map/ppermute | solution.py:27
  25.1 8.8 %copy-start.7 = (f32[16,256]{1,0:T(8,128)}, f32[16,256]{1,0:T(8,128)S(1)}, u32[]{:S(2)}) copy-start(f32[16,256]{1,0:T(8,128)S(1)} %collective-permute-done.6.high_low) | copy-start | bytes 49156
  25.1 8.8 %collective-permute-start.3 = (f32[144,256]{1,0:T(8,128)}, f32[144,256]{1,0:T(8,128)S(1)}, u32[]{:S(2)}, u32[]{:S(2)}) collective-permute-start(f32[144,256]{1,0:T(8,128)} %get-tuple-element.19), channel_id=1, source_target_pairs={{1,0},{2,1},{3,2},{4,3},{5,4},{6,5},{7,6},{9,8},{10,9},{11,10},{12... | collective-permute-start | bytes 442376 | tf_op jit(solution)/shard_map/ppermute | solution.py:27
  29.6 4.3 %copy-start.8 = (f32[16,256]{1,0:T(8,128)}, f32[16,256]{1,0:T(8,128)S(1)}, u32[]{:S(2)}) copy-start(f32[16,256]{1,0:T(8,128)S(1)} %collective-permute-done.7.high_high) | copy-start | bytes 49156
  29.6 4.3 %copy-start.4 = (f32[96,256]{1,0:T(8,128)}, f32[96,256]{1,0:T(8,128)S(1)}, u32[]{:S(2)}) copy-start(f32[96,256]{1,0:T(8,128)S(1)} %collective-permute-done.2.below_y) | copy-start | bytes 294916
  33.8 0.7 copy-start.3
  33.8 0.9 copy-start.1
  34.8 1.0 copy-start
  51.8 17.9 %copy-start.10 = (bf16[3,64]{1,0:T(4,128)(2,1)S(1)}, bf16[3,64]{1,0:T(4,128)(2,1)}, u32[]{:S(2)}) copy-start(bf16[3,64]{1,0:T(4,128)(2,1)} %param.9) | copy-start | bytes 1156
  51.8 27.0 %all-to-all-start = ((f32[128,1,128]{2,1,0:T(1,128)}), f32[128,1,128]{2,1,0:T(1,128)S(1)}, u32[]{:S(2)}, u32[]{:S(2)}) async-start(f32[128,1,128]{2,1,0:T(1,128)} %bitcast.12), calls=%async_computation | async-start | bytes 131072 | tf_op jit(solution)/shard_map/all_to_all | solution.py:16
  78.8 0.6 copy-start.2

commit v4 on v3

v4 whole, which is shorter than its diff:
```python
import jax
import jax.numpy as jnp
from jax import lax
from jax.experimental import pallas as pl
from jax.experimental.pallas import tpu as pltpu
from jax.sharding import PartitionSpec as P

F32 = jnp.float32
BF16 = jnp.bfloat16
FIRST = (((0,), (0,)), ((), ()))
VMEM = 56 * 2**20


def collect(copies):
    return lax.all_to_all(copies, ("gx", "gy"), 0, 0)


def neighbours(value, by_x, by_y):
    nx, ny = lax.axis_size("gx"), lax.axis_size("gy")
    pairs = [
        (i * ny + j, (i + by_x) * ny + j + by_y)
        for i in range(nx)
        for j in range(ny)
        if 0 <= i + by_x < nx and 0 <= j + by_y < ny
    ]
    return lax.ppermute(value, ("gx", "gy"), pairs)


def next_lane(plane):
    size = plane.shape[1]
    at = lax.broadcasted_iota(jnp.int32, plane.shape, 1)
    return jnp.where(at == size - 1, 0.0, pltpu.roll(plane, size - 1, 1))


def prior_lane(plane):
    at = lax.broadcasted_iota(jnp.int32, plane.shape, 1)
    return jnp.where(at == 0, 0.0, pltpu.roll(plane, 1, 1))


def next_row(plane):
    return pltpu.roll(plane, plane.shape[0] - 1, 0)


def prior_row(plane):
    return pltpu.roll(plane, 1, 0)


def fold(plane):
    return jnp.sum(plane.reshape(-1, 8, plane.shape[1]), 0)


LOWER_Y = ((0, 2), (1, 1), (2, 2), (3, 1))
UPPER_Y = ((0, 3), (1, 2), (2, 2), (3, 2))


def starts(plan):
    places, at = [], 0
    for _, width in plan:
        places.append(at)
        at += width
    return places, at


def pack_kernel(d_first, d_last, c_first, c_last, up, down):
    planes = d_first.shape[0]

    def line(field, x, y):
        if field == 0:
            block = d_first if y >= 0 else d_last
            return block[x, y % 8 : y % 8 + 1, :]
        block = c_first if y >= 0 else c_last
        return block[field - 1, x, y % 8 : y % 8 + 1, :]

    for plan, to, low in ((LOWER_Y, up, False), (UPPER_Y, down, True)):
        at = 0
        for field, width in plan:
            for y in range(width):
                for x in range(planes):
                    to[at : at + 1, :] = line(field, x, y if low else y - width)
                    at += 1


def sides(below_y, above_y, planes, field, x):
    low, high, width = LOWER_Y[field][1], UPPER_Y[field][1], below_y.shape[1]
    low_at, high_at = starts(LOWER_Y)[0][field], starts(UPPER_Y)[0][field]
    below = [below_y[pl.ds((low_at + k) * planes + x, 1), :] for k in range(low)]
    above = [above_y[pl.ds((high_at + k) * planes + x, 1), :] for k in range(high)]
    below = jnp.concatenate([jnp.zeros((8 - low, width), F32)] + below, 0)
    return below, jnp.concatenate(above + [jnp.zeros((8 - high, width), F32)], 0)


def weight(value, after):
    return jnp.where(value > 0, 2.0 / (value + after), 0.0)


def across(here, beta_y, beta_z, cot_y, cot_z):
    flux_y, flux_z = beta_y * cot_y, beta_z * cot_z
    return prior_row(flux_y) - flux_y + (prior_lane(flux_z) - flux_z)


def edge_kernel(d_low, d_high, c_low, c_high, below_y, above_y, up, down):
    planes = below_y.shape[0] // starts(LOWER_Y)[1]

    def plane(field, x):
        low, high = sides(below_y, above_y, planes, field, x)
        d, c, at = (d_low, c_low, x) if x < 4 else (d_high, c_high, x - planes + 2)
        return jnp.concatenate([low, d[at] if field == 0 else c[field - 1, at], high], 0)

    def part(x):
        here = plane(0, x)
        return across(here, weight(here, next_row(here)), weight(here, next_lane(here)), plane(2, x), plane(3, x))

    last = planes - 1
    here, before = plane(0, last), plane(0, last - 1)
    up[0] = here
    up[1] = plane(1, last)
    up[2] = jnp.where(here > 0, weight(before, here) * plane(1, last - 1) + part(last), 0.0)
    here, after = plane(0, 0), plane(0, 1)
    down[0] = here
    down[1] = after
    flux = weight(here, after) * plane(1, 0)
    down[2] = jnp.where(here > 0, part(0) - flux, 0.0)
    down[3] = jnp.where(after > 0, flux - weight(after, plane(0, 2)) * plane(1, 1) + part(1), 0.0)


def moments_kernel(
    dens_far, cot_far, below_x, above_x, below_y, above_y,
    s_out, q_out, sums, dens, cot, d_all, b_x, b_y, b_z, s_all, before, acc, sems,
):
    planes, rows, width = dens.shape
    own = slice(8, rows + 8)
    part = planes // 4
    copies = [pltpu.make_async_copy(dens_far, dens, sems.at[4])]
    for k in range(4):
        span = pl.ds(k * part, part)
        copies.append(pltpu.make_async_copy(cot_far.at[:, span], cot.at[:, span], sems.at[k]))
    for copy in copies:
        copy.start()

    def fill(x, carry):
        low, high = sides(below_y, above_y, planes, 0, x)
        d_all[x + 1, 0:8, :] = low
        d_all[x + 1, own, :] = dens[x]
        d_all[x + 1, rows + 8 : rows + 16, :] = high
        return carry

    d_all[0] = below_x[0]
    d_all[planes + 1] = above_x[0]
    d_all[planes + 2] = above_x[1]
    copies[0].wait()
    lax.fori_loop(0, planes, fill, 0)

    def weights(x):
        at = x + 1
        here = d_all[at]
        b_x[at] = weight(here, d_all[at + 1])
        b_y[at] = weight(here, next_row(here))
        b_z[at] = weight(here, next_lane(here))

    def field(index, x):
        low, high = sides(below_y, above_y, planes, index, x)
        return jnp.concatenate([low, cot[index - 1, x], high], 0)

    def source(x, carry):
        at = x + 1
        here = d_all[at]
        weights(x)
        flux = b_x[at] * field(1, x)
        out = before[...] - flux + across(here, b_y[at], b_z[at], field(2, x), field(3, x))
        before[...] = flux
        s_all[at] = jnp.where(here > 0, out, 0.0)
        return carry

    b_x[0] = weight(d_all[0], d_all[1])
    flux = b_x[0] * below_x[1]
    before[...] = flux
    s_all[0] = below_x[2] - flux
    for k in range(4):
        copies[1 + k].wait()
        lax.fori_loop(k * part, (k + 1) * part, source, 0)
    s_all[planes + 1] = jnp.where(d_all[planes + 1] > 0, above_x[2] + before[...], 0.0)
    s_all[planes + 2] = above_x[3]
    weights(planes)

    def image(x):
        at = x + 1
        here = s_all[at]
        flux = b_x[at] * (s_all[at + 1] - here)
        out = before[...] - flux
        before[...] = flux
        flux = b_y[at] * (next_row(here) - here)
        out = out + (prior_row(flux) - flux)
        flux = b_z[at] * (next_lane(here) - here)
        out = out + (prior_lane(flux) - flux)
        out = jnp.where(d_all[at] > 0, out, 0.0)
        s_out[x] = here[8:]
        q_out[x] = out[8:]
        return here, out

    def squares(x, out):
        at = x + 1
        jump = (next_row(out) - out)[own]
        jump_z = next_lane(out[own]) - out[own]
        acc[3] += fold(b_y[at, own, :] * jump * jump + b_z[at, own, :] * jump_z * jump_z)

    def jumps(x, out):
        jump = out[own] - q_out[x - 1, 0:rows, :]
        acc[3] += fold(b_x[x, own, :] * jump * jump)

    def products(here, out):
        here, out = here[own], out[own]
        acc[0] += fold(here * here)
        acc[1] += fold(here * out)
        acc[2] += fold(out * out)

    before[...] = b_x[0] * (s_all[1] - s_all[0])
    acc[...] = jnp.zeros_like(acc)
    here, out = image(0)
    products(here, out)
    squares(0, out)

    def own_image(x, carry):
        here, out = image(x)
        products(here, out)
        squares(x, out)
        jumps(x, out)
        return carry

    lax.fori_loop(1, planes, own_image, 0)
    here, out = image(planes)
    jumps(planes, out)
    at = lax.broadcasted_iota(jnp.int32, (1, 128), 1)
    row = jnp.zeros((1, 128), F32)
    for k in range(4):
        value = jnp.sum(jnp.sum(acc[k], 0, keepdims=True), 1, keepdims=True)
        row = row + jnp.where(at == k, value, 0.0)
    sums[...] = jnp.broadcast_to(row, sums.shape)


def closure_kernel(
    sums, cot, s, q, feats, w_in, w_out,
    grad, grads, scale, velocity, hid, slope, vel, prod, acc_o, acc_t,
):
    step, planes = pl.program_id(0), s.shape[0] - 1
    rows, width = cot.shape[2], s.shape[2]
    count = feats.shape[0]

    @pl.when(step == 0)
    def _():
        all_sums = jnp.sum(sums[...], 0, keepdims=True)
        at_lane = lax.broadcasted_iota(jnp.int32, (1, 128), 1)
        m0, m1, m2, m3 = (
            jnp.sum(jnp.where(at_lane == k, all_sums, 0.0), 1, keepdims=True) for k in range(4)
        )
        alpha0 = m0 / m1
        rr1 = alpha0 * alpha0 * m2 - m0
        beta = rr1 / m0
        more = 1.0 + beta
        alpha1 = rr1 / (more * more * m1 - 2.0 * more * alpha0 * m2 + alpha0 * alpha0 * m3)
        scale[0] = jnp.broadcast_to(alpha0 + alpha1 * more, scale.shape[1:])
        scale[1] = jnp.broadcast_to(-alpha1 * alpha0, scale.shape[1:])
        acc_o[...] = jnp.zeros_like(acc_o)
        acc_t[...] = jnp.zeros_like(acc_t)

    on_s, on_q = scale[0][:1], scale[1][:1]
    last = step == planes - 1
    wide = on_s * s[step] + on_q * q[step]
    here = wide[:rows]
    beyond = on_s * s[step + 1, :rows, :] + on_q * q[step + 1, :rows, :]
    for a, after in enumerate((beyond, next_row(wide)[:rows], next_lane(here))):
        value = cot[a, 0] - (after - here)
        grad[a, 0] = value
        velocity[a] = value.astype(BF16).astype(F32)

    half = w_in.shape[1] // 2
    blocks, wide_tile = rows // 16, 256

    def place(block, tile):
        part, column = divmod(tile * wide_tile, half)
        cells = (block * 2 + part) * width
        return slice(cells, cells + width), slice(column, column + wide_tile)

    def first_layer(block, tile):
        inner = feats[:, 0, block * 16 : block * 16 + 16, :].reshape(count * 16, width)
        weights = w_in[:, tile * wide_tile : (tile + 1) * wide_tile]
        pre = lax.dot_general(inner, weights, FIRST, preferred_element_type=F32)
        hidden = jnp.tanh(pre)
        to = place(block, tile)
        hid[to] = hidden.astype(BF16)
        slope[to] = (1.0 - hidden * hidden).astype(BF16)

    def outer(block, tile):
        cells, columns = place(block, tile)
        acc_o[:, columns] += jnp.dot(vel[:, cells], hid[cells, columns], preferred_element_type=F32)

    for block in range(blocks):
        at = slice(block * 16, block * 16 + 16)
        broad = [feats[c, 0, at, :].astype(F32) for c in range(count)]
        for part in range(2):
            to = slice((block * 2 + part) * width, (block * 2 + part + 1) * width)
            low = block * 16 + part * 8
            vs = [velocity[a, low : low + 8, :] for a in range(3)]
            vel[:, to] = jnp.concatenate(vs + [jnp.zeros_like(vs[0])], 0).astype(BF16)
            fs = [f[part * 8 : part * 8 + 8] for f in broad]
            prod[:, to] = jnp.concatenate([v * f for v in vs for f in fs], 0).astype(BF16)
    tiles = w_in.shape[1] // wide_tile
    late = 2
    for block in range(blocks + late):
        for tile in range(tiles):
            if block < blocks:
                first_layer(block, tile)
            if block >= late:
                outer(block - late, tile)
    acc_t[...] += jnp.dot(prod[...], slope[...], preferred_element_type=F32)

    @pl.when(last)
    def _():
        def own(value):
            at_row = lax.broadcasted_iota(jnp.int32, value.shape, 0) % 8
            at_col = lax.broadcasted_iota(jnp.int32, value.shape, 1) % 8
            kept = jnp.where(at_row == at_col, value, 0.0)
            return jnp.sum(kept.reshape(-1, 8, value.shape[1]), 1)

        outermost = own(acc_o[...])
        terms = own(acc_t[...])
        inner = sum(
            w_out[a : a + 1] * terms[a * count : (a + 1) * count] for a in range(3)
        )
        both = jnp.concatenate([inner, outermost[:3], jnp.zeros((5, half), F32)], 0)
        hidden_at = lax.broadcasted_iota(jnp.int32, (half, 64), 0) // 8
        column = lax.broadcasted_iota(jnp.int32, (half, 64), 1)
        pick = (hidden_at == column).astype(F32)
        sums16 = jnp.dot(both, pick, precision=lax.Precision.HIGHEST, preferred_element_type=F32)
        value = jnp.concatenate([sums16[:8], sums16[8:]], 1)
        grads[...] = jnp.broadcast_to(value[None], grads.shape)


def whole(shape):
    return pl.BlockSpec(shape, lambda i: (0,) * len(shape))


def shape(*dims):
    return jax.ShapeDtypeStruct(dims, F32)


def params():
    return pltpu.CompilerParams(vmem_limit_bytes=VMEM)


def body(density, cotangent, features, w_inner, w_outer):
    nx, ny, nz = density.shape
    count, hidden = features.shape[0], w_inner.shape[0]
    devices = lax.axis_size("gx") * lax.axis_size("gy")
    cells = float(density.size * devices)
    planes = pl.BlockSpec((3, 1, ny, nz), lambda i: (0, i, 0, 0))
    lines, ends = ny // 8 - 1, nx // 2 - 1
    around = (ny + 16, nz)
    to_up, to_down = pl.pallas_call(
        pack_kernel,
        grid=(1,),
        in_specs=[
            pl.BlockSpec((nx, 8, nz), lambda i: (0, 0, 0)),
            pl.BlockSpec((nx, 8, nz), lambda i: (0, lines, 0)),
            pl.BlockSpec((3, nx, 8, nz), lambda i: (0, 0, 0, 0)),
            pl.BlockSpec((3, nx, 8, nz), lambda i: (0, 0, lines, 0)),
        ],
        out_specs=[whole((starts(plan)[1] * nx, nz)) for plan in (LOWER_Y, UPPER_Y)],
        out_shape=[shape(starts(plan)[1] * nx, nz) for plan in (LOWER_Y, UPPER_Y)],
        compiler_params=params(),
    )(density, density, cotangent, cotangent)
    below_y, above_y = neighbours(to_up, 0, 1), neighbours(to_down, 0, -1)
    to_up, to_down = pl.pallas_call(
        edge_kernel,
        grid=(1,),
        in_specs=[
            pl.BlockSpec((4, ny, nz), lambda i: (0, 0, 0)),
            pl.BlockSpec((2, ny, nz), lambda i: (ends, 0, 0)),
            pl.BlockSpec((3, 2, ny, nz), lambda i: (0, 0, 0, 0)),
            pl.BlockSpec((3, 2, ny, nz), lambda i: (0, ends, 0, 0)),
            whole(below_y.shape),
            whole(above_y.shape),
        ],
        out_specs=[whole((3,) + around), whole((4,) + around)],
        out_shape=[shape(3, *around), shape(4, *around)],
        compiler_params=params(),
    )(density, density, cotangent, cotangent, below_y, above_y)
    halo = [neighbours(to_up, 1, 0), neighbours(to_down, -1, 0), below_y, above_y]

    pick = jnp.arange(16)[:, None, None] == jnp.arange(16).reshape(1, 2, 8)
    w_in = w_inner.T[:, None, None, :, None] * pick[None, :, :, None, :].astype(BF16)
    w_in = w_in.reshape(count * 16, 2 * hidden * 8)
    w_out = jnp.repeat(w_outer.astype(F32), 8, axis=1)

    extended = (nx + 1, ny + 8, nz)
    anywhere = pl.BlockSpec(memory_space=pl.ANY)
    near = pl.BlockSpec(memory_space=pltpu.VMEM)
    s, q, sums = pl.pallas_call(
        moments_kernel,
        in_specs=[anywhere] * 2 + [near] * 4,
        out_shape=[shape(*extended), shape(*extended), shape(devices, 128)],
        scratch_shapes=[pltpu.VMEM((nx, ny, nz), F32), pltpu.VMEM((3, nx, ny, nz), F32)]
        + [pltpu.VMEM((nx + 3,) + around, F32)]
        + [pltpu.VMEM((nx + 2,) + around, F32)] * 3
        + [pltpu.VMEM((nx + 3,) + around, F32)]
        + [pltpu.VMEM(around, F32), pltpu.VMEM((4, 8, nz), F32), pltpu.SemaphoreType.DMA((5,))],
        compiler_params=params(),
    )(density, cotangent, *halo)
    sums = collect(sums)

    half = hidden * 8
    long = ny // 8 * nz
    grad, grads = pl.pallas_call(
        closure_kernel,
        grid=(nx,),
        in_specs=[
            whole((devices, 128)), planes, whole(extended), whole(extended),
            pl.BlockSpec((count, 1, ny, nz), lambda i: (0, i, 0, 0)), whole(w_in.shape), whole(w_out.shape),
        ],
        out_specs=[planes, whole((devices, 8, 128))],
        out_shape=[shape(3, nx, ny, nz), shape(devices, 8, 128)],
        scratch_shapes=[
            pltpu.VMEM((2, 8, nz), F32),
            pltpu.VMEM((3, ny, nz), F32),
            pltpu.VMEM((long, half), BF16),
            pltpu.VMEM((long, half), BF16),
            pltpu.VMEM((32, long), BF16),
            pltpu.VMEM((24 * count, long), BF16),
            pltpu.VMEM((32, half), F32),
            pltpu.VMEM((24 * count, half), F32),
        ],
        compiler_params=params(),
    )(sums, cotangent, s, q, features, w_in, w_out)
    grads = jnp.sum(collect(grads), 0) / cells
    return grad, grads[:, :hidden].T, grads[:3, hidden:]


def solution(mesh):
    in_specs = (P("gx", "gy", None), P(None, "gx", "gy", None), P(None, "gx", "gy", None), P(), P())
    out_specs = (P(None, "gx", "gy", None), P(), P())
    return jax.shard_map(body, mesh=mesh, in_specs=in_specs, out_specs=out_specs, check_vma=False)
```

time: 153 us -> 137 us (0.90)
  starting transfers between devices: 39.5 us -> 30.9 us
  Pallas kernels: 73.3 us -> 66 us
  waiting for transfers between devices: 13.7 us -> 12 us
    ppermute x8 -> x4, starting transfers between devices: 21.9 us -> 12.1 us  [neighbours(): return lax.ppermute(value, ('gx', 'gy'), pairs)]
    pallas_call x1, Pallas kernels: 53.8 us -> 46.7 us  [body(): pl.pallas_call(closure_kernel, grid=(nx,), in_specs=[whole((devices, 128)...]
    ppermute x8 -> x4, waiting for transfers between devices: 7.56 us -> 5.86 us  [neighbours(): return lax.ppermute(value, ('gx', 'gy'), pairs)]
    pallas_call x1 -> x2, Pallas kernels: 15.9 us -> 17.2 us  [the longest x1 14.1 us: body(): pl.pallas_call(moments_kernel, in_specs=[anywhere] * 2 + [near] * 4, out_...]
    unnamed x22 -> x14, local copies, waits for them, and re-layouts: 2.55 us -> 3.5 us
  transfers between devices with their start and end apart: 9 -> 5, of which waited for: 4 -> 3; matrix products, arithmetic and copies ran while one was open for 2% -> 3% of each run, Pallas kernels for 0% -> 0%
where the time goes in v4:
time: 137 us; the launch traced here: 136 us
  Pallas kernels  66 us (48%)
  starting transfers between devices  30.9 us (23%)
  blocking collectives  18.2 us (13%)
  waiting for transfers between devices  12 us (9%)
  local copies, waits for them, and re-layouts  7.9 us (6%)
    pallas_call x1, Pallas kernels, body(): pl.pallas_call(closure_kernel, grid=(nx,), in_specs=[whole((devices, 128)...  46.7 us
    all_to_all x1, starting transfers between devices, collect(): return lax.all_to_all(copies, ('gx', 'gy'), 0, 0)  18.8 us
    all_to_all x1, blocking collectives, collect(): return lax.all_to_all(copies, ('gx', 'gy'), 0, 0)  18.2 us
    pallas_call x1, Pallas kernels, body(): pl.pallas_call(moments_kernel, in_specs=[anywhere] * 2 + [near] * 4, out_...  14.1 us
    ppermute x4, starting transfers between devices, neighbours(): return lax.ppermute(value, ('gx', 'gy'), pairs)  12.1 us
    all_to_all x1, waiting for transfers between devices, collect(): return lax.all_to_all(copies, ('gx', 'gy'), 0, 0)  6.1 us
    ppermute x4, waiting for transfers between devices, neighbours(): return lax.ppermute(value, ('gx', 'gy'), pairs)  5.86 us
    unnamed x14, local copies, waits for them, and re-layouts  3.5 us
  transfers between devices with their start and end apart: 5, of which 3 were waited for; matrix products, arithmetic and copies ran while one was open for 3% of the time, Pallas kernels for 0%

profile of v4, /device:TPU:0, one launch (start us, length us, event | category | flops | bytes accessed | tf_op | source)
XLA Modules:
  0.0 136.2 jit_solution(2283316967628403647)
XLA Ops:
  0.6 2.1 %shard_map.76 = (f32[96,256]{1,0:T(8,128)}, f32[144,256]{1,0:T(8,128)}) custom-call(f32[16,128,256]{2,1,0:T(8,128)} %dens_far.1, f32[16,128,256]{2,1,0:T(8,128)} %dens_far.1, f32[3,16,128,256]{3,2,1,0:T(8,128)} %cot.1, f32[3,16,128,256]{3,2,1,0:T(8,128)} %cot.1), custom_call_target="tpu_custom_call" | custom-call | tf_op jit(solution)/shard_map/pallas_call | solution.py:358
  2.7 1.3 collective-permute-start.1
  4.0 6.5 %collective-permute-start = (f32[96,256]{1,0:T(8,128)}, f32[96,256]{1,0:T(8,128)S(1)}, u32[]{:S(2)}, u32[]{:S(2)}) collective-permute-start(f32[96,256]{1,0:T(8,128)} %get-tuple-element.12), channel_id=1, source_target_pairs={{0,1},{1,2},{2,3},{3,4},{4,5},{5,6},{6,7},{8,9},{9,10},{10,11},{11... | collective-permute-start | bytes 294920 | tf_op jit(solution)/shard_map/ppermute | solution.py:26
  10.5 4.5 %collective-permute-done.below_y = f32[96,256]{1,0:T(8,128)S(1)} collective-permute-done((f32[96,256]{1,0:T(8,128)}, f32[96,256]{1,0:T(8,128)S(1)}, u32[]{:S(2)}, u32[]{:S(2)}) %collective-permute-start) | collective-permute-done | bytes 98336 | tf_op jit(solution)/shard_map/ppermute | solution.py:26
  15.0 0.6 copy-done.3
  15.6 0.6 copy-done.1
  16.3 3.1 %shard_map.77 = (f32[3,144,256]{2,1,0:T(8,128)}, f32[4,144,256]{2,1,0:T(8,128)}) custom-call(f32[16,128,256]{2,1,0:T(8,128)} %dens_far.1, f32[16,128,256]{2,1,0:T(8,128)} %dens_far.1, f32[3,16,128,256]{3,2,1,0:T(8,128)} %cot.1, f32[3,16,128,256]{3,2,1,0:T(8,128)} %cot.1, f32[96,256]{1,0:T(8,128)} %copy-done.3, f32[144,256]{1,0:T(8,128)} %copy-done.1), custom_call_target="tpu_custom_call" | custom-call | tf_op jit(solution)/shard_map/pallas_call | solution.py:372
  19.4 1.3 collective-permute-start.3
  20.7 3.1 %collective-permute-start.2 = (f32[3,144,256]{2,1,0:T(8,128)}, f32[3,144,256]{2,1,0:T(8,128)S(1)}, u32[]{:S(2)}, u32[]{:S(2)}) collective-permute-start(f32[3,144,256]{2,1,0:T(8,128)} %get-tuple-element.14), channel_id=1, source_target_pairs={{0,8},{1,9},{2,10},{3,11},{4,12},{5,13},{6,14},{7,15},{8,16},{9,17... | collective-permute-start | bytes 1327112 | tf_op jit(solution)/shard_map/ppermute | solution.py:26
  24.0 1.4 %collective-permute-done.2.below_x = f32[3,144,256]{2,1,0:T(8,128)S(1)} collective-permute-done((f32[3,144,256]{2,1,0:T(8,128)}, f32[3,144,256]{2,1,0:T(8,128)S(1)}, u32[]{:S(2)}, u32[]{:S(2)}) %collective-permute-start.2) | collective-permute-done | bytes 442400 | tf_op jit(solution)/shard_map/ppermute | solution.py:26
  25.4 0.8 copy-done.2
  26.1 0.8 copy-done
  26.9 14.1 %shard_map.78 = (f32[17,136,256]{2,1,0:T(8,128)}, f32[17,136,256]{2,1,0:T(8,128)}, f32[128,128]{1,0:T(8,128)}) custom-call(f32[16,128,256]{2,1,0:T(8,128)} %dens_far.1, f32[3,16,128,256]{3,2,1,0:T(8,128)} %cot.1, f32[3,144,256]{2,1,0:T(8,128)} %copy-done.2, f32[4,144,256]{2,1,0:T(8,128)} %copy-done, f32[96,256]{1,0:T(8,128)} %copy-done.3, f32[144,256]{1,0:T(8,128)} %copy-done.1), custom_call_target="tpu_custom_call" | custom-call | tf_op jit(solution)/shard_map/pallas_call | solution.py:397
  41.0 18.8 %all-to-all-start = ((f32[128,1,128]{2,1,0:T(1,128)}), f32[128,1,128]{2,1,0:T(1,128)S(1)}, u32[]{:S(2)}, u32[]{:S(2)}) async-start(f32[128,1,128]{2,1,0:T(1,128)} %bitcast.12), calls=%async_computation | async-start | bytes 131072 | tf_op jit(solution)/shard_map/all_to_all | solution.py:15
  59.9 0.2 broadcast_multiply_fusion
  60.2 0.7 reshape.41.w_out
  60.9 1.4 %mul.20 = bf16[128,1024]{0,1:T(8,128)(2,1)S(1)} reshape(bf16[8,16,2,64,8]{1,0,4,3,2:T(8,128)(2,1)S(1)} %broadcast_multiply_fusion) | data formatting | bytes 524288 | tf_op jit(solution)/shard_map/mul | solution.py:390
  62.3 0.9 copy.12.w_in
  63.2 6.1 %all-to-all-done = f32[128,1,128]{2,1,0:T(1,128)S(1)} async-done(((f32[128,1,128]{2,1,0:T(1,128)}), f32[128,1,128]{2,1,0:T(1,128)S(1)}, u32[]{:S(2)}, u32[]{:S(2)}) %all-to-all-start) | async-done | bytes 65568 | tf_op jit(solution)/shard_map/all_to_all | solution.py:15
  69.3 0.6 copy-done.4
  69.9 46.7 %shard_map.79 = (f32[3,16,128,256]{3,2,1,0:T(8,128)}, f32[128,8,128]{2,1,0:T(8,128)}) custom-call(f32[128,128]{1,0:T(8,128)} %bitcast.11, f32[3,16,128,256]{3,2,1,0:T(8,128)} %cot.1, f32[17,136,256]{2,1,0:T(8,128)} %get-tuple-element.17.s, f32[17,136,256]{2,1,0:T(8,128)} %get-tuple-element.18.q, bf16[8,16,128,256]{3,2,1,0:T(8,128)(2,1)} %feats.1, ...), custom_call_target="tpu_custom_call" | custom-call | tf_op jit(solution)/shard_map/pallas_call | solution.py:412
  116.6 18.2 %all_to_all.16 = f32[128,8,128]{2,1,0:T(8,128)S(1)} all-to-all(f32[128,8,128]{2,1,0:T(8,128)} %get-tuple-element.20), channel_id=1, replica_groups=mesh['gx'=16,'gy'=8] {'gx','gy'}, dimensions={0} | all-to-all | bytes 1048576 | tf_op jit(solution)/shard_map/all_to_all | solution.py:15
  135.0 0.7 slice.7
  135.6 0.6 slice_bitcast_fusion
  (17 shorter events, 0.4 us)
Async XLA Ops:
  2.7 12.3 %collective-permute-start.1 = (f32[144,256]{1,0:T(8,128)}, f32[144,256]{1,0:T(8,128)S(1)}, u32[]{:S(2)}, u32[]{:S(2)}) collective-permute-start(f32[144,256]{1,0:T(8,128)} %get-tuple-element.13), channel_id=1, source_target_pairs={{1,0},{2,1},{3,2},{4,3},{5,4},{6,5},{7,6},{9,8},{10,9},{11,10},{12... | collective-permute-start | bytes 442376 | tf_op jit(solution)/shard_map/ppermute | solution.py:26
  4.0 19.8 %copy-start.5 = (bf16[64,8]{0,1:T(8,128)(2,1)S(1)}, bf16[64,8]{0,1:T(8,128)(2,1)}, u32[]{:S(2)}) copy-start(bf16[64,8]{0,1:T(8,128)(2,1)} %param.8) | copy-start | bytes 3076
  4.0 11.0 %collective-permute-start = (f32[96,256]{1,0:T(8,128)}, f32[96,256]{1,0:T(8,128)S(1)}, u32[]{:S(2)}, u32[]{:S(2)}) collective-permute-start(f32[96,256]{1,0:T(8,128)} %get-tuple-element.12), channel_id=1, source_target_pairs={{0,1},{1,2},{2,3},{3,4},{4,5},{5,6},{6,7},{8,9},{9,10},{10,11},{11... | collective-permute-start | bytes 294920 | tf_op jit(solution)/shard_map/ppermute | solution.py:26
  15.0 0.6 copy-start.3
  15.6 0.6 copy-start.1
  19.4 5.9 %collective-permute-start.3 = (f32[4,144,256]{2,1,0:T(8,128)}, f32[4,144,256]{2,1,0:T(8,128)S(1)}, u32[]{:S(2)}, u32[]{:S(2)}) collective-permute-start(f32[4,144,256]{2,1,0:T(8,128)} %get-tuple-element.15), channel_id=1, source_target_pairs={{8,0},{9,1},{10,2},{11,3},{12,4},{13,5},{14,6},{15,7},{16,8},{17,9... | collective-permute-start | bytes 1769480 | tf_op jit(solution)/shard_map/ppermute | solution.py:26
  20.7 4.7 %collective-permute-start.2 = (f32[3,144,256]{2,1,0:T(8,128)}, f32[3,144,256]{2,1,0:T(8,128)S(1)}, u32[]{:S(2)}, u32[]{:S(2)}) collective-permute-start(f32[3,144,256]{2,1,0:T(8,128)} %get-tuple-element.14), channel_id=1, source_target_pairs={{0,8},{1,9},{2,10},{3,11},{4,12},{5,13},{6,14},{7,15},{8,16},{9,17... | collective-permute-start | bytes 1327112 | tf_op jit(solution)/shard_map/ppermute | solution.py:26
  24.0 36.1 %copy-start.6 = (bf16[3,64]{1,0:T(4,128)(2,1)S(1)}, bf16[3,64]{1,0:T(4,128)(2,1)}, u32[]{:S(2)}) copy-start(bf16[3,64]{1,0:T(4,128)(2,1)} %param.9) | copy-start | bytes 1156
  25.3 0.8 copy-start.2
  26.1 0.8 copy-start
  41.0 28.2 %all-to-all-start = ((f32[128,1,128]{2,1,0:T(1,128)}), f32[128,1,128]{2,1,0:T(1,128)S(1)}, u32[]{:S(2)}, u32[]{:S(2)}) async-start(f32[128,1,128]{2,1,0:T(1,128)} %bitcast.12), calls=%async_computation | async-start | bytes 131072 | tf_op jit(solution)/shard_map/all_to_all | solution.py:15
  69.3 0.6 copy-start.4

commit v5 on v4

--- a/solution.py
+++ b/solution.py
@@ -8,7 +8,7 @@
 F32 = jnp.float32
 BF16 = jnp.bfloat16
 FIRST = (((0,), (0,)), ((), ()))
-VMEM = 56 * 2**20
+LAST = (((1,), (1,)), ((), ()))
 
 
 def collect(copies):
@@ -123,12 +123,10 @@
     down[3] = jnp.where(after > 0, flux - weight(after, plane(0, 2)) * plane(1, 1) + part(1), 0.0)
 
 
-def moments_kernel(
-    dens_far, cot_far, below_x, above_x, below_y, above_y,
-    s_out, q_out, sums, dens, cot, d_all, b_x, b_y, b_z, s_all, before, acc, sems,
+def source_kernel(
+    dens_far, cot_far, below_y, above_y, s_part, b_x, b_y, b_z, dens, cot, d_all, before, sems
 ):
     planes, rows, width = dens.shape
-    own = slice(8, rows + 8)
     part = planes // 4
     copies = [pltpu.make_async_copy(dens_far, dens, sems.at[4])]
     for k in range(4):
@@ -139,110 +137,133 @@
 
     def fill(x, carry):
         low, high = sides(below_y, above_y, planes, 0, x)
-        d_all[x + 1, 0:8, :] = low
-        d_all[x + 1, own, :] = dens[x]
-        d_all[x + 1, rows + 8 : rows + 16, :] = high
+        d_all[x, 0:8, :] = low
+        d_all[x, 8 : rows + 8, :] = dens[x]
+        d_all[x, rows + 8 : rows + 16, :] = high
         return carry
-
-    d_all[0] = below_x[0]
-    d_all[planes + 1] = above_x[0]
-    d_all[planes + 2] = above_x[1]
-    copies[0].wait()
-    lax.fori_loop(0, planes, fill, 0)
-
-    def weights(x):
-        at = x + 1
-        here = d_all[at]
-        b_x[at] = weight(here, d_all[at + 1])
-        b_y[at] = weight(here, next_row(here))
-        b_z[at] = weight(here, next_lane(here))
 
     def field(index, x):
         low, high = sides(below_y, above_y, planes, index, x)
         return jnp.concatenate([low, cot[index - 1, x], high], 0)
 
+    def rest(x, here):
+        b_y[x] = weight(here, next_row(here))
+        b_z[x] = weight(here, next_lane(here))
+        return across(here, b_y[x], b_z[x], field(2, x), field(3, x))
+
     def source(x, carry):
-        at = x + 1
-        here = d_all[at]
-        weights(x)
-        flux = b_x[at] * field(1, x)
-        out = before[...] - flux + across(here, b_y[at], b_z[at], field(2, x), field(3, x))
+        here = d_all[x]
+        b_x[x] = weight(here, d_all[x + 1])
+        flux = b_x[x] * field(1, x)
+        out = before[...] - flux + rest(x, here)
         before[...] = flux
-        s_all[at] = jnp.where(here > 0, out, 0.0)
+        s_part[x] = jnp.where(here > 0, out, 0.0)
         return carry
 
-    b_x[0] = weight(d_all[0], d_all[1])
-    flux = b_x[0] * below_x[1]
-    before[...] = flux
-    s_all[0] = below_x[2] - flux
+    copies[0].wait()
+    lax.fori_loop(0, planes, fill, 0)
+    before[...] = jnp.zeros_like(before)
     for k in range(4):
         copies[1 + k].wait()
-        lax.fori_loop(k * part, (k + 1) * part, source, 0)
-    s_all[planes + 1] = jnp.where(d_all[planes + 1] > 0, above_x[2] + before[...], 0.0)
-    s_all[planes + 2] = above_x[3]
-    weights(planes)
-
-    def image(x):
-        at = x + 1
-        here = s_all[at]
-        flux = b_x[at] * (s_all[at + 1] - here)
+        lax.fori_loop(k * part, min((k + 1) * part, planes - 1), source, 0)
+    here = d_all[planes - 1]
+    b_x[planes - 1] = jnp.zeros_like(here)
+    s_part[planes - 1] = jnp.where(here > 0, before[...] + rest(planes - 1, here), 0.0)
+
+
+def moments_kernel(
+    below_x, above_x, own_up, own_down, s_part, b_x, b_y, b_z,
+    s_far, q_far, sums, s_out, q_out, first, final, b_final, before, acc, sems,
+):
+    planes, width = s_part.shape[0], s_part.shape[2]
+    rows = s_part.shape[1] - 16
+    own = slice(8, rows + 8)
+    last = planes - 1
+    beta = weight(below_x[0], own_down[0])
+    flux = beta * below_x[1]
+    first[...] = s_part[0] + flux
+    before[...] = beta * (first[...] - (below_x[2] - flux))
+    b_final[...] = weight(own_up[0], above_x[0])
+    flux = b_final[...] * own_up[1]
+    final[...] = s_part[last] - flux
+    s_after = jnp.where(above_x[0] > 0, above_x[2] + flux, 0.0)
+
+    def leaving(x):
+        return (
+            pltpu.make_async_copy(s_out.at[x], s_far.at[x], sems.at[0, x]),
+            pltpu.make_async_copy(q_out.at[x], q_far.at[x], sems.at[1, x]),
+        )
+
+    def image(x, here, after, beta_x, beta_y, beta_z):
+        flux = beta_x * (after - here)
         out = before[...] - flux
         before[...] = flux
-        flux = b_y[at] * (next_row(here) - here)
+        flux = beta_y * (next_row(here) - here)
         out = out + (prior_row(flux) - flux)
-        flux = b_z[at] * (next_lane(here) - here)
+        flux = beta_z * (next_lane(here) - here)
         out = out + (prior_lane(flux) - flux)
-        out = jnp.where(d_all[at] > 0, out, 0.0)
+        out = jnp.where(beta_y > 0, out, 0.0)
         s_out[x] = here[8:]
         q_out[x] = out[8:]
+        for copy in leaving(x):
+            copy.start()
         return here, out
 
-    def squares(x, out):
-        at = x + 1
+    def jumps(x, out, beta_x):
+        jump = out[own] - q_out[x - 1, 0:rows, :]
+        acc[3] += fold(beta_x * jump * jump)
+
+    def products(x, here, out):
         jump = (next_row(out) - out)[own]
-        jump_z = next_lane(out[own]) - out[own]
-        acc[3] += fold(b_y[at, own, :] * jump * jump + b_z[at, own, :] * jump_z * jump_z)
-
-    def jumps(x, out):
-        jump = out[own] - q_out[x - 1, 0:rows, :]
-        acc[3] += fold(b_x[x, own, :] * jump * jump)
-
-    def products(here, out):
         here, out = here[own], out[own]
+        jump_z = next_lane(out) - out
+        acc[3] += fold(b_y[x, own, :] * jump * jump + b_z[x, own, :] * jump_z * jump_z)
         acc[0] += fold(here * here)
         acc[1] += fold(here * out)
         acc[2] += fold(out * out)
 
-    before[...] = b_x[0] * (s_all[1] - s_all[0])
     acc[...] = jnp.zeros_like(acc)
-    here, out = image(0)
-    products(here, out)
-    squares(0, out)
-
-    def own_image(x, carry):
-        here, out = image(x)
-        products(here, out)
-        squares(x, out)
-        jumps(x, out)
+    products(0, *image(0, first[...], s_part[1], b_x[0], b_y[0], b_z[0]))
+
+    def inside(x, carry):
+        here, out = image(x, s_part[x], s_part[x + 1], b_x[x], b_y[x], b_z[x])
+        products(x, here, out)
+        jumps(x, out, b_x[x - 1, own, :])
         return carry
 
-    lax.fori_loop(1, planes, own_image, 0)
-    here, out = image(planes)
-    jumps(planes, out)
+    lax.fori_loop(1, last - 1, inside, 0)
+    here, out = image(last - 1, s_part[last - 1], final[...], b_x[last - 1], b_y[last - 1], b_z[last - 1])
+    products(last - 1, here, out)
+    jumps(last - 1, out, b_x[last - 2, own, :])
+    here, out = image(last, final[...], s_after, b_final[...], b_y[last], b_z[last])
+    products(last, here, out)
+    jumps(last, out, b_x[last - 1, own, :])
+    after = above_x[0]
+    betas = weight(after, above_x[1]), weight(after, next_row(after)), weight(after, next_lane(after))
+    here, out = image(planes, s_after, above_x[3], *betas)
+    jumps(planes, out, b_final[own, :])
     at = lax.broadcasted_iota(jnp.int32, (1, 128), 1)
     row = jnp.zeros((1, 128), F32)
     for k in range(4):
         value = jnp.sum(jnp.sum(acc[k], 0, keepdims=True), 1, keepdims=True)
         row = row + jnp.where(at == k, value, 0.0)
     sums[...] = jnp.broadcast_to(row, sums.shape)
+    for x in range(planes + 1):
+        for copy in leaving(x):
+            copy.wait()
+
+
+def spreading(columns):
+    at_column = lax.broadcasted_iota(jnp.int32, (64, columns), 1)
+    return (at_column // 8 % 64 == lax.broadcasted_iota(jnp.int32, (64, columns), 0)).astype(F32)
 
 
 def closure_kernel(
-    sums, cot, s, q, feats, w_in, w_out,
-    grad, grads, scale, velocity, hid, slope, vel, prod, acc_o, acc_t,
+    sums, cot, s, q, s_next, q_next, feats, w_inner, w_outer,
+    grad, grads, w_in, scale, velocity, hid, slope, vel, prod, acc_o, acc_t,
 ):
-    step, planes = pl.program_id(0), s.shape[0] - 1
-    rows, width = cot.shape[2], s.shape[2]
+    step, planes = pl.program_id(0), cot.shape[1]
+    rows, width = cot.shape[2], cot.shape[3]
     count = feats.shape[0]
 
     @pl.when(step == 0)
@@ -261,19 +282,36 @@
         scale[1] = jnp.broadcast_to(-alpha1 * alpha0, scale.shape[1:])
         acc_o[...] = jnp.zeros_like(acc_o)
         acc_t[...] = jnp.zeros_like(acc_t)
+        at_row, at_column = (lax.broadcasted_iota(jnp.int32, w_in.shape, k) for k in range(2))
+        pick = lax.broadcasted_iota(jnp.int32, (w_in.shape[0], count), 0) // 16
+        pick = (pick == lax.broadcasted_iota(jnp.int32, pick.shape, 1)).astype(BF16)
+        tall = lax.dot_general(pick, w_inner[...], LAST, preferred_element_type=F32).astype(BF16)
+        spread = jnp.dot(tall, spreading(w_in.shape[1]).astype(BF16), preferred_element_type=F32)
+        same = at_row % 16 == at_column // (w_in.shape[1] // 2) * 8 + at_column % 8
+        w_in[...] = jnp.where(same, spread, 0.0).astype(BF16)
 
     on_s, on_q = scale[0][:1], scale[1][:1]
-    last = step == planes - 1
-    wide = on_s * s[step] + on_q * q[step]
-    here = wide[:rows]
-    beyond = on_s * s[step + 1, :rows, :] + on_q * q[step + 1, :rows, :]
-    for a, after in enumerate((beyond, next_row(wide)[:rows], next_lane(here))):
-        value = cot[a, 0] - (after - here)
-        grad[a, 0] = value
-        velocity[a] = value.astype(BF16).astype(F32)
+    last = step == pl.num_programs(0) - 1
+    beyond = on_s * s[0] + on_q * q[0]
+    for x in range(planes):
+        wide = beyond
+        if x + 1 < planes:
+            beyond = on_s * s[x + 1] + on_q * q[x + 1]
+        else:
+            beyond = on_s * s_next[0] + on_q * q_next[0]
+        here = wide[:rows]
+        for a, after in enumerate((beyond[:rows], next_row(wide)[:rows], next_lane(here))):
+            value = cot[a, x] - (after - here)
+            grad[a, x] = value
+            velocity[a, x] = value.astype(BF16).astype(F32)
 
     half = w_in.shape[1] // 2
-    blocks, wide_tile = rows // 16, 256
+    per_plane, wide_tile = rows // 16, 256
+    blocks = planes * per_plane
+
+    def place_of(block):
+        x, at = divmod(block, per_plane)
+        return x, slice(at * 16, at * 16 + 16)
 
     def place(block, tile):
         part, column = divmod(tile * wide_tile, half)
@@ -281,7 +319,8 @@
         return slice(cells, cells + width), slice(column, column + wide_tile)
 
     def first_layer(block, tile):
-        inner = feats[:, 0, block * 16 : block * 16 + 16, :].reshape(count * 16, width)
+        x, at = place_of(block)
+        inner = feats[:, x, at, :].reshape(count * 16, width)
         weights = w_in[:, tile * wide_tile : (tile + 1) * wide_tile]
         pre = lax.dot_general(inner, weights, FIRST, preferred_element_type=F32)
         hidden = jnp.tanh(pre)
@@ -294,12 +333,12 @@
         acc_o[:, columns] += jnp.dot(vel[:, cells], hid[cells, columns], preferred_element_type=F32)
 
     for block in range(blocks):
-        at = slice(block * 16, block * 16 + 16)
-        broad = [feats[c, 0, at, :].astype(F32) for c in range(count)]
+        x, at = place_of(block)
+        broad = [feats[c, x, at, :].astype(F32) for c in range(count)]
         for part in range(2):
             to = slice((block * 2 + part) * width, (block * 2 + part + 1) * width)
-            low = block * 16 + part * 8
-            vs = [velocity[a, low : low + 8, :] for a in range(3)]
+            low = at.start + part * 8
+            vs = [velocity[a, x, low : low + 8, :] for a in range(3)]
             vel[:, to] = jnp.concatenate(vs + [jnp.zeros_like(vs[0])], 0).astype(BF16)
             fs = [f[part * 8 : part * 8 + 8] for f in broad]
             prod[:, to] = jnp.concatenate([v * f for v in vs for f in fs], 0).astype(BF16)
@@ -323,6 +362,7 @@
 
         outermost = own(acc_o[...])
         terms = own(acc_t[...])
+        w_out = jnp.dot(w_outer[...], spreading(half).astype(BF16), preferred_element_type=F32)
         inner = sum(
             w_out[a : a + 1] * terms[a * count : (a + 1) * count] for a in range(3)
         )
@@ -331,8 +371,8 @@
         column = lax.broadcasted_iota(jnp.int32, (half, 64), 1)
         pick = (hidden_at == column).astype(F32)
         sums16 = jnp.dot(both, pick, precision=lax.Precision.HIGHEST, preferred_element_type=F32)
-        value = jnp.concatenate([sums16[:8], sums16[8:]], 1)
-        grads[...] = jnp.broadcast_to(value[None], grads.shape)
+        value = [sums16[k : k + 1] for k in (0, 4, 1, 5, 2, 6, 3, 7, 8, 10, 9, 11)]
+        grads[...] = jnp.broadcast_to(jnp.concatenate(value, 1)[None], grads.shape)
 
 
 def whole(shape):
@@ -343,16 +383,28 @@
     return jax.ShapeDtypeStruct(dims, F32)
 
 
-def params():
-    return pltpu.CompilerParams(vmem_limit_bytes=VMEM)
+def held(*dims):
+    return pltpu.VMEM(dims, F32)
+
+
+def keep(value):
+    return pltpu.with_memory_space_constraint(value, pltpu.VMEM)
+
+
+def away(value):
+    return pltpu.with_memory_space_constraint(value, pltpu.HBM)
+
+
+def params(mebibytes=24):
+    return pltpu.CompilerParams(vmem_limit_bytes=mebibytes * 2**20)
 
 
 def body(density, cotangent, features, w_inner, w_outer):
     nx, ny, nz = density.shape
     count, hidden = features.shape[0], w_inner.shape[0]
+    density, cotangent, features = map(away, (density, cotangent, features))
     devices = lax.axis_size("gx") * lax.axis_size("gy")
     cells = float(density.size * devices)
-    planes = pl.BlockSpec((3, 1, ny, nz), lambda i: (0, i, 0, 0))
     lines, ends = ny // 8 - 1, nx // 2 - 1
     around = (ny + 16, nz)
     to_up, to_down = pl.pallas_call(
@@ -383,44 +435,57 @@
         out_specs=[whole((3,) + around), whole((4,) + around)],
         out_shape=[shape(3, *around), shape(4, *around)],
         compiler_params=params(),
-    )(density, density, cotangent, cotangent, below_y, above_y)
-    halo = [neighbours(to_up, 1, 0), neighbours(to_down, -1, 0), below_y, above_y]
-
-    pick = jnp.arange(16)[:, None, None] == jnp.arange(16).reshape(1, 2, 8)
-    w_in = w_inner.T[:, None, None, :, None] * pick[None, :, :, None, :].astype(BF16)
-    w_in = w_in.reshape(count * 16, 2 * hidden * 8)
-    w_out = jnp.repeat(w_outer.astype(F32), 8, axis=1)
+    )(density, density, cotangent, cotangent, keep(below_y), keep(above_y))
+    below_x, above_x = neighbours(to_up, 1, 0), neighbours(to_down, -1, 0)
 
     extended = (nx + 1, ny + 8, nz)
     anywhere = pl.BlockSpec(memory_space=pl.ANY)
     near = pl.BlockSpec(memory_space=pltpu.VMEM)
+    whole_planes = (nx,) + around
+    fields = pl.pallas_call(
+        source_kernel,
+        in_specs=[anywhere] * 2 + [near] * 2,
+        out_shape=[held(*whole_planes)] * 4,
+        scratch_shapes=[
+            pltpu.VMEM((nx, ny, nz), F32),
+            pltpu.VMEM((3, nx, ny, nz), F32),
+            pltpu.VMEM(whole_planes, F32),
+            pltpu.VMEM(around, F32),
+            pltpu.SemaphoreType.DMA((5,)),
+        ],
+        compiler_params=params(30),
+    )(density, cotangent, keep(below_y), keep(above_y))
     s, q, sums = pl.pallas_call(
         moments_kernel,
-        in_specs=[anywhere] * 2 + [near] * 4,
-        out_shape=[shape(*extended), shape(*extended), shape(devices, 128)],
-        scratch_shapes=[pltpu.VMEM((nx, ny, nz), F32), pltpu.VMEM((3, nx, ny, nz), F32)]
-        + [pltpu.VMEM((nx + 3,) + around, F32)]
-        + [pltpu.VMEM((nx + 2,) + around, F32)] * 3
-        + [pltpu.VMEM((nx + 3,) + around, F32)]
-        + [pltpu.VMEM(around, F32), pltpu.VMEM((4, 8, nz), F32), pltpu.SemaphoreType.DMA((5,))],
-        compiler_params=params(),
-    )(density, cotangent, *halo)
+        in_specs=[near] * 8,
+        out_specs=[pl.BlockSpec(memory_space=pltpu.HBM)] * 2 + [near],
+        out_shape=[pltpu.HBM(extended, F32)] * 2 + [held(devices, 128)],
+        scratch_shapes=[pltpu.VMEM(extended, F32)] * 2
+        + [pltpu.VMEM(around, F32)] * 4
+        + [pltpu.VMEM((4, 8, nz), F32), pltpu.SemaphoreType.DMA((2, nx + 1))],
+        compiler_params=params(30),
+    )(keep(below_x), keep(above_x), keep(to_up), keep(to_down), *fields)
     sums = collect(sums)
 
     half = hidden * 8
-    long = ny // 8 * nz
+    step = 2
+    long = step * ny // 8 * nz
+    planes = pl.BlockSpec((3, step, ny, nz), lambda i: (0, i, 0, 0))
+    here = pl.BlockSpec((step, ny + 8, nz), lambda i: (i, 0, 0))
+    after = pl.BlockSpec((1, ny + 8, nz), lambda i: (step * i + step, 0, 0))
     grad, grads = pl.pallas_call(
         closure_kernel,
-        grid=(nx,),
+        grid=(nx // step,),
         in_specs=[
-            whole((devices, 128)), planes, whole(extended), whole(extended),
-            pl.BlockSpec((count, 1, ny, nz), lambda i: (0, i, 0, 0)), whole(w_in.shape), whole(w_out.shape),
+            whole((devices, 128)), planes, here, here, after, after,
+            pl.BlockSpec((count, step, ny, nz), lambda i: (0, i, 0, 0)), whole(w_inner.shape), whole(w_outer.shape),
         ],
-        out_specs=[planes, whole((devices, 8, 128))],
-        out_shape=[shape(3, nx, ny, nz), shape(devices, 8, 128)],
+        out_specs=[planes, whole((devices, 1, 768))],
+        out_shape=[shape(3, nx, ny, nz), shape(devices, 1, 768)],
         scratch_shapes=[
+            pltpu.VMEM((count * 16, 2 * half), BF16),
             pltpu.VMEM((2, 8, nz), F32),
-            pltpu.VMEM((3, ny, nz), F32),
+            pltpu.VMEM((3, step, ny, nz), F32),
             pltpu.VMEM((long, half), BF16),
             pltpu.VMEM((long, half), BF16),
             pltpu.VMEM((32, long), BF16),
@@ -428,10 +493,11 @@
             pltpu.VMEM((32, half), F32),
             pltpu.VMEM((24 * count, half), F32),
         ],
-        compiler_params=params(),
-    )(sums, cotangent, s, q, features, w_in, w_out)
-    grads = jnp.sum(collect(grads), 0) / cells
-    return grad, grads[:, :hidden].T, grads[:3, hidden:]
+        compiler_params=params(48),
+    )(keep(sums), cotangent, *map(away, (s, q, s, q)), features, w_inner, w_outer)
+    grads = jnp.sum(collect(grads), 0).reshape(6, 128) / cells
+    low, high = grads[:, :hidden], grads[:, hidden:]
+    return grad, jnp.concatenate([low[:4], high[:4]]).T, jnp.concatenate([low[4:], high[4:5]])
 
 
 def solution(mesh):

time: 137 us -> 118 us (0.86)
  local copies, waits for them, and re-layouts: 7.9 us -> 0.26 us
  Pallas kernels: 66 us -> 59 us
  starting transfers between devices: 30.9 us -> 26.5 us
  blocking collectives: 18.2 us -> 16.4 us
  waiting for transfers between devices: 12 us -> 13.4 us
    pallas_call x2 -> x3, Pallas kernels: 60.8 us -> 55.4 us  [the longest x1 43 us: body(): pl.pallas_call(closure_kernel, grid=(nx // step,), in_specs=[whole((devic...]
    all_to_all x1, starting transfers between devices: 18.8 us -> 14.3 us  [collect(): return lax.all_to_all(copies, ('gx', 'gy'), 0, 0)]
    unnamed x14 -> x5, local copies, waits for them, and re-layouts: 3.5 us -> 0.11 us
    all_to_all x1, waiting for transfers between devices: 6.1 us -> 9.21 us  [collect(): return lax.all_to_all(copies, ('gx', 'gy'), 0, 0)]
    mul x2 -> x0, local copies, waits for them, and re-layouts: 2.26 us -> none  [body(): w_inner.T[:, None, None, :, None] * pick[None, :, :, None, :].astype(BF16)]
    all_to_all x1, blocking collectives: 18.2 us -> 16.4 us  [collect(): return lax.all_to_all(copies, ('gx', 'gy'), 0, 0)]
    ppermute x4, waiting for transfers between devices: 5.86 us -> 4.17 us  [neighbours(): return lax.ppermute(value, ('gx', 'gy'), pairs)]
  transfers between devices with their start and end apart: 5 -> 5, of which waited for: 3 -> 2; matrix products, arithmetic and copies ran while one was open for 3% -> 0% of each run, Pallas kernels for 0% -> 5%
where the time goes in v5:
time: 118 us
  Pallas kernels  59 us (50%)
  starting transfers between devices  26.5 us (22%)
  blocking collectives  16.4 us (14%)
  waiting for transfers between devices  13.4 us (11%)
  other arithmetic  1.47 us (1%)
    pallas_call x1, Pallas kernels, body(): pl.pallas_call(closure_kernel, grid=(nx // step,), in_specs=[whole((devic...  43 us
    all_to_all x1, blocking collectives, collect(): return lax.all_to_all(copies, ('gx', 'gy'), 0, 0)  16.4 us
    all_to_all x1, starting transfers between devices, collect(): return lax.all_to_all(copies, ('gx', 'gy'), 0, 0)  14.3 us
    ppermute x4, starting transfers between devices, neighbours(): return lax.ppermute(value, ('gx', 'gy'), pairs)  12.1 us
    all_to_all x1, waiting for transfers between devices, collect(): return lax.all_to_all(copies, ('gx', 'gy'), 0, 0)  9.21 us
    pallas_call x1, Pallas kernels, body(): pl.pallas_call(moments_kernel, in_specs=[near] * 8, out_specs=[pl.BlockSp...  6.49 us
    pallas_call x1, Pallas kernels, body(): pl.pallas_call(source_kernel, in_specs=[anywhere] * 2 + [near] * 2, out_s...  5.94 us
    ppermute x4, waiting for transfers between devices, neighbours(): return lax.ppermute(value, ('gx', 'gy'), pairs)  4.17 us
  transfers between devices with their start and end apart: 5, of which 2 were waited for; matrix products, arithmetic and copies ran while one was open for 0% of the time, Pallas kernels for 5%

profile of v5, /device:TPU:0, one launch (start us, length us, event | category | flops | bytes accessed | tf_op | source)
XLA Modules:
  0.0 117.7 jit_solution(2464820164286123251)
XLA Ops:
  0.6 1.4 %shard_map.76 = (f32[96,256]{1,0:T(8,128)S(1)}, f32[144,256]{1,0:T(8,128)S(1)}) custom-call(f32[16,128,256]{2,1,0:T(8,128)} %dens_far.1, f32[16,128,256]{2,1,0:T(8,128)} %dens_far.1, f32[3,16,128,256]{3,2,1,0:T(8,128)} %cot.1, f32[3,16,128,256]{3,2,1,0:T(8,128)} %cot.1), custom_call_target="tpu_custom_call" | custom-call | tf_op jit(solution)/shard_map/pallas_call | solution.py:410
  2.0 1.3 %collective-permute-start.1 = (f32[144,256]{1,0:T(8,128)S(1)}, f32[144,256]{1,0:T(8,128)S(1)}, u32[]{:S(2)}, u32[]{:S(2)}) collective-permute-start(f32[144,256]{1,0:T(8,128)S(1)} %get-tuple-element.17), channel_id=1, source_target_pairs={{1,0},{2,1},{3,2},{4,3},{5,4},{6,5},{7,6},{9,8},{10,9},{11,10},{12... | collective-permute-start | bytes 442376 | tf_op jit(solution)/shard_map/ppermute | solution.py:26
  3.3 6.5 %collective-permute-start = (f32[96,256]{1,0:T(8,128)S(1)}, f32[96,256]{1,0:T(8,128)S(1)}, u32[]{:S(2)}, u32[]{:S(2)}) collective-permute-start(f32[96,256]{1,0:T(8,128)S(1)} %get-tuple-element.16), channel_id=1, source_target_pairs={{0,1},{1,2},{2,3},{3,4},{4,5},{5,6},{6,7},{8,9},{9,10},{10,11},{11... | collective-permute-start | bytes 294920 | tf_op jit(solution)/shard_map/ppermute | solution.py:26
  9.8 4.2 %collective-permute-done.below_y = f32[96,256]{1,0:T(8,128)S(1)} collective-permute-done((f32[96,256]{1,0:T(8,128)S(1)}, f32[96,256]{1,0:T(8,128)S(1)}, u32[]{:S(2)}, u32[]{:S(2)}) %collective-permute-start) | collective-permute-done | bytes 98336 | tf_op jit(solution)/shard_map/ppermute | solution.py:26
  14.0 0.0 collective-permute-done.1.above_y
  14.0 2.2 %shard_map.77 = (f32[3,144,256]{2,1,0:T(8,128)S(1)}, f32[4,144,256]{2,1,0:T(8,128)S(1)}) custom-call(f32[16,128,256]{2,1,0:T(8,128)} %dens_far.1, f32[16,128,256]{2,1,0:T(8,128)} %dens_far.1, f32[3,16,128,256]{3,2,1,0:T(8,128)} %cot.1, f32[3,16,128,256]{3,2,1,0:T(8,128)} %cot.1, f32[96,256]{1,0:T(8,128)S(1)} %collective-permute-done.below_y, ...), custom_call_target="tpu_custom_call" | custom-call | tf_op jit(solution)/shard_map/pallas_call | solution.py:424
  16.2 1.3 %collective-permute-start.3 = (f32[4,144,256]{2,1,0:T(8,128)S(1)}, f32[4,144,256]{2,1,0:T(8,128)S(1)}, u32[]{:S(2)}, u32[]{:S(2)}) collective-permute-start(f32[4,144,256]{2,1,0:T(8,128)S(1)} %get-tuple-element.19.own_down), channel_id=1, source_target_pairs={{8,0},{9,1},{10,2},{11,3},{12,4},{13,5},{14,6},{15,7},{16,8},{17,9... | collective-permute-start | bytes 1769480 | tf_op jit(solution)/shard_map/ppermute | solution.py:26
  17.5 3.1 %collective-permute-start.2 = (f32[3,144,256]{2,1,0:T(8,128)S(1)}, f32[3,144,256]{2,1,0:T(8,128)S(1)}, u32[]{:S(2)}, u32[]{:S(2)}) collective-permute-start(f32[3,144,256]{2,1,0:T(8,128)S(1)} %get-tuple-element.18.own_up), channel_id=1, source_target_pairs={{0,8},{1,9},{2,10},{3,11},{4,12},{5,13},{6,14},{7,15},{8,16},{9,17... | collective-permute-start | bytes 1327112 | tf_op jit(solution)/shard_map/ppermute | solution.py:26
  20.5 5.9 %shard_map.78 = (f32[16,144,256]{2,1,0:T(8,128)S(1)}, f32[16,144,256]{2,1,0:T(8,128)S(1)}, f32[16,144,256]{2,1,0:T(8,128)S(1)}, f32[16,144,256]{2,1,0:T(8,128)S(1)}) custom-call(f32[16,128,256]{2,1,0:T(8,128)} %dens_far.1, f32[3,16,128,256]{3,2,1,0:T(8,128)} %cot.1, f32[96,256]{1,0:T(8,128)S(1)} %collective-permute-done.below_y, ...), custom_call_target="tpu_custom_call" | custom-call | tf_op jit(solution)/shard_map/pallas_call | solution.py:445
  26.5 0.0 collective-permute-done.2.below_x
  26.5 0.0 collective-permute-done.3.above_x
  26.5 0.0 copy-start.1
  26.5 0.0 copy-start
  26.5 6.5 %shard_map.79 = (f32[17,136,256]{2,1,0:T(8,128)}, f32[17,136,256]{2,1,0:T(8,128)}, f32[128,128]{1,0:T(8,128)}) custom-call(f32[3,144,256]{2,1,0:T(8,128)S(1)} %collective-permute-done.2.below_x, f32[4,144,256]{2,1,0:T(8,128)S(1)} %collective-permute-done.3.above_x, f32[3,144,256]{2,1,0:T(8,128)S(1)} %get-tuple-element.18.own_up, ...), custom_call_target="tpu_custom_call" | custom-call | tf_op jit(solution)/shard_map/pallas_call | solution.py:458
  33.0 14.3 %all-to-all-start = ((f32[128,1,128]{2,1,0:T(1,128)}), f32[128,1,128]{2,1,0:T(1,128)S(1)}, u32[]{:S(2)}, u32[]{:S(2)}) async-start(f32[128,1,128]{2,1,0:T(1,128)} %bitcast.1), calls=%async_computation | async-start | bytes 131072 | tf_op jit(solution)/shard_map/all_to_all | solution.py:15
  47.4 0.1 copy.10.w_inner
  47.5 9.2 %all-to-all-done = f32[128,1,128]{2,1,0:T(1,128)S(1)} async-done(((f32[128,1,128]{2,1,0:T(1,128)}), f32[128,1,128]{2,1,0:T(1,128)S(1)}, u32[]{:S(2)}, u32[]{:S(2)}) %all-to-all-start) | async-done | bytes 65568 | tf_op jit(solution)/shard_map/all_to_all | solution.py:15
  56.7 43.0 %shard_map.80 = (f32[3,16,128,256]{3,2,1,0:T(8,128)}, f32[128,1,768]{2,1,0:T(1,128)S(1)}) custom-call(f32[128,128]{1,0:T(8,128)S(1)} %bitcast.8, f32[3,16,128,256]{3,2,1,0:T(8,128)} %cot.1, f32[17,136,256]{2,1,0:T(8,128)} %get-tuple-element.25.s.s_next, f32[17,136,256]{2,1,0:T(8,128)} %get-tuple-element.26.q.q_next, ...), custom_call_target="tpu_custom_call" | custom-call | tf_op jit(solution)/shard_map/pallas_call | solution.py:476
  99.7 16.4 %all_to_all.16 = f32[128,1,768]{2,1,0:T(1,128)S(1)} all-to-all(f32[128,1,768]{2,1,0:T(1,128)S(1)} %get-tuple-element.28), channel_id=1, replica_groups=mesh['gx'=16,'gy'=8] {'gx','gy'}, dimensions={0} | all-to-all | bytes 786432 | tf_op jit(solution)/shard_map/all_to_all | solution.py:15
  116.1 0.3 reduce_sum.9
  116.4 0.1 slice.21
  116.5 0.1 fusion
  116.5 0.6 pad_maximum_fusion
  117.1 0.6 maximum_bitcast_fusion
  (4 shorter events, 0.0 us)
Async XLA Ops:
  2.0 12.0 %collective-permute-start.1 = (f32[144,256]{1,0:T(8,128)S(1)}, f32[144,256]{1,0:T(8,128)S(1)}, u32[]{:S(2)}, u32[]{:S(2)}) collective-permute-start(f32[144,256]{1,0:T(8,128)S(1)} %get-tuple-element.17), channel_id=1, source_target_pairs={{1,0},{2,1},{3,2},{4,3},{5,4},{6,5},{7,6},{9,8},{10,9},{11,10},{12... | collective-permute-start | bytes 442376 | tf_op jit(solution)/shard_map/ppermute | solution.py:26
  3.3 10.7 %collective-permute-start = (f32[96,256]{1,0:T(8,128)S(1)}, f32[96,256]{1,0:T(8,128)S(1)}, u32[]{:S(2)}, u32[]{:S(2)}) collective-permute-start(f32[96,256]{1,0:T(8,128)S(1)} %get-tuple-element.16), channel_id=1, source_target_pairs={{0,1},{1,2},{2,3},{3,4},{4,5},{5,6},{6,7},{8,9},{9,10},{10,11},{11... | collective-permute-start | bytes 294920 | tf_op jit(solution)/shard_map/ppermute | solution.py:26
  16.2 10.3 %collective-permute-start.3 = (f32[4,144,256]{2,1,0:T(8,128)S(1)}, f32[4,144,256]{2,1,0:T(8,128)S(1)}, u32[]{:S(2)}, u32[]{:S(2)}) collective-permute-start(f32[4,144,256]{2,1,0:T(8,128)S(1)} %get-tuple-element.19.own_down), channel_id=1, source_target_pairs={{8,0},{9,1},{10,2},{11,3},{12,4},{13,5},{14,6},{15,7},{16,8},{17,9... | collective-permute-start | bytes 1769480 | tf_op jit(solution)/shard_map/ppermute | solution.py:26
  17.5 9.0 %collective-permute-start.2 = (f32[3,144,256]{2,1,0:T(8,128)S(1)}, f32[3,144,256]{2,1,0:T(8,128)S(1)}, u32[]{:S(2)}, u32[]{:S(2)}) collective-permute-start(f32[3,144,256]{2,1,0:T(8,128)S(1)} %get-tuple-element.18.own_up), channel_id=1, source_target_pairs={{0,8},{1,9},{2,10},{3,11},{4,12},{5,13},{6,14},{7,15},{8,16},{9,17... | collective-permute-start | bytes 1327112 | tf_op jit(solution)/shard_map/ppermute | solution.py:26
  26.5 20.8 %copy-start.1 = (bf16[64,8]{0,1:T(8,128)(2,1)S(1)}, bf16[64,8]{0,1:T(8,128)(2,1)}, u32[]{:S(2)}) copy-start(bf16[64,8]{0,1:T(8,128)(2,1)} %param.8) | copy-start | bytes 3076
  26.5 30.2 %copy-start = (bf16[3,64]{1,0:T(4,128)(2,1)S(1)}, bf16[3,64]{1,0:T(4,128)(2,1)}, u32[]{:S(2)}) copy-start(bf16[3,64]{1,0:T(4,128)(2,1)} %w_outer.1) | copy-start | bytes 1156
  33.0 23.6 %all-to-all-start = ((f32[128,1,128]{2,1,0:T(1,128)}), f32[128,1,128]{2,1,0:T(1,128)S(1)}, u32[]{:S(2)}, u32[]{:S(2)}) async-start(f32[128,1,128]{2,1,0:T(1,128)} %bitcast.1), calls=%async_computation | async-start | bytes 131072 | tf_op jit(solution)/shard_map/all_to_all | solution.py:15

commit v6 on v5

--- a/solution.py
+++ b/solution.py
@@ -98,13 +98,12 @@
     return prior_row(flux_y) - flux_y + (prior_lane(flux_z) - flux_z)
 
 
-def edge_kernel(d_low, d_high, c_low, c_high, below_y, above_y, up, down):
-    planes = below_y.shape[0] // starts(LOWER_Y)[1]
+def edge_kernel(dens, cot, below_y, above_y, up, down):
+    planes = dens.shape[0]
 
     def plane(field, x):
         low, high = sides(below_y, above_y, planes, field, x)
-        d, c, at = (d_low, c_low, x) if x < 4 else (d_high, c_high, x - planes + 2)
-        return jnp.concatenate([low, d[at] if field == 0 else c[field - 1, at], high], 0)
+        return jnp.concatenate([low, dens[x] if field == 0 else cot[field - 1, x], high], 0)
 
     def part(x):
         here = plane(0, x)
@@ -124,16 +123,9 @@
 
 
 def source_kernel(
-    dens_far, cot_far, below_y, above_y, s_part, b_x, b_y, b_z, dens, cot, d_all, before, sems
+    dens, cot, below_y, above_y, s_part, b_x, b_y, b_z, d_all, before
 ):
     planes, rows, width = dens.shape
-    part = planes // 4
-    copies = [pltpu.make_async_copy(dens_far, dens, sems.at[4])]
-    for k in range(4):
-        span = pl.ds(k * part, part)
-        copies.append(pltpu.make_async_copy(cot_far.at[:, span], cot.at[:, span], sems.at[k]))
-    for copy in copies:
-        copy.start()
 
     def fill(x, carry):
         low, high = sides(below_y, above_y, planes, 0, x)
@@ -160,97 +152,135 @@
         s_part[x] = jnp.where(here > 0, out, 0.0)
         return carry
 
-    copies[0].wait()
     lax.fori_loop(0, planes, fill, 0)
     before[...] = jnp.zeros_like(before)
-    for k in range(4):
-        copies[1 + k].wait()
-        lax.fori_loop(k * part, min((k + 1) * part, planes - 1), source, 0)
+    lax.fori_loop(0, planes - 1, source, 0)
     here = d_all[planes - 1]
     b_x[planes - 1] = jnp.zeros_like(here)
     s_part[planes - 1] = jnp.where(here > 0, before[...] + rest(planes - 1, here), 0.0)
 
 
-def moments_kernel(
-    below_x, above_x, own_up, own_down, s_part, b_x, b_y, b_z,
-    s_far, q_far, sums, s_out, q_out, first, final, b_final, before, acc, sems,
-):
-    planes, width = s_part.shape[0], s_part.shape[2]
-    rows = s_part.shape[1] - 16
-    own = slice(8, rows + 8)
-    last = planes - 1
-    beta = weight(below_x[0], own_down[0])
-    flux = beta * below_x[1]
-    first[...] = s_part[0] + flux
-    before[...] = beta * (first[...] - (below_x[2] - flux))
-    b_final[...] = weight(own_up[0], above_x[0])
-    flux = b_final[...] * own_up[1]
-    final[...] = s_part[last] - flux
-    s_after = jnp.where(above_x[0] > 0, above_x[2] + flux, 0.0)
+def image(here, after, before, beta_x, beta_y, beta_z):
+    flux_x = beta_x * (after - here)
+    out = before - flux_x
+    flux = beta_y * (next_row(here) - here)
+    out = out + (prior_row(flux) - flux)
+    flux = beta_z * (next_lane(here) - here)
+    out = out + (prior_lane(flux) - flux)
+    return jnp.where(beta_y > 0, out, 0.0), flux_x
+
+
+def products(acc, here, out, beta_y, beta_z):
+    own = slice(8, here.shape[0] - 8)
+    jump = (next_row(out) - out)[own]
+    here, out = here[own], out[own]
+    jump_z = next_lane(out) - out
+    acc[3] += fold(beta_y[own] * jump * jump + beta_z[own] * jump_z * jump_z)
+    acc[0] += fold(here * here)
+    acc[1] += fold(here * out)
+    acc[2] += fold(out * out)
+
+
+def jumps(acc, out, prior, beta_x):
+    rows = prior.shape[0] - 8
+    jump = out[8 : rows + 8] - prior[:rows]
+    acc[3] += fold(beta_x[8 : rows + 8] * jump * jump)
+
+
+def inner_kernel(s_part, b_x, b_y, b_z, s_far, q_far, ends, acc, q_out, before, sems):
+    planes, rows = s_part.shape[0], s_part.shape[1]
+    first, last = 2, planes - 3
 
     def leaving(x):
         return (
-            pltpu.make_async_copy(s_out.at[x], s_far.at[x], sems.at[0, x]),
+            pltpu.make_async_copy(s_part.at[x, pl.ds(8, rows - 8)], s_far.at[x], sems.at[0, x]),
             pltpu.make_async_copy(q_out.at[x], q_far.at[x], sems.at[1, x]),
         )
 
-    def image(x, here, after, beta_x, beta_y, beta_z):
-        flux = beta_x * (after - here)
-        out = before[...] - flux
+    def plane(x):
+        here = s_part[x]
+        out, flux = image(here, s_part[x + 1], before[...], b_x[x], b_y[x], b_z[x])
         before[...] = flux
-        flux = beta_y * (next_row(here) - here)
-        out = out + (prior_row(flux) - flux)
-        flux = beta_z * (next_lane(here) - here)
-        out = out + (prior_lane(flux) - flux)
-        out = jnp.where(beta_y > 0, out, 0.0)
-        s_out[x] = here[8:]
         q_out[x] = out[8:]
         for copy in leaving(x):
             copy.start()
-        return here, out
-
-    def jumps(x, out, beta_x):
-        jump = out[own] - q_out[x - 1, 0:rows, :]
-        acc[3] += fold(beta_x * jump * jump)
-
-    def products(x, here, out):
-        jump = (next_row(out) - out)[own]
-        here, out = here[own], out[own]
-        jump_z = next_lane(out) - out
-        acc[3] += fold(b_y[x, own, :] * jump * jump + b_z[x, own, :] * jump_z * jump_z)
-        acc[0] += fold(here * here)
-        acc[1] += fold(here * out)
-        acc[2] += fold(out * out)
+        products(acc, here, out, b_y[x], b_z[x])
+        return out
+
+    def inside(x, carry):
+        jumps(acc, plane(x), q_out[x - 1], b_x[x - 1])
+        return carry
 
     acc[...] = jnp.zeros_like(acc)
-    products(0, *image(0, first[...], s_part[1], b_x[0], b_y[0], b_z[0]))
-
-    def inside(x, carry):
-        here, out = image(x, s_part[x], s_part[x + 1], b_x[x], b_y[x], b_z[x])
-        products(x, here, out)
-        jumps(x, out, b_x[x - 1, own, :])
-        return carry
-
-    lax.fori_loop(1, last - 1, inside, 0)
-    here, out = image(last - 1, s_part[last - 1], final[...], b_x[last - 1], b_y[last - 1], b_z[last - 1])
-    products(last - 1, here, out)
-    jumps(last - 1, out, b_x[last - 2, own, :])
-    here, out = image(last, final[...], s_after, b_final[...], b_y[last], b_z[last])
-    products(last, here, out)
-    jumps(last, out, b_x[last - 1, own, :])
+    before[...] = b_x[first - 1] * (s_part[first] - s_part[first - 1])
+    plane(first)
+    lax.fori_loop(first + 1, last + 1, inside, 0)
+    ends[0] = q_out[first]
+    ends[1] = q_out[last]
+    for x in range(first, last + 1):
+        for copy in leaving(x):
+            copy.wait()
+
+
+def moments_kernel(
+    below_x, above_x, own_up, own_down, s_part, b_x, b_y, b_z, ends, inner, s_in, q_in,
+    s_far, q_far, sums, s_out, q_out, acc, sems,
+):
+    planes = s_part.shape[0]
+    last = planes - 1
+    copies = []
+
+    def leave(x, here, out):
+        at = len(copies) // 2
+        s_out[at] = here[8:]
+        q_out[at] = out[8:]
+        for kind, (source, to) in enumerate(((s_out, s_far), (q_out, q_far))):
+            copies.append(pltpu.make_async_copy(source.at[at], to.at[x], sems.at[kind, at]))
+            copies[-1].start()
+
+    acc[...] = inner[...]
+    beta = weight(below_x[0], own_down[0])
+    flux = beta * below_x[1]
+    here = s_part[0] + flux
+    before = beta * (here - (below_x[2] - flux))
+    out, before = image(here, s_part[1], before, b_x[0], b_y[0], b_z[0])
+    products(acc, here, out, b_y[0], b_z[0])
+    leave(0, here, out)
+    here = s_part[1]
+    out, before = image(here, s_part[2], before, b_x[1], b_y[1], b_z[1])
+    products(acc, here, out, b_y[1], b_z[1])
+    jumps(acc, out, q_out[0], b_x[0])
+    leave(1, here, out)
+    jump = ends[0, : s_part.shape[1] - 16, :] - q_out[1, : s_part.shape[1] - 16, :]
+    acc[3] += fold(b_x[1, 8 : s_part.shape[1] - 8, :] * jump * jump)
+
+    b_final = weight(own_up[0], above_x[0])
+    flux = b_final * own_up[1]
+    final = s_part[last] - flux
+    s_after = jnp.where(above_x[0] > 0, above_x[2] + flux, 0.0)
+    here = s_part[last - 1]
+    before = b_x[last - 2] * (here - s_part[last - 2])
+    out, before = image(here, final, before, b_x[last - 1], b_y[last - 1], b_z[last - 1])
+    products(acc, here, out, b_y[last - 1], b_z[last - 1])
+    jumps(acc, out, ends[1], b_x[last - 2])
+    leave(last - 1, here, out)
+    out, before = image(final, s_after, before, b_final, b_y[last], b_z[last])
+    products(acc, final, out, b_y[last], b_z[last])
+    jumps(acc, out, q_out[2], b_x[last - 1])
+    leave(last, final, out)
     after = above_x[0]
     betas = weight(after, above_x[1]), weight(after, next_row(after)), weight(after, next_lane(after))
-    here, out = image(planes, s_after, above_x[3], *betas)
-    jumps(planes, out, b_final[own, :])
+    out, _ = image(s_after, above_x[3], before, *betas)
+    jumps(acc, out, q_out[3], b_final)
+    leave(planes, s_after, out)
     at = lax.broadcasted_iota(jnp.int32, (1, 128), 1)
     row = jnp.zeros((1, 128), F32)
     for k in range(4):
         value = jnp.sum(jnp.sum(acc[k], 0, keepdims=True), 1, keepdims=True)
         row = row + jnp.where(at == k, value, 0.0)
     sums[...] = jnp.broadcast_to(row, sums.shape)
-    for x in range(planes + 1):
-        for copy in leaving(x):
-            copy.wait()
+    for copy in copies:
+        copy.wait()
 
 
 def spreading(columns):
@@ -274,7 +304,7 @@
             jnp.sum(jnp.where(at_lane == k, all_sums, 0.0), 1, keepdims=True) for k in range(4)
         )
         alpha0 = m0 / m1
-        rr1 = alpha0 * alpha0 * m2 - m0
+        rr1 = jnp.maximum(alpha0 * alpha0 * m2 - m0, 0.0)
         beta = rr1 / m0
         more = 1.0 + beta
         alpha1 = rr1 / (more * more * m1 - 2.0 * more * alpha0 * m2 + alpha0 * alpha0 * m3)
@@ -343,7 +373,7 @@
             fs = [f[part * 8 : part * 8 + 8] for f in broad]
             prod[:, to] = jnp.concatenate([v * f for v in vs for f in fs], 0).astype(BF16)
     tiles = w_in.shape[1] // wide_tile
-    late = 2
+    late = 1
     for block in range(blocks + late):
         for tile in range(tiles):
             if block < blocks:
@@ -402,10 +432,10 @@
 def body(density, cotangent, features, w_inner, w_outer):
     nx, ny, nz = density.shape
     count, hidden = features.shape[0], w_inner.shape[0]
-    density, cotangent, features = map(away, (density, cotangent, features))
     devices = lax.axis_size("gx") * lax.axis_size("gy")
     cells = float(density.size * devices)
-    lines, ends = ny // 8 - 1, nx // 2 - 1
+    lines = ny // 8 - 1
+    near = pl.BlockSpec(memory_space=pltpu.VMEM)
     around = (ny + 16, nz)
     to_up, to_down = pl.pallas_call(
         pack_kernel,
@@ -419,52 +449,48 @@
         out_specs=[whole((starts(plan)[1] * nx, nz)) for plan in (LOWER_Y, UPPER_Y)],
         out_shape=[shape(starts(plan)[1] * nx, nz) for plan in (LOWER_Y, UPPER_Y)],
         compiler_params=params(),
-    )(density, density, cotangent, cotangent)
+    )(*map(away, (density, density, cotangent, cotangent)))
     below_y, above_y = neighbours(to_up, 0, 1), neighbours(to_down, 0, -1)
     to_up, to_down = pl.pallas_call(
         edge_kernel,
-        grid=(1,),
-        in_specs=[
-            pl.BlockSpec((4, ny, nz), lambda i: (0, 0, 0)),
-            pl.BlockSpec((2, ny, nz), lambda i: (ends, 0, 0)),
-            pl.BlockSpec((3, 2, ny, nz), lambda i: (0, 0, 0, 0)),
-            pl.BlockSpec((3, 2, ny, nz), lambda i: (0, ends, 0, 0)),
-            whole(below_y.shape),
-            whole(above_y.shape),
-        ],
-        out_specs=[whole((3,) + around), whole((4,) + around)],
-        out_shape=[shape(3, *around), shape(4, *around)],
-        compiler_params=params(),
-    )(density, density, cotangent, cotangent, keep(below_y), keep(above_y))
+        in_specs=[near] * 4,
+        out_shape=[held(3, *around), held(4, *around)],
+        compiler_params=params(12),
+    )(*map(keep, (density, cotangent, below_y, above_y)))
     below_x, above_x = neighbours(to_up, 1, 0), neighbours(to_down, -1, 0)
 
     extended = (nx + 1, ny + 8, nz)
-    anywhere = pl.BlockSpec(memory_space=pl.ANY)
-    near = pl.BlockSpec(memory_space=pltpu.VMEM)
     whole_planes = (nx,) + around
     fields = pl.pallas_call(
         source_kernel,
-        in_specs=[anywhere] * 2 + [near] * 2,
+        in_specs=[near] * 4,
         out_shape=[held(*whole_planes)] * 4,
+        scratch_shapes=[pltpu.VMEM(whole_planes, F32), pltpu.VMEM(around, F32)],
+        compiler_params=params(12),
+    )(*map(keep, (density, cotangent, below_y, above_y)))
+    far = pl.BlockSpec(memory_space=pltpu.HBM)
+    s, q, ends, inner = pl.pallas_call(
+        inner_kernel,
+        in_specs=[near] * 4,
+        out_specs=[far] * 2 + [near] * 2,
+        out_shape=[pltpu.HBM(extended, F32)] * 2 + [held(2, *extended[1:]), held(4, 8, nz)],
         scratch_shapes=[
-            pltpu.VMEM((nx, ny, nz), F32),
-            pltpu.VMEM((3, nx, ny, nz), F32),
-            pltpu.VMEM(whole_planes, F32),
+            pltpu.VMEM(extended, F32),
             pltpu.VMEM(around, F32),
-            pltpu.SemaphoreType.DMA((5,)),
+            pltpu.SemaphoreType.DMA((2, nx)),
         ],
-        compiler_params=params(30),
-    )(density, cotangent, keep(below_y), keep(above_y))
+        compiler_params=params(12),
+    )(*fields)
     s, q, sums = pl.pallas_call(
         moments_kernel,
-        in_specs=[near] * 8,
-        out_specs=[pl.BlockSpec(memory_space=pltpu.HBM)] * 2 + [near],
+        in_specs=[near] * 10 + [far] * 2,
+        out_specs=[far] * 2 + [near],
         out_shape=[pltpu.HBM(extended, F32)] * 2 + [held(devices, 128)],
-        scratch_shapes=[pltpu.VMEM(extended, F32)] * 2
-        + [pltpu.VMEM(around, F32)] * 4
-        + [pltpu.VMEM((4, 8, nz), F32), pltpu.SemaphoreType.DMA((2, nx + 1))],
-        compiler_params=params(30),
-    )(keep(below_x), keep(above_x), keep(to_up), keep(to_down), *fields)
+        input_output_aliases={10: 0, 11: 1},
+        scratch_shapes=[pltpu.VMEM((5,) + extended[1:], F32)] * 2
+        + [pltpu.VMEM((4, 8, nz), F32), pltpu.SemaphoreType.DMA((2, 5))],
+        compiler_params=params(16),
+    )(*map(keep, (below_x, above_x, to_up, to_down, *fields, ends, inner)), s, q)
     sums = collect(sums)
 
     half = hidden * 8
@@ -494,7 +520,7 @@
             pltpu.VMEM((24 * count, half), F32),
         ],
         compiler_params=params(48),
-    )(keep(sums), cotangent, *map(away, (s, q, s, q)), features, w_inner, w_outer)
+    )(keep(sums), *map(away, (cotangent, s, q, s, q, features)), w_inner, w_outer)
     grads = jnp.sum(collect(grads), 0).reshape(6, 128) / cells
     low, high = grads[:, :hidden], grads[:, hidden:]
     return grad, jnp.concatenate([low[:4], high[:4]]).T, jnp.concatenate([low[4:], high[4:5]])

time: 118 us -> 114 us (0.966)
  Pallas kernels: 59 us -> 55.4 us
    pallas_call x3 -> x4, Pallas kernels: 14.6 us -> 11.7 us  [the longest x1 4.23 us: body(): pl.pallas_call(inner_kernel, in_specs=[near] * 4, out_specs=[far] * 2 + [...]
  transfers between devices with their start and end apart: 5 -> 5, of which waited for: 2 -> 2; matrix products, arithmetic and copies ran while one was open for 0% -> 0% of each run, Pallas kernels for 5% -> 7%
where the time goes in v6:
time: 114 us
  Pallas kernels  55.4 us (49%)
  starting transfers between devices  26.2 us (23%)
  blocking collectives  16.4 us (14%)
  waiting for transfers between devices  13.4 us (12%)
  other arithmetic  1.47 us (1%)
    pallas_call x1, Pallas kernels, body(): pl.pallas_call(closure_kernel, grid=(nx // step,), in_specs=[whole((devic...  42.2 us
    all_to_all x1, blocking collectives, collect(): return lax.all_to_all(copies, ('gx', 'gy'), 0, 0)  16.4 us
    all_to_all x1, starting transfers between devices, collect(): return lax.all_to_all(copies, ('gx', 'gy'), 0, 0)  13.8 us
    ppermute x4, starting transfers between devices, neighbours(): return lax.ppermute(value, ('gx', 'gy'), pairs)  12.4 us
    all_to_all x1, waiting for transfers between devices, collect(): return lax.all_to_all(copies, ('gx', 'gy'), 0, 0)  9.21 us
    pallas_call x1, Pallas kernels, body(): pl.pallas_call(inner_kernel, in_specs=[near] * 4, out_specs=[far] * 2 + [...  4.23 us
    ppermute x4, waiting for transfers between devices, neighbours(): return lax.ppermute(value, ('gx', 'gy'), pairs)  4.17 us
    pallas_call x1, Pallas kernels, body(): pl.pallas_call(source_kernel, in_specs=[near] * 4, out_shape=[held(*whole...  4.08 us
  transfers between devices with their start and end apart: 5, of which 2 were waited for; matrix products, arithmetic and copies ran while one was open for 0% of the time, Pallas kernels for 7%

profile of v6, /device:TPU:0, one launch (start us, length us, event | category | flops | bytes accessed | tf_op | source)
XLA Modules:
  0.0 113.9 jit_solution(15038496356361993715)
XLA Ops:
  0.6 0.0 copy-start
  0.7 1.5 %shard_map.76 = (f32[96,256]{1,0:T(8,128)S(1)}, f32[144,256]{1,0:T(8,128)S(1)}) custom-call(f32[16,128,256]{2,1,0:T(8,128)} %dens.3, f32[16,128,256]{2,1,0:T(8,128)} %dens.3, f32[3,16,128,256]{3,2,1,0:T(8,128)} %cot.5, f32[3,16,128,256]{3,2,1,0:T(8,128)} %cot.5), custom_call_target="tpu_custom_call" | custom-call | tf_op jit(solution)/shard_map/pallas_call | solution.py:440
  2.2 1.6 %collective-permute-start.1 = (f32[144,256]{1,0:T(8,128)S(1)}, f32[144,256]{1,0:T(8,128)S(1)}, u32[]{:S(2)}, u32[]{:S(2)}) collective-permute-start(f32[144,256]{1,0:T(8,128)S(1)} %get-tuple-element.21), channel_id=1, source_target_pairs={{1,0},{2,1},{3,2},{4,3},{5,4},{6,5},{7,6},{9,8},{10,9},{11,10},{12... | collective-permute-start | bytes 442376 | tf_op jit(solution)/shard_map/ppermute | solution.py:26
  3.7 6.5 %collective-permute-start = (f32[96,256]{1,0:T(8,128)S(1)}, f32[96,256]{1,0:T(8,128)S(1)}, u32[]{:S(2)}, u32[]{:S(2)}) collective-permute-start(f32[96,256]{1,0:T(8,128)S(1)} %get-tuple-element.20), channel_id=1, source_target_pairs={{0,1},{1,2},{2,3},{3,4},{4,5},{5,6},{6,7},{8,9},{9,10},{10,11},{11... | collective-permute-start | bytes 294920 | tf_op jit(solution)/shard_map/ppermute | solution.py:26
  10.2 4.2 %collective-permute-done.below_y = f32[96,256]{1,0:T(8,128)S(1)} collective-permute-done((f32[96,256]{1,0:T(8,128)S(1)}, f32[96,256]{1,0:T(8,128)S(1)}, u32[]{:S(2)}, u32[]{:S(2)}) %collective-permute-start) | collective-permute-done | bytes 98336 | tf_op jit(solution)/shard_map/ppermute | solution.py:26
  14.4 0.6 shard_map.77
  15.0 1.3 %collective-permute-start.3 = (f32[4,144,256]{2,1,0:T(8,128)S(1)}, f32[4,144,256]{2,1,0:T(8,128)S(1)}, u32[]{:S(2)}, u32[]{:S(2)}) collective-permute-start(f32[4,144,256]{2,1,0:T(8,128)S(1)} %get-tuple-element.23.own_down), channel_id=1, source_target_pairs={{8,0},{9,1},{10,2},{11,3},{12,4},{13,5},{14,6},{15,7},{16,8},{17,9... | collective-permute-start | bytes 1769480 | tf_op jit(solution)/shard_map/ppermute | solution.py:26
  16.3 3.1 %collective-permute-start.2 = (f32[3,144,256]{2,1,0:T(8,128)S(1)}, f32[3,144,256]{2,1,0:T(8,128)S(1)}, u32[]{:S(2)}, u32[]{:S(2)}) collective-permute-start(f32[3,144,256]{2,1,0:T(8,128)S(1)} %get-tuple-element.22.own_up), channel_id=1, source_target_pairs={{0,8},{1,9},{2,10},{3,11},{4,12},{5,13},{6,14},{7,15},{8,16},{9,17... | collective-permute-start | bytes 1327112 | tf_op jit(solution)/shard_map/ppermute | solution.py:26
  19.4 4.1 %shard_map.78 = (f32[16,144,256]{2,1,0:T(8,128)S(1)}, f32[16,144,256]{2,1,0:T(8,128)S(1)}, f32[16,144,256]{2,1,0:T(8,128)S(1)}, f32[16,144,256]{2,1,0:T(8,128)S(1)}) custom-call(f32[16,128,256]{2,1,0:T(8,128)S(1)} %copy-done.1, f32[3,16,128,256]{3,2,1,0:T(8,128)S(1)} %copy-done, f32[96,256]{1,0:T(8,128)S(1)} %collective-permute-done.below_y, ...), custom_call_target="tpu_custom_call" | custom-call | tf_op jit(solution)/shard_map/pallas_call | solution.py:464
  23.5 4.2 %shard_map.79 = (f32[17,136,256]{2,1,0:T(8,128)}, f32[17,136,256]{2,1,0:T(8,128)}, f32[2,136,256]{2,1,0:T(8,128)S(1)}, f32[4,8,256]{2,1,0:T(8,128)S(1)}) custom-call(f32[16,144,256]{2,1,0:T(8,128)S(1)} %get-tuple-element.24.s_part, f32[16,144,256]{2,1,0:T(8,128)S(1)} %get-tuple-element.25.b_x, f32[16,144,256]{2,1,0:T(8,128)S(1)} %get-tuple-element.26.b_y, ...), custom_call_target="tpu_custom_call" | custom-call | tf_op jit(solution)/shard_map/pallas_call | solution.py:472
  27.7 0.0 collective-permute-done.2.below_x
  27.7 0.0 copy-start.3
  27.7 0.0 copy-start.2
  27.7 2.8 %shard_map.80 = (f32[17,136,256]{2,1,0:T(8,128)}, f32[17,136,256]{2,1,0:T(8,128)}, f32[128,128]{1,0:T(8,128)}) custom-call(f32[3,144,256]{2,1,0:T(8,128)S(1)} %collective-permute-done.2.below_x, f32[4,144,256]{2,1,0:T(8,128)S(1)} %collective-permute-done.3.above_x, ...), custom_call_target="tpu_custom_call", output_to_operand_aliasing={{0}: (10, {}), {1}: (11, {})} | custom-call | tf_op jit(solution)/shard_map/pallas_call | solution.py:484
  30.5 13.8 %all-to-all-start = ((f32[128,1,128]{2,1,0:T(1,128)}), f32[128,1,128]{2,1,0:T(1,128)S(1)}, u32[]{:S(2)}, u32[]{:S(2)}) async-start(f32[128,1,128]{2,1,0:T(1,128)} %bitcast.1), calls=%async_computation | async-start | bytes 131072 | tf_op jit(solution)/shard_map/all_to_all | solution.py:15
  44.3 0.1 copy.12.w_inner
  44.4 9.2 %all-to-all-done = f32[128,1,128]{2,1,0:T(1,128)S(1)} async-done(((f32[128,1,128]{2,1,0:T(1,128)}), f32[128,1,128]{2,1,0:T(1,128)S(1)}, u32[]{:S(2)}, u32[]{:S(2)}) %all-to-all-start) | async-done | bytes 65568 | tf_op jit(solution)/shard_map/all_to_all | solution.py:15
  53.6 42.2 %shard_map.81 = (f32[3,16,128,256]{3,2,1,0:T(8,128)}, f32[128,1,768]{2,1,0:T(1,128)S(1)}) custom-call(f32[128,128]{1,0:T(8,128)S(1)} %bitcast.8, f32[3,16,128,256]{3,2,1,0:T(8,128)} %cot.5, f32[17,136,256]{2,1,0:T(8,128)} %get-tuple-element.33.s.s_next, f32[17,136,256]{2,1,0:T(8,128)} %get-tuple-element.34.q.q_next, ...), custom_call_target="tpu_custom_call" | custom-call | tf_op jit(solution)/shard_map/pallas_call | solution.py:502
  95.9 16.4 %all_to_all.16 = f32[128,1,768]{2,1,0:T(1,128)S(1)} all-to-all(f32[128,1,768]{2,1,0:T(1,128)S(1)} %get-tuple-element.36), channel_id=1, replica_groups=mesh['gx'=16,'gy'=8] {'gx','gy'}, dimensions={0} | all-to-all | bytes 786432 | tf_op jit(solution)/shard_map/all_to_all | solution.py:15
  112.3 0.3 reduce_sum.9
  112.6 0.1 slice.21
  112.7 0.1 fusion
  112.7 0.6 pad_maximum_fusion
  113.3 0.6 maximum_bitcast_fusion
  (9 shorter events, 0.0 us)
Async XLA Ops:
  0.6 13.8 %copy-start.1 = (f32[16,128,256]{2,1,0:T(8,128)S(1)}, f32[16,128,256]{2,1,0:T(8,128)}, u32[]{:S(2)}) copy-start(f32[16,128,256]{2,1,0:T(8,128)} %dens.3) | copy-start | bytes 6291460
  0.6 13.8 %copy-start = (f32[3,16,128,256]{3,2,1,0:T(8,128)S(1)}, f32[3,16,128,256]{3,2,1,0:T(8,128)}, u32[]{:S(2)}) copy-start(f32[3,16,128,256]{3,2,1,0:T(8,128)} %cot.5) | copy-start | bytes 18874372
  2.2 12.2 %collective-permute-start.1 = (f32[144,256]{1,0:T(8,128)S(1)}, f32[144,256]{1,0:T(8,128)S(1)}, u32[]{:S(2)}, u32[]{:S(2)}) collective-permute-start(f32[144,256]{1,0:T(8,128)S(1)} %get-tuple-element.21), channel_id=1, source_target_pairs={{1,0},{2,1},{3,2},{4,3},{5,4},{6,5},{7,6},{9,8},{10,9},{11,10},{12... | collective-permute-start | bytes 442376 | tf_op jit(solution)/shard_map/ppermute | solution.py:26
  3.7 10.7 %collective-permute-start = (f32[96,256]{1,0:T(8,128)S(1)}, f32[96,256]{1,0:T(8,128)S(1)}, u32[]{:S(2)}, u32[]{:S(2)}) collective-permute-start(f32[96,256]{1,0:T(8,128)S(1)} %get-tuple-element.20), channel_id=1, source_target_pairs={{0,1},{1,2},{2,3},{3,4},{4,5},{5,6},{6,7},{8,9},{9,10},{10,11},{11... | collective-permute-start | bytes 294920 | tf_op jit(solution)/shard_map/ppermute | solution.py:26
  15.0 12.7 %collective-permute-start.3 = (f32[4,144,256]{2,1,0:T(8,128)S(1)}, f32[4,144,256]{2,1,0:T(8,128)S(1)}, u32[]{:S(2)}, u32[]{:S(2)}) collective-permute-start(f32[4,144,256]{2,1,0:T(8,128)S(1)} %get-tuple-element.23.own_down), channel_id=1, source_target_pairs={{8,0},{9,1},{10,2},{11,3},{12,4},{13,5},{14,6},{15,7},{16,8},{17,9... | collective-permute-start | bytes 1769480 | tf_op jit(solution)/shard_map/ppermute | solution.py:26
  16.3 11.4 %collective-permute-start.2 = (f32[3,144,256]{2,1,0:T(8,128)S(1)}, f32[3,144,256]{2,1,0:T(8,128)S(1)}, u32[]{:S(2)}, u32[]{:S(2)}) collective-permute-start(f32[3,144,256]{2,1,0:T(8,128)S(1)} %get-tuple-element.22.own_up), channel_id=1, source_target_pairs={{0,8},{1,9},{2,10},{3,11},{4,12},{5,13},{6,14},{7,15},{8,16},{9,17... | collective-permute-start | bytes 1327112 | tf_op jit(solution)/shard_map/ppermute | solution.py:26
  27.7 16.6 %copy-start.3 = (bf16[64,8]{0,1:T(8,128)(2,1)S(1)}, bf16[64,8]{0,1:T(8,128)(2,1)}, u32[]{:S(2)}) copy-start(bf16[64,8]{0,1:T(8,128)(2,1)} %param.8) | copy-start | bytes 3076
  27.7 25.9 %copy-start.2 = (bf16[3,64]{1,0:T(4,128)(2,1)S(1)}, bf16[3,64]{1,0:T(4,128)(2,1)}, u32[]{:S(2)}) copy-start(bf16[3,64]{1,0:T(4,128)(2,1)} %w_outer.1) | copy-start | bytes 1156
  30.5 23.1 %all-to-all-start = ((f32[128,1,128]{2,1,0:T(1,128)}), f32[128,1,128]{2,1,0:T(1,128)S(1)}, u32[]{:S(2)}, u32[]{:S(2)}) async-start(f32[128,1,128]{2,1,0:T(1,128)} %bitcast.1), calls=%async_computation | async-start | bytes 131072 | tf_op jit(solution)/shard_map/all_to_all | solution.py:15

commit v7 on v6

--- a/solution.py
+++ b/solution.py
@@ -362,7 +362,7 @@
         cells, columns = place(block, tile)
         acc_o[:, columns] += jnp.dot(vel[:, cells], hid[cells, columns], preferred_element_type=F32)
 
-    for block in range(blocks):
+    def right(block):
         x, at = place_of(block)
         broad = [feats[c, x, at, :].astype(F32) for c in range(count)]
         for part in range(2):
@@ -372,12 +372,15 @@
             vel[:, to] = jnp.concatenate(vs + [jnp.zeros_like(vs[0])], 0).astype(BF16)
             fs = [f[part * 8 : part * 8 + 8] for f in broad]
             prod[:, to] = jnp.concatenate([v * f for v in vs for f in fs], 0).astype(BF16)
+
     tiles = w_in.shape[1] // wide_tile
     late = 1
     for block in range(blocks + late):
         for tile in range(tiles):
             if block < blocks:
                 first_layer(block, tile)
+                if tile == 1:
+                    right(block)
             if block >= late:
                 outer(block - late, tile)
     acc_t[...] += jnp.dot(prod[...], slope[...], preferred_element_type=F32)
@@ -494,7 +497,7 @@
     sums = collect(sums)
 
     half = hidden * 8
-    step = 2
+    step = 4
     long = step * ny // 8 * nz
     planes = pl.BlockSpec((3, step, ny, nz), lambda i: (0, i, 0, 0))
     here = pl.BlockSpec((step, ny + 8, nz), lambda i: (i, 0, 0))
@@ -519,7 +522,7 @@
             pltpu.VMEM((32, half), F32),
             pltpu.VMEM((24 * count, half), F32),
         ],
-        compiler_params=params(48),
+        compiler_params=params(60),
     )(keep(sums), *map(away, (cotangent, s, q, s, q, features)), w_inner, w_outer)
     grads = jnp.sum(collect(grads), 0).reshape(6, 128) / cells
     low, high = grads[:, :hidden], grads[:, hidden:]

time: 114 us -> 114 us (level)
  transfers between devices with their start and end apart: 5 -> 5, of which waited for: 2 -> 2; matrix products, arithmetic and copies ran while one was open for 0% -> 1% of each run, Pallas kernels for 7% -> 7%
where the time goes in v7:
time: 114 us
  Pallas kernels  54.8 us (48%)
  starting transfers between devices  26.4 us (23%)
  blocking collectives  16.9 us (15%)
  waiting for transfers between devices  12.6 us (11%)
  other arithmetic  1.47 us (1%)
    pallas_call x1, Pallas kernels, body(): pl.pallas_call(closure_kernel, grid=(nx // step,), in_specs=[whole((devic...  41.6 us
    all_to_all x1, blocking collectives, collect(): return lax.all_to_all(copies, ('gx', 'gy'), 0, 0)  16.9 us
    all_to_all x1, starting transfers between devices, collect(): return lax.all_to_all(copies, ('gx', 'gy'), 0, 0)  14 us
    ppermute x4, starting transfers between devices, neighbours(): return lax.ppermute(value, ('gx', 'gy'), pairs)  12.4 us
    all_to_all x1, waiting for transfers between devices, collect(): return lax.all_to_all(copies, ('gx', 'gy'), 0, 0)  8.45 us
    pallas_call x1, Pallas kernels, body(): pl.pallas_call(inner_kernel, in_specs=[near] * 4, out_specs=[far] * 2 + [...  4.22 us
    ppermute x4, waiting for transfers between devices, neighbours(): return lax.ppermute(value, ('gx', 'gy'), pairs)  4.17 us
    pallas_call x1, Pallas kernels, body(): pl.pallas_call(source_kernel, in_specs=[near] * 4, out_shape=[held(*whole...  4.08 us
  transfers between devices with their start and end apart: 5, of which 2 were waited for; matrix products, arithmetic and copies ran while one was open for 1% of the time, Pallas kernels for 7%

profile of v7, /device:TPU:0, one launch (start us, length us, event | category | flops | bytes accessed | tf_op | source)
XLA Modules:
  0.0 113.8 jit_solution(15905802194667576616)
XLA Ops:
  0.6 0.0 copy-start
  0.7 1.5 %shard_map.76 = (f32[96,256]{1,0:T(8,128)S(1)}, f32[144,256]{1,0:T(8,128)S(1)}) custom-call(f32[16,128,256]{2,1,0:T(8,128)} %dens.3, f32[16,128,256]{2,1,0:T(8,128)} %dens.3, f32[3,16,128,256]{3,2,1,0:T(8,128)} %cot.5, f32[3,16,128,256]{3,2,1,0:T(8,128)} %cot.5), custom_call_target="tpu_custom_call" | custom-call | tf_op jit(solution)/shard_map/pallas_call | solution.py:443
  2.2 1.6 %collective-permute-start.1 = (f32[144,256]{1,0:T(8,128)S(1)}, f32[144,256]{1,0:T(8,128)S(1)}, u32[]{:S(2)}, u32[]{:S(2)}) collective-permute-start(f32[144,256]{1,0:T(8,128)S(1)} %get-tuple-element.21), channel_id=1, source_target_pairs={{1,0},{2,1},{3,2},{4,3},{5,4},{6,5},{7,6},{9,8},{10,9},{11,10},{12... | collective-permute-start | bytes 442376 | tf_op jit(solution)/shard_map/ppermute | solution.py:26
  3.7 6.5 %collective-permute-start = (f32[96,256]{1,0:T(8,128)S(1)}, f32[96,256]{1,0:T(8,128)S(1)}, u32[]{:S(2)}, u32[]{:S(2)}) collective-permute-start(f32[96,256]{1,0:T(8,128)S(1)} %get-tuple-element.20), channel_id=1, source_target_pairs={{0,1},{1,2},{2,3},{3,4},{4,5},{5,6},{6,7},{8,9},{9,10},{10,11},{11... | collective-permute-start | bytes 294920 | tf_op jit(solution)/shard_map/ppermute | solution.py:26
  10.2 4.2 %collective-permute-done.below_y = f32[96,256]{1,0:T(8,128)S(1)} collective-permute-done((f32[96,256]{1,0:T(8,128)S(1)}, f32[96,256]{1,0:T(8,128)S(1)}, u32[]{:S(2)}, u32[]{:S(2)}) %collective-permute-start) | collective-permute-done | bytes 98336 | tf_op jit(solution)/shard_map/ppermute | solution.py:26
  14.4 0.0 collective-permute-done.1.above_y
  14.4 0.6 shard_map.77
  15.0 1.3 %collective-permute-start.3 = (f32[4,144,256]{2,1,0:T(8,128)S(1)}, f32[4,144,256]{2,1,0:T(8,128)S(1)}, u32[]{:S(2)}, u32[]{:S(2)}) collective-permute-start(f32[4,144,256]{2,1,0:T(8,128)S(1)} %get-tuple-element.23.own_down), channel_id=1, source_target_pairs={{8,0},{9,1},{10,2},{11,3},{12,4},{13,5},{14,6},{15,7},{16,8},{17,9... | collective-permute-start | bytes 1769480 | tf_op jit(solution)/shard_map/ppermute | solution.py:26
  16.3 3.1 %collective-permute-start.2 = (f32[3,144,256]{2,1,0:T(8,128)S(1)}, f32[3,144,256]{2,1,0:T(8,128)S(1)}, u32[]{:S(2)}, u32[]{:S(2)}) collective-permute-start(f32[3,144,256]{2,1,0:T(8,128)S(1)} %get-tuple-element.22.own_up), channel_id=1, source_target_pairs={{0,8},{1,9},{2,10},{3,11},{4,12},{5,13},{6,14},{7,15},{8,16},{9,17... | collective-permute-start | bytes 1327112 | tf_op jit(solution)/shard_map/ppermute | solution.py:26
  19.4 4.1 %shard_map.78 = (f32[16,144,256]{2,1,0:T(8,128)S(1)}, f32[16,144,256]{2,1,0:T(8,128)S(1)}, f32[16,144,256]{2,1,0:T(8,128)S(1)}, f32[16,144,256]{2,1,0:T(8,128)S(1)}) custom-call(f32[16,128,256]{2,1,0:T(8,128)S(1)} %copy-done.1, f32[3,16,128,256]{3,2,1,0:T(8,128)S(1)} %copy-done, f32[96,256]{1,0:T(8,128)S(1)} %collective-permute-done.below_y, ...), custom_call_target="tpu_custom_call" | custom-call | tf_op jit(solution)/shard_map/pallas_call | solution.py:467
  23.5 4.2 %shard_map.79 = (f32[17,136,256]{2,1,0:T(8,128)}, f32[17,136,256]{2,1,0:T(8,128)}, f32[2,136,256]{2,1,0:T(8,128)S(1)}, f32[4,8,256]{2,1,0:T(8,128)S(1)}) custom-call(f32[16,144,256]{2,1,0:T(8,128)S(1)} %get-tuple-element.24.s_part, f32[16,144,256]{2,1,0:T(8,128)S(1)} %get-tuple-element.25.b_x, f32[16,144,256]{2,1,0:T(8,128)S(1)} %get-tuple-element.26.b_y, ...), custom_call_target="tpu_custom_call" | custom-call | tf_op jit(solution)/shard_map/pallas_call | solution.py:475
  27.7 0.0 collective-permute-done.2.below_x
  27.7 0.0 copy-start.2
  27.7 2.8 %shard_map.80 = (f32[17,136,256]{2,1,0:T(8,128)}, f32[17,136,256]{2,1,0:T(8,128)}, f32[128,128]{1,0:T(8,128)}) custom-call(f32[3,144,256]{2,1,0:T(8,128)S(1)} %collective-permute-done.2.below_x, f32[4,144,256]{2,1,0:T(8,128)S(1)} %collective-permute-done.3.above_x, ...), custom_call_target="tpu_custom_call", output_to_operand_aliasing={{0}: (10, {}), {1}: (11, {})} | custom-call | tf_op jit(solution)/shard_map/pallas_call | solution.py:487
  30.5 14.0 %all-to-all-start = ((f32[128,1,128]{2,1,0:T(1,128)}), f32[128,1,128]{2,1,0:T(1,128)S(1)}, u32[]{:S(2)}, u32[]{:S(2)}) async-start(f32[128,1,128]{2,1,0:T(1,128)} %bitcast.1), calls=%async_computation | async-start | bytes 131072 | tf_op jit(solution)/shard_map/all_to_all | solution.py:15
  44.5 0.7 copy.12.w_inner
  45.2 8.4 %all-to-all-done = f32[128,1,128]{2,1,0:T(1,128)S(1)} async-done(((f32[128,1,128]{2,1,0:T(1,128)}), f32[128,1,128]{2,1,0:T(1,128)S(1)}, u32[]{:S(2)}, u32[]{:S(2)}) %all-to-all-start) | async-done | bytes 65568 | tf_op jit(solution)/shard_map/all_to_all | solution.py:15
  53.6 41.6 %shard_map.81 = (f32[3,16,128,256]{3,2,1,0:T(8,128)}, f32[128,1,768]{2,1,0:T(1,128)}) custom-call(f32[128,128]{1,0:T(8,128)S(1)} %bitcast.8, f32[3,16,128,256]{3,2,1,0:T(8,128)} %cot.5, f32[17,136,256]{2,1,0:T(8,128)} %get-tuple-element.33.s.s_next, f32[17,136,256]{2,1,0:T(8,128)} %get-tuple-element.34.q.q_next, f32[17,136,256]{2,1,0:T(8,128)} %get-tuple-element.33.s.s_next, ...), custom_call_target="tpu_custom_call" | custom-call | tf_op jit(solution)/shard_map/pallas_call | solution.py:505
  95.2 16.9 %all_to_all.16 = f32[128,1,768]{2,1,0:T(1,128)S(1)} all-to-all(f32[128,1,768]{2,1,0:T(1,128)} %get-tuple-element.36), channel_id=1, replica_groups=mesh['gx'=16,'gy'=8] {'gx','gy'}, dimensions={0} | all-to-all | bytes 786432 | tf_op jit(solution)/shard_map/all_to_all | solution.py:15
  112.1 0.3 reduce_sum.9
  112.4 0.1 slice.21
  112.5 0.1 fusion
  112.6 0.6 pad_maximum_fusion
  113.2 0.6 maximum_bitcast_fusion
  (7 shorter events, 0.0 us)
Async XLA Ops:
  0.6 13.8 %copy-start.1 = (f32[16,128,256]{2,1,0:T(8,128)S(1)}, f32[16,128,256]{2,1,0:T(8,128)}, u32[]{:S(2)}) copy-start(f32[16,128,256]{2,1,0:T(8,128)} %dens.3) | copy-start | bytes 6291460
  0.6 13.8 %copy-start = (f32[3,16,128,256]{3,2,1,0:T(8,128)S(1)}, f32[3,16,128,256]{3,2,1,0:T(8,128)}, u32[]{:S(2)}) copy-start(f32[3,16,128,256]{3,2,1,0:T(8,128)} %cot.5) | copy-start | bytes 18874372
  2.2 12.2 %collective-permute-start.1 = (f32[144,256]{1,0:T(8,128)S(1)}, f32[144,256]{1,0:T(8,128)S(1)}, u32[]{:S(2)}, u32[]{:S(2)}) collective-permute-start(f32[144,256]{1,0:T(8,128)S(1)} %get-tuple-element.21), channel_id=1, source_target_pairs={{1,0},{2,1},{3,2},{4,3},{5,4},{6,5},{7,6},{9,8},{10,9},{11,10},{12... | collective-permute-start | bytes 442376 | tf_op jit(solution)/shard_map/ppermute | solution.py:26
  3.7 10.7 %collective-permute-start = (f32[96,256]{1,0:T(8,128)S(1)}, f32[96,256]{1,0:T(8,128)S(1)}, u32[]{:S(2)}, u32[]{:S(2)}) collective-permute-start(f32[96,256]{1,0:T(8,128)S(1)} %get-tuple-element.20), channel_id=1, source_target_pairs={{0,1},{1,2},{2,3},{3,4},{4,5},{5,6},{6,7},{8,9},{9,10},{10,11},{11... | collective-permute-start | bytes 294920 | tf_op jit(solution)/shard_map/ppermute | solution.py:26
  15.0 12.7 %collective-permute-start.3 = (f32[4,144,256]{2,1,0:T(8,128)S(1)}, f32[4,144,256]{2,1,0:T(8,128)S(1)}, u32[]{:S(2)}, u32[]{:S(2)}) collective-permute-start(f32[4,144,256]{2,1,0:T(8,128)S(1)} %get-tuple-element.23.own_down), channel_id=1, source_target_pairs={{8,0},{9,1},{10,2},{11,3},{12,4},{13,5},{14,6},{15,7},{16,8},{17,9... | collective-permute-start | bytes 1769480 | tf_op jit(solution)/shard_map/ppermute | solution.py:26
  16.3 11.4 %collective-permute-start.2 = (f32[3,144,256]{2,1,0:T(8,128)S(1)}, f32[3,144,256]{2,1,0:T(8,128)S(1)}, u32[]{:S(2)}, u32[]{:S(2)}) collective-permute-start(f32[3,144,256]{2,1,0:T(8,128)S(1)} %get-tuple-element.22.own_up), channel_id=1, source_target_pairs={{0,8},{1,9},{2,10},{3,11},{4,12},{5,13},{6,14},{7,15},{8,16},{9,17... | collective-permute-start | bytes 1327112 | tf_op jit(solution)/shard_map/ppermute | solution.py:26
  27.7 16.7 %copy-start.2 = (bf16[64,8]{0,1:T(8,128)(2,1)S(1)}, bf16[64,8]{0,1:T(8,128)(2,1)}, u32[]{:S(2)}) copy-start(bf16[64,8]{0,1:T(8,128)(2,1)} %param.8) | copy-start | bytes 3076
  30.5 23.1 %all-to-all-start = ((f32[128,1,128]{2,1,0:T(1,128)}), f32[128,1,128]{2,1,0:T(1,128)S(1)}, u32[]{:S(2)}, u32[]{:S(2)}) async-start(f32[128,1,128]{2,1,0:T(1,128)} %bitcast.1), calls=%async_computation | async-start | bytes 131072 | tf_op jit(solution)/shard_map/all_to_all | solution.py:15
